TPU v7x, 32 devices: a whole 2x2x4 slice. The times are simulated.
32 devices in a mesh: dp: 8 (over z, y), row: 2 (over x), col: 2 (over core).
Axes of the slice: x: 2, y: 2, z: 4, core: 2. Of those that a mesh axis runs over, the one named last changes fastest.
Arguments:
- images: bfloat16 [128, 14, 14, 256], P('dp', 'row', 'col'), may hold values from -6 to 6
- cotangent: bfloat16 [128, 14, 14, 256], P('dp', 'row', 'col'), may hold values from -6 to 6
- mix_partner: int32 [128], replicated, may hold values from 0 to 127, as said below
- cut_partner: int32 [128], replicated, may hold values from 0 to 127, as said below
- ratios: float32 [128], P('dp'), may hold values from 0.3 to 0.9
- corners: int32 [128, 4], P('dp'), may hold values from 0 to 13, as said below
- drop_masks: int32 [128, 4], P('dp'), may hold values 0 or 1
- norm_gains: float32 [2, 2, 256], replicated, may hold values from 0.25 to 1.75
- norm_shifts: float32 [2, 2, 256], replicated, may hold values from -2 to 2
- entry_weight: bfloat16 [2, 256, 768], replicated, may hold values from -0.5 to 0.5
- entry_bias: float32 [2, 512], replicated, may hold values from -3 to 3
- position_kernel: float32 [2, 3, 3, 256], replicated, may hold values from -2 to 2
- position_bias: float32 [2, 256], replicated, may hold values from -2 to 2
- exit_weight: bfloat16 [2, 256, 256], replicated, may hold values from -0.5 to 0.5
- exit_bias: float32 [2, 256], replicated, may hold values from -2 to 2
- expand_weight: bfloat16 [2, 256, 1024], replicated, may hold values from -0.375 to 0.375
- expand_bias: float32 [2, 1024], replicated, may hold values from -2 to 2
- shrink_weight: bfloat16 [2, 1024, 256], replicated, may hold values from -0.25 to 0.25
- shrink_bias: float32 [2, 256], replicated, may hold values from -2 to 2
Outputs:
- activations: bfloat16 [128, 14, 14, 256], P('dp', 'row', 'col')
- input_gradient: float32 [128, 14, 14, 256], P('dp', 'row', 'col')
- norm_gains_gradient: float32 [2, 2, 256], replicated
- norm_shifts_gradient: float32 [2, 2, 256], replicated
- entry_weight_gradient: float32 [2, 256, 768], replicated
- entry_bias_gradient: float32 [2, 512], replicated
- position_kernel_gradient: float32 [2, 3, 3, 256], replicated
- position_bias_gradient: float32 [2, 256], replicated
- exit_weight_gradient: float32 [2, 256, 256], replicated
- exit_bias_gradient: float32 [2, 256], replicated
- expand_weight_gradient: float32 [2, 256, 1024], replicated
- expand_bias_gradient: float32 [2, 1024], replicated
- shrink_weight_gradient: float32 [2, 1024, 256], replicated
- shrink_bias_gradient: float32 [2, 256], replicated
Inputs may be any that keep to these rules, and one draw needn't show every extreme that they name: `mix_partner`: of the 32 mixup and cutmix partners of the images of one index of dp, at most 4 lie on any one index of dp, and in every draw some pair of indices reaches 4. `cut_partner`: counted with mix_partner in its bound. `corners`: each box spans 4 to 6 rows and 4 to 6 columns, bottom and right exclusive.
All inputs are finite; a program needn't handle non-finite values. No bound on the sum of `drop_masks` on one device may be relied on, other than what follows from the above.
Results may differ from a plain program's by a relative error of at most 0.017.
Values may be sent and summed in bfloat16 or wider, within the bound.
No kernel may reach another device: no remote copies, remote signals or barrier semaphores. Data moves between devices by JAX's collectives and lax.ppermute only.
A program may use at most 128 MiB of HBM per device.

v0:
```python
import functools

import jax
import jax.numpy as jnp
from jax import lax
from jax.experimental import pallas as pl
from jax.experimental.pallas import tpu as pltpu
from jax.sharding import PartitionSpec as P

TILE = 7
PAD = 56
HEAD_DIM = 32
SIDE_HEADS = 4
HALF = 128
WIN = 2 * PAD
CHUNK = 8 * PAD
LANES = SIDE_HEADS * 128
SCALE = HEAD_DIM ** (-0.5)
LOG2E = 1.4426950408889634
EPS = 1e-05
BF = jnp.bfloat16
F32 = jnp.float32


def dot_nn(a, b):
    return lax.dot_general(a, b, (((1,), (0,)), ((), ())), preferred_element_type=F32)


def dot_nt(a, b):
    return lax.dot_general(a, b, (((1,), (1,)), ((), ())), preferred_element_type=F32)


def dot_tn(a, b):
    return lax.dot_general(a, b, (((0,), (0,)), ((), ())), preferred_element_type=F32)


def norm_parts(values):
    centered = values - jnp.mean(values, axis=-1, keepdims=True)
    inverse = lax.rsqrt(jnp.mean(centered * centered, axis=-1, keepdims=True) + EPS)
    return centered * inverse, inverse


def norm_back(delta, hat, inverse, gain):
    scaled = delta * gain
    first = jnp.mean(scaled, axis=-1, keepdims=True)
    second = jnp.mean(scaled * hat, axis=-1, keepdims=True)
    return inverse * (scaled - first - hat * second)


def gelu_parts(values):
    chance = 0.5 + 0.5 * lax.erf(values * (0.5**0.5))
    density = jnp.exp2(values * values * (-0.5 * LOG2E)) * 0.3989422804014327
    return chance, density


def row_sums(values):
    count, width = values.shape
    return jnp.sum(values.reshape(count // 8, 8, width), axis=0)


def scale_rows(place_ref, mask_ref, column):
    scales = [
        mask_ref[column, 4 * place_ref[3] + i].astype(F32) * 1.25 for i in range(4)
    ]
    columns = [jnp.full((PAD, 1), scale, F32) for scale in scales]
    return jnp.concatenate(columns * (CHUNK // (4 * PAD)), axis=0)


def add_row(acc_ref, row, values):
    acc_ref[row] += values


def spread_heads(values):
    lane = lax.broadcasted_iota(jnp.int32, values.shape, 1) // HEAD_DIM
    empty = jnp.zeros((128 - WIN, HALF), F32)
    blocks = []
    for head in range(SIDE_HEADS):
        blocks.append(jnp.where(lane == head, values, 0.0))
        blocks.append(empty)
    return jnp.concatenate(blocks, axis=0).astype(BF)


def over_keys(weights, values):
    weights = fill_rows(weights)
    stacked = jnp.concatenate(
        [weights[:, head * 128 : (head + 1) * 128] for head in range(SIDE_HEADS)], axis=0
    )
    return dot_tn(stacked, spread_heads(values))[:WIN]


def fill_rows(values):
    empty = jnp.zeros((128 - WIN, values.shape[1]), values.dtype)
    return jnp.concatenate([values, empty], axis=0)


def valid_column(shape):
    return lax.broadcasted_iota(jnp.int32, shape, 1) != 7


def valid_rows(shape):
    return lax.broadcasted_iota(jnp.int32, shape, 0) % 8 != 7


def column_shifts(values, across):
    cube = values.reshape(2 * TILE, 8, HALF)
    if not across:
        return (pltpu.roll(cube, 1, 1), cube, pltpu.roll(cube, 7, 1))
    left, right = cube[:TILE], cube[TILE:]
    column = lax.broadcasted_iota(jnp.int32, left.shape, 1)
    before = jnp.concatenate(
        [
            pltpu.roll(left, 1, 1),
            jnp.where(column == 0, pltpu.roll(left, 2, 1), pltpu.roll(right, 1, 1)),
        ],
        axis=0,
    )
    after = jnp.concatenate(
        [
            jnp.where(column == 6, pltpu.roll(right, 6, 1), pltpu.roll(left, 7, 1)),
            pltpu.roll(right, 7, 1),
        ],
        axis=0,
    )
    return (before, cube, after)


def row_shift(cube, step, across):
    if step == 0:
        return cube
    empty = jnp.zeros((1, 8, HALF), F32)

    def move(part):
        if step < 0:
            return jnp.concatenate([empty, part[:-1]], axis=0)
        return jnp.concatenate([part[1:], empty], axis=0)

    if across:
        return jnp.concatenate([move(cube[:TILE]), move(cube[TILE:])], axis=0)
    return move(cube)


def window_conv(shifts, kernel_at, across):
    total = None
    for i in range(3):
        part = None
        for j in range(3):
            term = kernel_at(i, j) * shifts[j]
            part = term if part is None else part + term
        part = row_shift(part, i - 1, across)
        total = part if total is None else total + part
    return total.reshape(WIN, HALF)


def window_rows(across, window):
    side, image = window // 4, window % 4
    if across:
        first, second = 2 * side, 2 * side + 1
    else:
        first, second = side, 2 + side
    return (
        pl.multiple_of((first * 4 + image) * PAD, 8),
        pl.multiple_of((second * 4 + image) * PAD, 8),
    )


def take_window(ref, at, lane):
    return jnp.concatenate(
        [ref[pl.ds(at[0], PAD), lane : lane + HALF], ref[pl.ds(at[1], PAD), lane : lane + HALF]],
        axis=0,
    )


def put_window(ref, at, lane, values):
    ref[pl.ds(at[0], PAD), lane : lane + HALF] = values[:PAD]
    ref[pl.ds(at[1], PAD), lane : lane + HALF] = values[PAD:]


def round_bf(values):
    return values.astype(BF).astype(F32)


def attention_forward(
    block, hidden_ref, gains, shifts, entry_w, entry_b, conv_k, conv_b, wide, stripe, win_out, chance_out
):
    width = hidden_ref.shape[1]

    @pl.loop(0, 2)
    def _(t):
        rows = chunk(t)
        hat, _ = norm_parts(hidden_ref[rows, :])
        normed = (hat * gains[block, 0:1, :] + shifts[block, 0:1, :]).astype(BF)
        for part in range(3):
            out = dot_nn(normed, entry_w[block, :, part * width : (part + 1) * width])
            if part != 1:
                at = 0 if part == 0 else width
                out = out + entry_b[block : block + 1, at : at + width]
            wide[rows, part * width : (part + 1) * width] = round_bf(out)

    for direction in range(2):
        across = direction == 0
        lane = direction * HALF

        @pl.loop(0, 8, unroll=4)
        def _(window, across=across, lane=lane, direction=direction):
            at = window_rows(across, window)
            queries = take_window(wide, at, lane)
            keys = take_window(wide, at, width + lane)
            values = take_window(wide, at, 2 * width + lane)
            keys_bf = keys.astype(BF)
            win_out[direction * 8 + window, :, 0:HALF] = queries.astype(BF)
            win_out[direction * 8 + window, :, HALF : 2 * HALF] = keys_bf
            win_out[direction * 8 + window, :, 2 * HALF : 3 * HALF] = values.astype(BF)
            scores = dot_nt(keys_bf, spread_heads(queries)).reshape(2 * TILE, 8, LANES)
            scores = jnp.where(valid_column((1, 8, LANES)), scores, -1e30)
            top = jnp.max(jnp.max(scores, axis=0), axis=0, keepdims=True)
            lifted = jnp.exp2((scores - top) * (SCALE * LOG2E))
            totals = jnp.sum(jnp.sum(lifted, axis=0), axis=0, keepdims=True)
            chances = (lifted * (1.0 / totals)).reshape(WIN, LANES).astype(BF)
            chance_out[direction * 8 + window] = chances
            attended = over_keys(chances, values)
            clean = jnp.where(valid_rows(values.shape), values, 0.0)
            position = window_conv(
                column_shifts(clean, across),
                lambda i, j: conv_k[i, j, block : block + 1, lane : lane + HALF],
                across,
            )
            put_window(
                stripe, at, lane, attended + position + conv_b[block : block + 1, lane : lane + HALF]
            )


def attention_backward(
    ready,
    block,
    win_in,
    chance_in,
    conv_k,
    stripe_delta,
    wide,
    conv_acc,
):
    width = stripe_delta.shape[1]
    for direction in range(2):
        ready(direction)
        across = direction == 0
        lane = direction * HALF

        @pl.loop(0, 8, unroll=4)
        def _(window, across=across, lane=lane, direction=direction):
            at = window_rows(across, window)
            out_delta = take_window(stripe_delta, at, lane)
            queries = win_in[direction * 8 + window, :, 0:HALF].astype(F32)
            keys = win_in[direction * 8 + window, :, HALF : 2 * HALF].astype(F32)
            values_bf = win_in[direction * 8 + window, :, 2 * HALF : 3 * HALF]
            values = values_bf.astype(F32)
            chances = chance_in[direction * 8 + window]
            delta_spread = spread_heads(out_delta)
            chance_delta = dot_nt(values_bf, delta_spread)
            cubes = (2 * TILE, 8, LANES)
            wide_chances = chances.astype(F32).reshape(cubes)
            weighted = wide_chances * chance_delta.reshape(cubes)
            common = jnp.sum(jnp.sum(weighted, axis=0), axis=0, keepdims=True)
            score_delta = (weighted - wide_chances * common).reshape(WIN, LANES).astype(BF)
            values_delta = dot_nn(chances, delta_spread)
            keys_delta = dot_nn(score_delta, spread_heads(queries)) * SCALE
            query_delta = over_keys(score_delta, keys) * SCALE
            keep = valid_rows(values.shape)
            clean = jnp.where(keep, values, 0.0)
            shifts = column_shifts(clean, across)
            cube = out_delta.reshape(2 * TILE, 8, HALF)
            for i in range(3):
                moved = row_shift(cube, 1 - i, across)
                for j in range(3):
                    conv_acc[3 * i + j, :, lane : lane + HALF] += jnp.sum(moved * shifts[j], axis=0)
            back = window_conv(
                column_shifts(out_delta, across),
                lambda i, j: conv_k[2 - i, 2 - j, block : block + 1, lane : lane + HALF],
                across,
            )
            values_delta = jnp.where(keep, values_delta + back, 0.0)
            put_window(wide, at, lane, query_delta)
            put_window(wide, at, width + lane, keys_delta)
            put_window(wide, at, 2 * width + lane, values_delta)


def chunk(t):
    return pl.ds(pl.multiple_of(t * CHUNK, CHUNK), CHUNK)


class Bundle:
    def __init__(self, place_ref, keep, away, chunks=1, spot=lambda chunk: chunk):
        self.place_ref, self.keep, self.away = place_ref, keep, away
        self.step, self.spot = keep.shape[0] // chunks, spot

    def put(self, at, values):
        values = values.astype(BF)
        half, step = self.keep.shape[0], self.step
        last = at + values.shape[0]
        first = at
        while first < last:
            stop = min(last, (first // step + 1) * step)
            number = first // half
            start = self.spot(first % half // step) * step
            inner, count = first % step, stop - first
            if not isinstance(start, int):
                start = pl.multiple_of(start, step)
            rows = pl.ds(start + inner, count)
            piece = values[first - at : stop - at]

            @pl.when(self.place_ref[2] == number)
            def _(piece=piece, rows=rows):
                self.keep[rows, :] = piece

            @pl.when(self.place_ref[2] != number)
            def _(piece=piece, rows=rows):
                self.away[rows, :] = piece

            first = stop


def put_squares(bundle, at, values, side):
    for part in range(values.shape[1] // side):
        bundle.put(at + part * side, values[:, part * side : (part + 1) * side])


def load_tiles(place_ref, tiles, hidden):
    for d, tile in enumerate(tiles):
        at = jnp.bitwise_xor(place_ref[3], d) * (4 * PAD)
        rows = pl.ds(pl.multiple_of(at, 4 * PAD), 4 * PAD)
        hidden[rows, :] = tile[...].astype(F32).reshape(4 * PAD, hidden.shape[1])


def store_tile(place_ref, tiles, t, values):
    count = CHUNK // (4 * PAD)
    values = values.reshape((count,) + tiles[0].shape).astype(BF)
    for part in range(count):
        for d, tile in enumerate(tiles):

            @pl.when(jnp.bitwise_xor(place_ref[3], d) == count * t + part)
            def _(tile=tile, part=part):
                tile[...] = values[part]


def first_kernel(
    spots,
    moves,
    place_ref,
    mask_ref,
    mixed_a,
    mixed_b,
    mixed_c,
    mixed_d,
    gains,
    shifts,
    entry_b,
    conv_k,
    conv_b,
    exit_b,
    expand_b,
    shrink_b,
    cot_a,
    cot_b,
    cot_c,
    cot_d,
    entry_w,
    exit_w,
    expand_w,
    shrink_w,
    vec_out,
    keep_out,
    away_out,
    act_a,
    act_b,
    act_c,
    act_d,
    active0_out,
    slope0_out,
    win0_out,
    chance0_out,
    stripe0_out,
    mid0_out,
    win1_out,
    chance1_out,
    stripe1_out,
    hidden1_out,
    grad_out,
    hidden,
    wide,
    stripe,
    active1,
    pre1,
    feed1,
    inner1,
):
    width = hidden.shape[1]
    hidden_units = expand_w.shape[2]
    bundle = Bundle(place_ref, keep_out, away_out, len(spots), lambda chunk: spots[chunk])
    vec_out[...] = jnp.zeros(vec_out.shape, F32)
    moves.fetch(entry_w)
    load_tiles(place_ref, (mixed_a, mixed_b, mixed_c, mixed_d), hidden)
    moves.need(entry_w)
    moves.fetch(exit_w, expand_w, shrink_w, cot_a, cot_b, cot_c, cot_d)

    for block in range(2):
        win_out, chance_out, stripe_out = (
            (win0_out, chance0_out, stripe0_out),
            (win1_out, chance1_out, stripe1_out),
        )[block]
        attention_forward(
            block, hidden, gains, shifts, entry_w, entry_b, conv_k, conv_b, wide, stripe, win_out, chance_out
        )
        moves.send(win_out, chance_out)
        moves.need(exit_w, expand_w, shrink_w)
        if block == 1:
            moves.need(cot_a, cot_b, cot_c, cot_d)
            load_tiles(place_ref, (cot_a, cot_b, cot_c, cot_d), grad_out)

        @pl.loop(0, 2)
        def _(t, block=block, stripe_out=stripe_out):
            rows = chunk(t)
            striped = stripe[rows, :].astype(BF)
            stripe_out[rows, :] = striped
            branch = dot_nn(striped, exit_w[block]) + exit_b[block : block + 1, :]
            midway = hidden[rows, :] + scale_rows(place_ref, mask_ref, 2 * block) * branch
            if block == 0:
                mid0_out[rows, :] = midway
            hat, inverse = norm_parts(midway)
            normed = (hat * gains[block, 1:2, :] + shifts[block, 1:2, :]).astype(BF)
            feed_scale = scale_rows(place_ref, mask_ref, 2 * block + 1)
            feed = shrink_b[block : block + 1, :]
            if block == 1:
                inner1[rows, :] = normed
                gradient = grad_out[rows, :]
                feed_delta = (feed_scale * gradient).astype(BF)
                feed1[rows, :] = feed_delta
                add_row(vec_out, 4, row_sums(feed_delta.astype(F32)))
                inner_delta = jnp.zeros((CHUNK, width), F32)
            for part in range(hidden_units // width):
                at = slice(part * width, (part + 1) * width)
                pre_act = dot_nn(normed, expand_w[block, :, at]) + expand_b[block : block + 1, at]
                chance, density = gelu_parts(pre_act)
                active = (pre_act * chance).astype(BF)
                slope = chance + pre_act * density
                if block == 0:
                    active0_out[rows, at] = active
                    slope0_out[rows, at] = slope.astype(BF)
                else:
                    active1[rows, at] = active
                    pre_delta = (dot_nt(feed_delta, shrink_w[block, at, :]) * slope).astype(BF)
                    pre1[rows, at] = pre_delta
                    add_row(vec_out, part, row_sums(pre_delta.astype(F32)))
                    inner_delta = inner_delta + dot_nt(pre_delta, expand_w[block, :, at])
                feed = feed + dot_nn(active, shrink_w[block, at, :])
            output = midway + feed_scale * feed
            if block == 0:
                hidden[rows, :] = output
                hidden1_out[rows, :] = output
            else:
                store_tile(place_ref, (act_a, act_b, act_c, act_d), t, output)
                add_row(vec_out, 5, row_sums(inner_delta * hat))
                add_row(vec_out, 6, row_sums(inner_delta))
                grad_out[rows, :] = gradient + norm_back(
                    inner_delta, hat, inverse, gains[block, 1:2, :]
                )

        moves.send(stripe_out)
        if block == 0:
            moves.send(mid0_out, active0_out, slope0_out, hidden1_out)
        else:
            moves.send(act_a, act_b, act_c, act_d, grad_out)

    put_squares(bundle, 0, dot_tn(inner1[...], pre1[...]), width)
    for part in range(hidden_units // width):
        bundle.put(
            hidden_units + part * width,
            dot_tn(active1[:, part * width : (part + 1) * width], feed1[...]),
        )


def delta_rows(block, place_ref, mask_ref, exit_w, grad_ref, stripe_delta, branch_delta, vec_out, at):
    @pl.loop(0, 2)
    def _(t):
        rows = chunk(t)
        rounded = (scale_rows(place_ref, mask_ref, 2 * block) * grad_ref[rows, :]).astype(BF)
        branch_delta[rows, :] = rounded
        add_row(vec_out, at, row_sums(rounded.astype(F32)))
        out = round_bf(dot_nt(rounded, exit_w[block]))
        stripe_delta[rows, :] = out
        add_row(vec_out, at + 1, row_sums(out))


def entry_backward(block, hidden_ref, gains, shifts, entry_w, grad_ref, wide, wide_bf, normed_bf, vec_out, at, emit):
    width = hidden_ref.shape[1]

    @pl.loop(0, 2)
    def _(t):
        rows = chunk(t)
        hat, inverse = norm_parts(hidden_ref[rows, :])
        normed_bf[rows, :] = (hat * gains[block, 0:1, :] + shifts[block, 0:1, :]).astype(BF)
        delta = jnp.zeros((CHUNK, width), F32)
        for part in range(3):
            lanes = slice(part * width, (part + 1) * width)
            rounded = wide[rows, lanes].astype(BF)
            wide_bf[rows, lanes] = rounded
            if part != 1:
                add_row(vec_out, at + part // 2, row_sums(rounded.astype(F32)))
            delta = delta + dot_nt(rounded, entry_w[block, :, lanes])
        add_row(vec_out, at + 2, row_sums(delta * hat))
        add_row(vec_out, at + 3, row_sums(delta))
        emit(t, rows, grad_ref[rows, :] + norm_back(delta, hat, inverse, gains[block, 0:1, :]))


def second_kernel(
    moves,
    place_ref,
    mask_ref,
    gains,
    shifts,
    conv_k,
    grad_in,
    exit_w,
    win1,
    chance1,
    hidden1,
    entry_w,
    stripe1,
    mid0,
    shrink_w,
    slope0,
    expand_w,
    active0,
    stripe0,
    vec_out,
    conv_out,
    keep_out,
    away_out,
    grad_out,
    stripe_delta_out,
    stripe_delta,
    branch_delta,
    wide,
    wide_bf,
    normed_bf,
    feed0,
    pre0,
):
    grad = grad_out
    width = grad.shape[1]
    hidden_units = expand_w.shape[2]
    bundle = Bundle(
        place_ref, keep_out, away_out, 4, lambda chunk: jnp.bitwise_xor(place_ref[5], chunk)
    )
    vec_out[...] = jnp.zeros(vec_out.shape, F32)
    conv_out[...] = jnp.zeros(conv_out.shape, F32)
    moves.fetch(grad_in, exit_w)
    moves.fetch(win1, chance1, part=0)
    moves.need(grad_in, exit_w)
    moves.fetch(win1, chance1, part=1)
    delta_rows(1, place_ref, mask_ref, exit_w, grad_in, stripe_delta, branch_delta, vec_out, 0)

    def ready(direction):
        moves.need(win1, chance1, part=direction)
        if direction == 0:
            moves.fetch(hidden1, entry_w, stripe1)
        else:
            moves.fetch(mid0, shrink_w, slope0, expand_w, active0, stripe0)

    attention_backward(ready, 1, win1, chance1, conv_k, stripe_delta, wide, conv_out)

    def emit(t, rows, values):
        grad[rows, :] = values

    moves.need(hidden1, entry_w)
    entry_backward(
        1, hidden1, gains, shifts, entry_w, grad_in, wide, wide_bf, normed_bf, vec_out, 2, emit
    )
    put_squares(bundle, 0, dot_tn(normed_bf[...], wide_bf[...]), width)
    moves.need(stripe1)
    bundle.put(3 * width, dot_tn(stripe1[...], branch_delta[...]))
    moves.need(mid0, shrink_w, slope0, expand_w)

    @pl.loop(0, 2)
    def _(t):
        rows = chunk(t)
        gradient = grad[rows, :]
        hat, inverse = norm_parts(mid0[rows, :])
        normed_bf[rows, :] = (hat * gains[0, 1:2, :] + shifts[0, 1:2, :]).astype(BF)
        feed_delta = (scale_rows(place_ref, mask_ref, 1) * gradient).astype(BF)
        feed0[rows, :] = feed_delta
        add_row(vec_out, 6, row_sums(feed_delta.astype(F32)))
        inner_delta = jnp.zeros((CHUNK, width), F32)
        for part in range(hidden_units // width):
            at = slice(part * width, (part + 1) * width)
            pre_delta = (
                dot_nt(feed_delta, shrink_w[0, at, :]) * slope0[rows, at].astype(F32)
            ).astype(BF)
            pre0[rows, at] = pre_delta
            add_row(vec_out, 7 + part, row_sums(pre_delta.astype(F32)))
            inner_delta = inner_delta + dot_nt(pre_delta, expand_w[0, :, at])
        add_row(vec_out, 11, row_sums(inner_delta * hat))
        add_row(vec_out, 12, row_sums(inner_delta))
        grad[rows, :] = gradient + norm_back(inner_delta, hat, inverse, gains[0, 1:2, :])

    delta_rows(0, place_ref, mask_ref, exit_w, grad, stripe_delta_out, branch_delta, vec_out, 13)
    moves.send(grad_out, stripe_delta_out)
    moves.need(active0, stripe0)
    put_squares(bundle, 4 * width, dot_tn(normed_bf[...], pre0[...]), width)
    for part in range(hidden_units // width):
        bundle.put(
            (8 + part) * width,
            dot_tn(active0[:, part * width : (part + 1) * width], feed0[...]),
        )
    bundle.put(12 * width, dot_tn(stripe0[...], branch_delta[...]))


def third_kernel(
    moves,
    place_ref,
    gains,
    shifts,
    conv_k,
    vec1,
    vec2,
    conv2,
    mixed_a,
    mixed_b,
    mixed_c,
    mixed_d,
    stripe_delta,
    win0,
    chance0,
    entry_w,
    grad_in,
    out_a,
    out_b,
    out_c,
    out_d,
    keep_out,
    away_out,
    hidden,
    wide,
    wide_bf,
    normed_bf,
    vec3,
    conv3,
    flat,
):
    width = hidden.shape[1]
    bundle = Bundle(
        place_ref, keep_out, away_out, 4, lambda chunk: jnp.bitwise_xor(place_ref[5], chunk)
    )
    vec3[...] = jnp.zeros(vec3.shape, F32)
    conv3[...] = jnp.zeros(conv3.shape, F32)
    moves.fetch(stripe_delta)
    moves.fetch(win0, chance0, part=0)
    moves.need(stripe_delta)
    moves.fetch(win0, chance0, part=1)

    def ready(direction):
        moves.need(win0, chance0, part=direction)
        if direction == 0:
            moves.fetch(mixed_a, mixed_b, mixed_c, mixed_d, entry_w, grad_in)

    attention_backward(ready, 0, win0, chance0, conv_k, stripe_delta, wide, conv3)

    def emit(t, rows, values):
        store_tile(place_ref, (out_a, out_b, out_c, out_d), t, values)

    moves.need(mixed_a, mixed_b, mixed_c, mixed_d, entry_w, grad_in)
    load_tiles(place_ref, (mixed_a, mixed_b, mixed_c, mixed_d), hidden)
    entry_backward(
        0, hidden, gains, shifts, entry_w, grad_in, wide, wide_bf, normed_bf, vec3, 0, emit
    )
    moves.send(out_a, out_b, out_c, out_d)
    flat[...] = jnp.zeros(flat.shape, F32)
    at = 0
    for ref in (vec1, vec2, conv2, vec3, conv3):
        flat[at : at + ref.shape[0], :] = jnp.sum(ref[...], axis=1)
        at += ref.shape[0]
    spread = dot_tn(normed_bf[...], wide_bf[...])
    half = keep_out.shape[0]
    middle = width // 2
    lots = flat.shape[0] // 2
    bundle.put(0, spread[:, :width])
    bundle.put(width, spread[:middle, width : 2 * width])
    bundle.put(width + middle, flat[:lots, :])
    bundle.put(half, spread[middle:, width : 2 * width])
    bundle.put(half + middle, spread[:, 2 * width :])
    bundle.put(half + middle + width, flat[lots:, :])


def untangle(source, flat, target):
    count, width = source.shape[2:]
    lanes = flat.shape[0]
    for row in range(TILE):
        flat[:, pl.ds(row * 8 + 7, count, stride=PAD), :] = jnp.zeros((lanes, count, 128), F32)
        for col in range(TILE):
            token = source[row, col].astype(F32)
            for lane in range(lanes):
                flat[lane, pl.ds(row * 8 + col, count, stride=PAD), :] = token[
                    :, lane * 128 : (lane + 1) * 128
                ]

    @pl.loop(0, count)
    def _(n):
        rows = pl.ds(pl.multiple_of(n * PAD, 8), PAD)
        tile = jnp.concatenate([flat[lane, rows, :] for lane in range(lanes)], axis=1)
        target(n, tile.reshape(TILE, 8, width).astype(BF))


def owner_of(wanted, count):
    if count & (count - 1) == 0:
        return lax.shift_right_logical(wanted, count.bit_length() - 1)
    return lax.div(wanted, count)


def pick_kernel(
    place_ref, mix_ref, cut_ref, images_ref, index_out, take_out, sent_out, own_out, flat, counts
):
    count = images_ref.shape[2]
    slots = sent_out.shape[0]
    capacity = slots // counts.shape[0]
    me = place_ref[0]

    def put(n, tile):
        own_out[n] = tile

    untangle(images_ref, flat, put)

    @pl.loop(0, slots, unroll=8)
    def _(s):
        index_out[s] = count

    @pl.loop(0, counts.shape[0])
    def _(g):
        counts[g] = 0
        rank = g * capacity
        for ref in (mix_ref, cut_ref):
            for j in range(count):
                wanted = ref[g * count + j]
                owner = owner_of(wanted, count)
                hit = owner == me
                index_out[jnp.where(hit, rank, slots)] = wanted - owner * count
                rank = rank + hit.astype(jnp.int32)

    @pl.loop(0, slots)
    def _(s):
        sent_out[s] = own_out[jnp.minimum(index_out[s], count - 1)]

    for part, ref in enumerate((mix_ref, cut_ref)):

        @pl.loop(0, count)
        def _(j, part=part, ref=ref):
            owner = owner_of(ref[me * count + j], count)
            rank = counts[owner]
            take_out[part * count + j] = owner * capacity + rank
            counts[owner] = rank + 1


def deal_kernel(place_ref, source, out_a, out_b, out_c, out_d, flat):
    outs = (out_a, out_b, out_c, out_d)
    share = out_a.shape[0]

    def put(n, tile):
        for d, out in enumerate(outs):

            @pl.when(jnp.bitwise_xor(place_ref[3], d) == n // share)
            def _(out=out):
                out[n % share] = tile

    untangle(source, flat, put)


def inside_box(corner_ref, n, place_ref):
    shape = (TILE, 8, 1)
    row = place_ref[1] * TILE + lax.broadcasted_iota(jnp.int32, shape, 0)
    col = place_ref[2] * TILE + lax.broadcasted_iota(jnp.int32, shape, 1)
    hit = (
        (row >= corner_ref[0, n])
        & (row < corner_ref[1, n])
        & (col >= corner_ref[2, n])
        & (col < corner_ref[3, n])
    )
    return jnp.where(hit, 1.0, 0.0)


def mix_kernel(
    place_ref, take_ref, corner_ref, ratio_ref, arrived, own_ref, out_a, out_b, out_c, out_d
):
    count = own_ref.shape[0]
    share = out_a.shape[0]
    for d, out in enumerate((out_a, out_b, out_c, out_d)):

        @pl.loop(0, share)
        def _(i, d=d, out=out):
            n = jnp.bitwise_xor(place_ref[3], d) * share + i
            inside = inside_box(corner_ref, n, place_ref)
            ratio = ratio_ref[n]
            own = own_ref[n].astype(F32)
            blend = arrived[take_ref[n]].astype(F32)
            cut = arrived[take_ref[count + n]].astype(F32)
            mixed = inside * cut + (1.0 - inside) * (ratio * own + (1.0 - ratio) * blend)
            out[i] = mixed.astype(BF)


def split_kernel(
    place_ref, take_ref, corner_ref, ratio_ref, grad_a, grad_b, grad_c, grad_d, out_ref
):
    share = grad_a.shape[0]
    count = 4 * share
    if out_ref.shape[0] > 2 * count:
        out_ref[...] = jnp.zeros(out_ref.shape, BF)
    for d, grad_ref in enumerate((grad_a, grad_b, grad_c, grad_d)):

        @pl.loop(0, share)
        def _(i, d=d, grad_ref=grad_ref):
            n = jnp.bitwise_xor(place_ref[3], d) * share + i
            inside = inside_box(corner_ref, n, place_ref)
            gradient = grad_ref[i].astype(F32)
            cut = inside * gradient
            out_ref[take_ref[n]] = ((1.0 - ratio_ref[n]) * (gradient - cut)).astype(BF)
            out_ref[take_ref[count + n]] = cut.astype(BF)


def join_kernel(
    place_ref,
    index_ref,
    corner_ref,
    ratio_ref,
    grad_a,
    grad_b,
    grad_c,
    grad_d,
    back_ref,
    out_ref,
    total,
):
    count, width = out_ref.shape[2:]
    share = grad_a.shape[0]

    def tile_rows(n):
        return pl.ds(pl.multiple_of(n * PAD, 8), PAD)

    for d, grad_ref in enumerate((grad_a, grad_b, grad_c, grad_d)):

        @pl.loop(0, share)
        def _(i, d=d, grad_ref=grad_ref):
            n = jnp.bitwise_xor(place_ref[3], d) * share + i
            outside = 1.0 - inside_box(corner_ref, n, place_ref)
            kept = ratio_ref[n] * outside * grad_ref[i].astype(F32)
            kept = kept.reshape(PAD, width)
            for lane in range(total.shape[0]):
                total[lane, tile_rows(n), :] = kept[:, lane * 128 : (lane + 1) * 128]

    @pl.loop(0, back_ref.shape[0])
    def _(s):
        piece = back_ref[s].astype(F32).reshape(PAD, width)
        for lane in range(total.shape[0]):
            total[lane, tile_rows(index_ref[s]), :] += piece[:, lane * 128 : (lane + 1) * 128]

    for row in range(TILE):
        for col in range(TILE):
            out_ref[row, col] = jnp.concatenate(
                [
                    total[lane, pl.ds(row * 8 + col, count, stride=PAD), :]
                    for lane in range(total.shape[0])
                ],
                axis=1,
            )


def lay_kernel(place_ref, act_a, act_b, act_c, act_d, out_ref, flat):
    count, width = out_ref.shape[2:]
    share = act_a.shape[0]
    for d, act_ref in enumerate((act_a, act_b, act_c, act_d)):

        @pl.loop(0, share)
        def _(i, d=d, act_ref=act_ref):
            n = jnp.bitwise_xor(place_ref[3], d) * share + i
            tile = act_ref[i].astype(F32).reshape(PAD, width)
            for lane in range(flat.shape[0]):
                flat[lane, pl.ds(pl.multiple_of(n * PAD, 8), PAD), :] = tile[
                    :, lane * 128 : (lane + 1) * 128
                ]

    for row in range(TILE):
        for col in range(TILE):
            out_ref[row, col] = jnp.concatenate(
                [
                    flat[lane, pl.ds(row * 8 + col, count, stride=PAD), :]
                    for lane in range(flat.shape[0])
                ],
                axis=1,
            ).astype(BF)


def unpack_kernel(
    ranks,
    counts,
    place_ref,
    *refs,
):
    pieces, refs = refs[:8], refs[8:]
    outs, (vectors, *buffers, send_sem) = refs[:12], refs[12:]
    (
        gain_out,
        shift_out,
        entry_out,
        entry_b_out,
        conv_out,
        conv_b_out,
        exit_out,
        exit_b_out,
        expand_out,
        expand_b_out,
        shrink_out,
        shrink_b_out,
    ) = buffers
    width = exit_out.shape[1]
    units = expand_out.shape[2]
    middle = width // 2

    def squares(out_ref, block, count):
        return [(out_ref, block, 0, part * width, width) for part in range(count)]

    def tall(out_ref, block, count):
        return [(out_ref, block, part * width, 0, width) for part in range(count)]

    plans = (
        squares(expand_out, 1, units // width) + tall(shrink_out, 1, units // width),
        [
            (entry_out, 0, 0, 0, width),
            (entry_out, 0, 0, width, middle),
            (vectors, None, 0, 0, middle),
            (entry_out, 0, middle, width, middle),
            (entry_out, 0, 0, 2 * width, width),
        ],
        squares(entry_out, 1, 3)
        + tall(exit_out, 1, 1)
        + squares(expand_out, 0, units // width)
        + tall(shrink_out, 0, units // width)
        + tall(exit_out, 0, 1),
    )
    inner_ranks = ranks // 4
    moves = []
    base = 0
    for plan, count in zip(plans, counts):
        at = 0
        for out_ref, block, first_row, lane, length in plan:
            done = 0
            while done < length:
                step = min(length - done, count - at % count)
                moves.append((out_ref, block, first_row + done, lane, base, count, at, step))
                at += step
                done += step
        base += count
    big = (expand_out, shrink_out, entry_out, exit_out)
    leaving = []

    def leave(buffer, out):
        copy = pltpu.make_async_copy(buffer, out, send_sem.at[len(leaving)])
        leaving.append(copy)
        return copy

    def place_parts(target, wanted, col, own):
        for out_ref, block, first_row, lane, base, count, at, step in moves:
            if out_ref is not target or block != wanted:
                continue
            shard, start = at // count, base + at % count
            half, shard = shard // ranks, shard % ranks
            first, inner = shard // inner_ranks, shard % inner_ranks
            piece = pieces[4 * (col ^ half) + (own ^ first)]
            inner = jnp.bitwise_xor(place_ref[6], inner)
            values = piece[inner, start : start + step, :].astype(F32)
            place = slice(first_row, first_row + step)
            if block is None:
                out_ref[place, :] = values
            else:
                out_ref[block, place, lane : lane + width] = values

    first_sends = {}
    for block in (1, 0):
        for target in big:
            i = [j for j, ref in enumerate(buffers) if ref is target][0]
            first_sends[block, i] = leave(target.at[block], outs[i].at[block])
    for col in range(2):
        for own in range(4):

            @pl.when((place_ref[2] == col) & (place_ref[5] == own))
            def _(col=col, own=own):
                place_parts(vectors, None, col, own)
                for (block, i), copy in first_sends.items():
                    place_parts(buffers[i], block, col, own)
                    copy.start()

    def line(n):
        return vectors[n : n + 1, :]

    gain_out[0] = jnp.concatenate([line(33), line(18)], axis=0)
    gain_out[1] = jnp.concatenate([line(11), line(5)], axis=0)
    shift_out[0] = jnp.concatenate([line(34), line(19)], axis=0)
    shift_out[1] = jnp.concatenate([line(12), line(6)], axis=0)
    for part in range(2):
        lanes = slice(part * width, (part + 1) * width)
        entry_b_out[:, lanes] = jnp.concatenate([line(31 + part), line(9 + part)], axis=0)
    for i in range(3):
        for j in range(3):
            conv_out[i, j] = jnp.concatenate(
                [line(35 + 3 * i + j), line(22 + 3 * i + j)], axis=0
            )
    conv_b_out[...] = jnp.concatenate([line(21), line(8)], axis=0)
    exit_b_out[...] = jnp.concatenate([line(20), line(7)], axis=0)
    for part in range(units // width):
        lanes = slice(part * width, (part + 1) * width)
        expand_b_out[:, lanes] = jnp.concatenate([line(14 + part), line(part)], axis=0)
    shrink_b_out[...] = jnp.concatenate([line(13), line(4)], axis=0)
    for buffer, out in zip(buffers, outs):
        if not any(buffer is ref for ref in big):
            leave(buffer, out).start()
    for copy in leaving:
        copy.wait()


SMEM = pl.BlockSpec(memory_space=pltpu.SMEM)
VMEM = pl.BlockSpec(memory_space=pltpu.VMEM)


ANYWHERE = pl.BlockSpec(memory_space=pl.ANY)
FAR = pl.BlockSpec(memory_space=pltpu.HBM)


def far(values):
    return pltpu.with_memory_space_constraint(values, pltpu.HBM)


class Moves:
    def __init__(self, fetched, sent):
        self.fetched, self.sent = dict(fetched), dict(sent)
        self.waited, self.started = set(), set()

    def copies(self, ref, part):
        copies = self.fetched.get(id(ref), [])
        return [
            ((id(ref), i), copy)
            for i, copy in enumerate(copies)
            if part is None or len(copies) == 1 or i == part
        ]

    def fetch(self, *refs, part=None):
        for ref in refs:
            for key, copy in self.copies(ref, part):
                if key not in self.started:
                    copy.start()
                    self.started.add(key)

    def need(self, *refs, part=None):
        self.fetch(*refs, part=part)
        for ref in refs:
            for key, copy in self.copies(ref, part):
                if key not in self.waited:
                    copy.wait()
                    self.waited.add(key)

    def send(self, *refs):
        for ref in refs:
            if id(ref) in self.sent:
                self.sent[id(ref)].start()
                self.started.add(id(ref))

    def finish(self):
        for key, copies in self.fetched.items():
            for i, copy in enumerate(copies):
                if (key, i) not in self.started:
                    copy.start()
                if (key, i) not in self.waited:
                    copy.wait()
        for key, copy in self.sent.items():
            if key not in self.started:
                copy.start()
        for copy in self.sent.values():
            copy.wait()


def halves(ref):
    if ref.shape[-2] != WIN:
        return [pl.ds(0, ref.shape[0])]
    count = ref.shape[0] // 2
    return [pl.ds(0, count), pl.ds(count, count)]


def run(
    kernel,
    scalars,
    arrays,
    outs,
    scratch=(),
    flops=0,
    name=None,
    after=(),
    scalar_outs=(),
    lazy=None,
    vmem=16,
    near=((), ()),
):
    outs = list(outs)
    first_in, first_out = (len(arrays), len(outs)) if lazy is None else lazy
    eager, late = list(arrays[:first_in]), list(arrays[first_in:])
    n_in = len(scalars) + len(eager)
    scratch_shapes = [
        kind if dtype is None else pltpu.VMEM(kind, dtype) for kind, dtype in scratch
    ]
    n_own = len(scratch_shapes)
    n_late, n_sent = len(late), len(outs) - first_out
    if lazy is not None:
        scratch_shapes += [pltpu.VMEM(a.shape, a.dtype) for a in late]
        scratch_shapes += [pltpu.VMEM(*out) for out in outs[first_out:]]
        scratch_shapes += [pltpu.SemaphoreType.DMA((n_late, 2)), pltpu.SemaphoreType.DMA((max(n_sent, 1),))]

    def body(*refs):
        given, refs = refs[:n_in], refs[n_in:]
        sources, refs = refs[:n_late], refs[n_late + len(after) :]
        results, refs = refs[: len(scalar_outs) + first_out], refs[len(scalar_outs) + first_out :]
        targets, refs = refs[:n_sent], refs[n_sent:]
        own, refs = refs[:n_own], refs[n_own:]
        if lazy is None:
            kernel(*given, *results, *own)
            return
        buffers, leaving = refs[:n_late], refs[n_late : n_late + n_sent]
        fetch_sem, send_sem = refs[n_late + n_sent :]
        moves = Moves(
            [
                (
                    id(buffer),
                    [
                        pltpu.make_async_copy(source.at[part], buffer.at[part], fetch_sem.at[i, j])
                        for j, part in enumerate(halves(buffer))
                    ],
                )
                for i, (source, buffer) in enumerate(zip(sources, buffers))
            ],
            [
                (id(buffer), pltpu.make_async_copy(buffer, target, send_sem.at[i]))
                for i, (buffer, target) in enumerate(zip(leaving, targets))
            ],
        )
        kernel(moves, *given, *buffers, *results, *leaving, *own)
        moves.finish()

    out_shape = [jax.ShapeDtypeStruct(shape, dtype) for shape, dtype in scalar_outs] + [
        pltpu.HBM(shape, dtype)
        if lazy is not None and i not in near[1]
        else jax.ShapeDtypeStruct(shape, dtype)
        for i, (shape, dtype) in enumerate(outs)
    ]
    late = [
        a if i in near[0] else far(a)
        for i, a in enumerate(late, first_in)
    ]
    moved = sum(a.size * a.dtype.itemsize for a in arrays)
    return pl.pallas_call(
        body,
        out_shape=out_shape,
        in_specs=[SMEM] * len(scalars)
        + [VMEM] * len(eager)
        + [ANYWHERE if i in near[0] else FAR for i in range(first_in, len(arrays))]
        + [ANYWHERE] * len(after),
        out_specs=[SMEM] * len(scalar_outs)
        + [VMEM] * first_out
        + [ANYWHERE if i in near[1] else FAR for i in range(first_out, len(outs))],
        scratch_shapes=scratch_shapes,
        compiler_params=pltpu.CompilerParams(vmem_limit_bytes=vmem * 1024 * 1024),
        cost_estimate=pl.CostEstimate(flops=flops, bytes_accessed=moved, transcendentals=0),
        name=name,
    )(*scalars, *eager, *late, *after)


def gate(values, after):
    values, after = list(values), list(after)
    return list(lax.optimization_barrier(tuple(values + after)))[: len(values)]


def swap(values, axis):
    return lax.ppermute(values, axis, [(0, 1), (1, 0)])


def added(values, others):
    return (values.astype(F32) + others.astype(F32)).astype(BF)


def shards(values, ranks):
    return values.reshape(ranks, values.shape[0] // ranks, values.shape[1])


def spread_sum(pieces):
    mine = jnp.sum(pieces.astype(F32), axis=0).astype(BF)
    return jnp.broadcast_to(mine[None], pieces.shape)


def across(values, axes, size, mask):
    return lax.ppermute(values, axes, [(i, i ^ mask) for i in range(size)])


def deal(parts):
    return [parts[0]] + [across(parts[d], ("row", "col"), 4, d) for d in (1, 2, 3)]


RANKS = ("dp", "row")


def stages(ranks):
    bits = ranks.bit_length() - 1
    return [(bit, min(2, bits - bit)) for bit in range(0, bits, 2)]


def scatter_send(values, ranks, stage):
    bit, count = stage
    size = 1 << count
    me = (lax.axis_index(RANKS) >> bit) & (size - 1)
    cut = values.reshape(size, values.shape[0] // size, values.shape[1])
    return [lax.dynamic_index_in_dim(cut, me ^ d, 0, keepdims=False) for d in range(size)]


def scatter_move(parts, ranks, stage):
    return [parts[0]] + [
        across(parts[d], RANKS, ranks, d << stage[0]) for d in range(1, len(parts))
    ]


def scatter_sum(parts):
    return sum(part.astype(F32) for part in parts).astype(BF)


def gather(values, ranks, stage):
    return jnp.stack(
        [values]
        + [across(values, RANKS, ranks, d << stage[0]) for d in range(1, 1 << stage[1])]
    )


def rank_order(rank, ranks):
    order = 0
    for bit, count in stages(ranks):
        order = order * (1 << count) + ((rank >> bit) & ((1 << count) - 1))
    return order


def local(
    groups,
    images,
    cotangent,
    mix_partner,
    cut_partner,
    ratios,
    corners,
    drop_masks,
    norm_gains,
    norm_shifts,
    entry_weight,
    entry_bias,
    position_kernel,
    position_bias,
    exit_weight,
    exit_bias,
    expand_weight,
    expand_bias,
    shrink_weight,
    shrink_bias,
):
    images_here = images.shape[0]
    width = images.shape[3]
    units = expand_weight.shape[2]
    row, col = lax.axis_index("row"), lax.axis_index("col")
    share = images_here // 4
    rows = 4 * share * PAD
    ranks = 2 * groups
    capacity = (2 * images_here + groups - 1) // groups
    slots = groups * capacity
    order = rank_order(lax.axis_index(RANKS), ranks)
    place = jnp.stack(
        [
            lax.axis_index("dp"),
            row,
            col,
            2 * row + col,
            order,
            order // (ranks // 4),
            order % (ranks // 4),
        ]
    ).astype(jnp.int32)
    spots = [0] * ranks
    for rank in range(ranks):
        spots[rank_order(rank, ranks)] = rank
    quad = ((share, TILE, 8, width), BF)
    corners = corners.T
    masks = drop_masks.T
    flat = ((width // 128, images_here * PAD, 128), F32)
    index, take, outgoing, own = run(
        pick_kernel,
        [place, mix_partner, cut_partner],
        [images.transpose(1, 2, 0, 3)],
        [((slots, TILE, 8, width), BF), ((images_here, TILE, 8, width), BF)],
        [flat, (pltpu.SMEM((groups,), jnp.int32), None)],
        name="pick",
        vmem=60,
        scalar_outs=(((slots + 8,), jnp.int32), ((2 * images_here,), jnp.int32)),
    )
    arrived = lax.all_to_all(outgoing, "dp", split_axis=0, concat_axis=0, tiled=True)
    cot = deal(
        run(deal_kernel, [place], [cotangent.transpose(1, 2, 0, 3)], [quad] * 4, [flat], name="deal", vmem=60)
    )
    mixed = deal(
        run(
            mix_kernel,
            [place, take, corners, ratios],
            [arrived, own],
            [quad] * 4,
            name="mix",
            after=cot,
        )
    )
    conv_k = position_kernel.transpose(1, 2, 0, 3)
    tall = (rows, width)
    (
        vec1,
        keep1,
        away1,
        act_a,
        act_b,
        act_c,
        act_d,
        active0,
        slope0,
        win0,
        chance0,
        stripe0,
        mid0,
        win1,
        chance1,
        stripe1,
        hidden1,
        grad1,
    ) = run(
        functools.partial(first_kernel, spots),
        [place, masks],
        [
            *mixed,
            norm_gains,
            norm_shifts,
            entry_bias,
            conv_k,
            position_bias,
            exit_bias,
            expand_bias,
            shrink_bias,
            *cot,
            entry_weight,
            exit_weight,
            expand_weight,
            shrink_weight,
        ],
        [
            ((7, 8, width), F32),
            ((units, width), BF),
            ((units, width), BF),
            *([quad] * 4),
            ((rows, units), BF),
            ((rows, units), BF),
            ((4 * share, WIN, 3 * HALF), BF),
            ((4 * share, WIN, LANES), BF),
            (tall, BF),
            (tall, F32),
            ((4 * share, WIN, 3 * HALF), BF),
            ((4 * share, WIN, LANES), BF),
            (tall, BF),
            (tall, F32),
            (tall, F32),
        ],
        [
            (tall, F32),
            ((rows, 3 * width), F32),
            (tall, F32),
            ((rows, units), BF),
            ((rows, units), BF),
            (tall, BF),
            (tall, BF),
        ],
        flops=10 * rows * width * width * 120,
        name="first",
        vmem=46,
        near=((), (1, 2)),
        lazy=(17, 3),
    )
    sent1 = shards(added(keep1, swap(away1, "col")), ranks)
    pieces1 = lax.all_to_all(sent1, RANKS, split_axis=0, concat_axis=0, tiled=True)
    vec2, conv2, keep2, away2, grad0, delta0 = run(
        second_kernel,
        [place, masks],
        [
            norm_gains,
            norm_shifts,
            conv_k,
            grad1,
            exit_weight,
            win1,
            chance1,
            hidden1,
            entry_weight,
            stripe1,
            mid0,
            shrink_weight,
            slope0,
            expand_weight,
            active0,
            stripe0,
        ],
        [
            ((15, 8, width), F32),
            ((9, 8, width), F32),
            ((13 * width // 2, width), BF),
            ((13 * width // 2, width), BF),
            (tall, F32),
            (tall, F32),
        ],
        [
            (tall, F32),
            (tall, BF),
            ((rows, 3 * width), F32),
            ((rows, 3 * width), BF),
            (tall, BF),
            (tall, BF),
            ((rows, units), BF),
        ],
        flops=6 * rows * width * width * 120,
        name="second",
        vmem=42,
        near=((), (2, 3)),
        after=[sent1],
        lazy=(3, 4),
    )
    act = deal([act_a, act_b, act_c, act_d])
    keep2, away2, *act = gate([keep2, away2, *act], [pieces1])
    steps = stages(ranks)

    def first_parts(keep, away):
        other = swap(away, "col")
        count = keep.shape[0] // 4
        return [
            added(keep[d * count : (d + 1) * count], other[d * count : (d + 1) * count])
            for d in range(4)
        ]

    parts2 = first_parts(keep2, away2)
    moved2 = scatter_move(parts2, ranks, steps[0])
    *out_tiles, keep3, away3 = run(
        third_kernel,
        [place],
        [
            norm_gains,
            norm_shifts,
            conv_k,
            vec1,
            vec2,
            conv2,
            *mixed,
            delta0,
            win0,
            chance0,
            entry_weight,
            grad0,
        ],
        [quad] * 4 + [((2 * width, width), BF), ((2 * width, width), BF)],
        [
            (tall, F32),
            ((rows, 3 * width), F32),
            ((rows, 3 * width), BF),
            (tall, BF),
            ((4, 8, width), F32),
            ((9, 8, width), F32),
            ((width, width), F32),
        ],
        flops=3 * rows * width * width * 120,
        name="third",
        vmem=36,
        near=((), range(6)),
        after=parts2,
        lazy=(10, 6),
    )
    *moved2, keep3, away3 = gate([*moved2, keep3, away3], out_tiles)
    gradient = deal(out_tiles)
    (parted,) = run(
        split_kernel,
        [place, take, corners, ratios],
        gradient,
        [((slots, TILE, 8, width), BF)],
        name="split",
    )
    mine1 = jnp.sum(pieces1.astype(F32), axis=0).astype(BF)
    mine2 = scatter_sum(moved2)
    moved3 = scatter_move(first_parts(keep3, away3), ranks, steps[0])
    mine3 = scatter_sum(gate(moved3, [mine1]))
    cut = mine2.shape[0] * 4 // ranks
    lot = mine3.shape[0] * 4 // ranks
    joint = jnp.concatenate(
        [
            mine3.reshape(ranks // 4, lot, width),
            mine2.reshape(ranks // 4, cut, width),
        ],
        axis=1,
    ).reshape(-1, width)
    for step in steps[1:]:
        joint = scatter_sum(scatter_move(scatter_send(joint, ranks, step), ranks, step))
    joint = jnp.concatenate([mine1, joint], axis=0)
    counts = (mine1.shape[0], lot, cut)
    for step in reversed(steps[1:]):
        joint = gather(joint, ranks, step).reshape(-1, width)
    joint = shards(joint, ranks // 4)
    (parted,) = gate([parted], [joint])
    (activations,) = run(
        lay_kernel, [place], [far(a) for a in act], [((TILE, TILE, images_here, width), BF)], [flat], name="lay"
    )
    back = lax.all_to_all(parted, "dp", split_axis=0, concat_axis=0, tiled=True)
    (back,) = gate([back], [activations])
    (input_gradient,) = run(
        join_kernel,
        [place, index, corners, ratios],
        [*gradient, back],
        [((TILE, TILE, images_here, width), F32)],
        [((width // 128, (images_here + 1) * PAD, 128), F32)],
        name="join",
    )
    full = [joint] + [across(joint, RANKS, ranks, d) for d in (1, 2, 3)]
    full[2:] = gate(full[2:], [input_gradient])
    full += [swap(piece, "col") for piece in full]
    shapes = [
        (2, 2, width),
        (2, 2, width),
        (2, width, 3 * width),
        (2, 2 * width),
        (3, 3, 2, width),
        (2, width),
        (2, width, width),
        (2, width),
        (2, width, units),
        (2, units),
        (2, units, width),
        (2, width),
    ]
    gains, shifts, entry, entry_b, conv, conv_b, exit_, exit_b, expand, expand_b, shrink, shrink_b = (
        pl.pallas_call(
            functools.partial(unpack_kernel, ranks, counts),
            out_shape=[jax.ShapeDtypeStruct(shape, F32) for shape in shapes],
            in_specs=[SMEM] + [VMEM] * 8,
            out_specs=[ANYWHERE] * 12,
            scratch_shapes=[
                pltpu.VMEM((width // 2, width), F32),
            ]
            + [pltpu.VMEM(shape, F32) for shape in shapes]
            + [pltpu.SemaphoreType.DMA((16,))],
            compiler_params=pltpu.CompilerParams(vmem_limit_bytes=24 * 1024 * 1024),
            name="unpack",
        )(place, *full)
    )
    return (
        activations.transpose(2, 0, 1, 3),
        input_gradient.transpose(2, 0, 1, 3),
        gains,
        shifts,
        entry,
        entry_b,
        conv.transpose(2, 0, 1, 3),
        conv_b,
        exit_,
        exit_b,
        expand,
        expand_b,
        shrink,
        shrink_b,
    )


def solution(mesh):
    tiles = P("dp", "row", "col", None)
    return jax.shard_map(
        functools.partial(local, mesh.shape["dp"]),
        mesh=mesh,
        in_specs=(tiles, tiles, P(), P(), P("dp"), P("dp", None), P("dp", None)) + (P(),) * 12,
        out_specs=(tiles, tiles) + (P(),) * 12,
        check_vma=False,
    )
```

profile of v0, /device:TPU:0, one launch (start us, length us, event | category | flops | bytes accessed | tf_op | source)
XLA Modules:
  0.0 181.4 jit_solution(1021755386242927253)
XLA Ops:
  1.3 3.9 %pick.1 = (s32[40]{0:T(128)}, s32[32]{0:T(128)}, bf16[32,7,8,256]{3,2,1,0:T(8,128)(2,1)}, bf16[16,7,8,256]{3,2,1,0:T(8,128)(2,1)}) custom-call(s32[7]{0:T(128)} %stack.46.refs_0_.place_ref, s32[128]{0:T(128)} %refs_1_.2, s32[128]{0:T(128)} %refs_2_.3, bf16[7,7,16,256]{3,2,1,0:T(8,128)(2,1)} %bitcast.47), custom_call_target="tpu_custom_call" | custom-call | bytes 401408 | tf_op jit(solution)/shard_map/pick/pallas_call | solution.py:1160
  5.3 7.4 %all-to-all-start = ((bf16[32,7,8,256]{3,2,1,0:T(8,128)(2,1)}), bf16[32,7,8,256]{3,2,1,0:T(8,128)(2,1)S(1)}, u32[]{:S(2)}, u32[]{:S(2)}) async-start(bf16[32,7,8,256]{3,2,1,0:T(8,128)(2,1)} %get-tuple-element.89), calls=%async_computation | async-start | bytes 1835008 | tf_op jit(solution)/shard_map/all_to_all | solution.py:1307
  12.8 2.7 %deal.1 = (bf16[4,7,8,256]{3,2,1,0:T(8,128)(2,1)}, bf16[4,7,8,256]{3,2,1,0:T(8,128)(2,1)}, bf16[4,7,8,256]{3,2,1,0:T(8,128)(2,1)}, bf16[4,7,8,256]{3,2,1,0:T(8,128)(2,1)}) custom-call(s32[7]{0:T(128)} %stack.46.refs_0_.place_ref, bf16[7,7,16,256]{3,2,1,0:T(8,128)(2,1)} %bitcast.48), custom_call_target="tpu_custom_call" | custom-call | bytes 401408 | tf_op jit(solution)/shard_map/deal/pallas_call | solution.py:1160
  17.3 4.3 %collective-permute-done.1.refs_8_.refs_16_ = bf16[4,7,8,256]{3,2,1,0:T(8,128)(2,1)S(1)} collective-permute-done((bf16[4,7,8,256]{3,2,1,0:T(8,128)(2,1)}, bf16[4,7,8,256]{3,2,1,0:T(8,128)(2,1)S(1)}, u32[]{:S(2)}, u32[]{:S(2)}) %collective-permute-start.1) | collective-permute-done | bytes 114720 | tf_op jit(solution)/shard_map/ppermute | solution.py:1200
  23.3 12.5 %all-to-all-done.refs_4_ = bf16[32,7,8,256]{3,2,1,0:T(8,128)(2,1)S(1)} async-done(((bf16[32,7,8,256]{3,2,1,0:T(8,128)(2,1)}), bf16[32,7,8,256]{3,2,1,0:T(8,128)(2,1)S(1)}, u32[]{:S(2)}, u32[]{:S(2)}) %all-to-all-start) | async-done | bytes 917536 | tf_op jit(solution)/shard_map/all_to_all | solution.py:1307
  39.9 4.1 %collective-permute-done.4.refs_4_.refs_9_ = bf16[4,7,8,256]{3,2,1,0:T(8,128)(2,1)S(1)} collective-permute-done((bf16[4,7,8,256]{3,2,1,0:T(8,128)(2,1)S(1)}, bf16[4,7,8,256]{3,2,1,0:T(8,128)(2,1)S(1)}, u32[]{:S(2)}, u32[]{:S(2)}) %collective-permute-start.4) | collective-permute-done | bytes 114720 | tf_op jit(solution)/shard_map/ppermute | solution.py:1200
  45.7 27.1 %first.1 = (f32[7,8,256]{2,1,0:T(8,128)}, bf16[1024,256]{1,0:T(8,128)(2,1)S(1)}, bf16[1024,256]{1,0:T(8,128)(2,1)S(1)}, bf16[4,7,8,256]{3,2,1,0:T(8,128)(2,1)}, ...) custom-call(s32[7]{0:T(128)S(1)} %copy-done.3, ...), custom_call_target="tpu_custom_call" | custom-call | flops 70464307200 | bytes 4108288 | tf_op jit(solution)/shard_map/first/pallas_call | solution.py:1160
  76.0 4.5 %all-to-all-start.1 = ((bf16[16,64,256]{2,1,0:T(8,128)(2,1)}), bf16[16,64,256]{2,1,0:T(8,128)(2,1)S(1)}, u32[]{:S(2)}, u32[]{:S(2)}) async-start(bf16[16,64,256]{2,1,0:T(8,128)(2,1)} %bitcast.12.refs_18_), calls=%async_computation.1 | async-start | bytes 1048576 | tf_op jit(solution)/shard_map/all_to_all | solution.py:1394
  80.5 17.8 %second.1 = (f32[15,8,256]{2,1,0:T(8,128)}, f32[9,8,256]{2,1,0:T(8,128)}, bf16[1664,256]{1,0:T(8,128)(2,1)S(1)}, bf16[1664,256]{1,0:T(8,128)(2,1)S(1)}, f32[896,256]{1,0:T(8,128)}, /*index=5*/f32[896,256]{1,0:T(8,128)}) custom-call(s32[7]{0:T(128)S(1)} %copy-done.3, s32[4,16]{1,0:T(4,128)S(1)} %bitcast.41, f32[2,2,256]{2,1,0:T(2,128)S(1)} %copy-done.12, ...), custom_call_target="tpu_custom_call" | custom-call | flops 42278584320 | bytes 13723648 | tf_op jit(solution)/shard_map/second/pallas_call | solution.py:1160
  98.7 2.1 %collective-permute-done.10 = bf16[1664,256]{1,0:T(8,128)(2,1)S(1)} collective-permute-done((bf16[1664,256]{1,0:T(8,128)(2,1)S(1)}, bf16[1664,256]{1,0:T(8,128)(2,1)S(1)}, u32[]{:S(2)}, u32[]{:S(2)}) %collective-permute-start.10) | collective-permute-done | bytes 852000 | tf_op jit(solution)/shard_map/ppermute | solution.py:1183
  101.1 2.0 %collective-permute-start.14 = (bf16[416,256]{1,0:T(8,128)(2,1)S(1)}, bf16[416,256]{1,0:T(8,128)(2,1)S(1)}, u32[]{:S(2)}, u32[]{:S(2)}) collective-permute-start(bf16[416,256]{1,0:T(8,128)(2,1)S(1)} %get-tuple-element.164.refs_17_), channel_id=1, source_target_pairs={{0,2},{2,0},{4,6},{6,4},{8,10},{10,8},{12,14},{14,12},{16,18},{18,... | collective-permute-start | bytes 638984 | tf_op jit(solution)/shard_map/ppermute | solution.py:1200
  104.6 10.3 %third.1 = (bf16[4,7,8,256]{3,2,1,0:T(8,128)(2,1)S(1)}, bf16[4,7,8,256]{3,2,1,0:T(8,128)(2,1)S(1)}, bf16[4,7,8,256]{3,2,1,0:T(8,128)(2,1)S(1)}, bf16[4,7,8,256]{...) custom-call(s32[7]{0:T(128)S(1)} %copy-done.3, f32[2,2,256]{2,1,0:T(2,128)S(1)} %copy-done.12, ...), custom_call_target="tpu_custom_call" | custom-call | flops 21139292160 | bytes 6572032 | tf_op jit(solution)/shard_map/third/pallas_call | solution.py:1160
  122.9 2.4 %collective-permute-done.20 = bf16[128,256]{1,0:T(8,128)(2,1)S(1)} collective-permute-done((bf16[128,256]{1,0:T(8,128)(2,1)S(1)}, bf16[128,256]{1,0:T(8,128)(2,1)S(1)}, u32[]{:S(2)}, u32[]{:S(2)}) %collective-permute-start.20) | collective-permute-done | bytes 65568 | tf_op jit(solution)/shard_map/ppermute | solution.py:1200
  126.9 2.4 %collective-permute-start.22 = (bf16[136,256]{1,0:T(8,128)(2,1)S(1)}, bf16[136,256]{1,0:T(8,128)(2,1)S(1)}, u32[]{:S(2)}, u32[]{:S(2)}) collective-permute-start(bf16[136,256]{1,0:T(8,128)(2,1)S(1)} %get-tuple-element.171), channel_id=1, source_target_pairs={{0,16},{2,18},{4,20},{6,22},{8,24},{10,26},{12,28},{14,30},{16,0},... | collective-permute-start | bytes 208904 | tf_op jit(solution)/shard_map/ppermute | solution.py:1200
  137.0 2.9 %collective-permute-start.26 = (bf16[200,256]{1,0:T(8,128)(2,1)S(1)}, bf16[200,256]{1,0:T(8,128)(2,1)S(1)}, u32[]{:S(2)}, u32[]{:S(2)}) collective-permute-start(bf16[200,256]{1,0:T(8,128)(2,1)S(1)} %get-tuple-element.174), channel_id=1, source_target_pairs={{0,24},{2,26},{4,28},{6,30},{8,16},{10,18},{12,20},{14,22},{16,8},... | collective-permute-start | bytes 307208 | tf_op jit(solution)/shard_map/ppermute | solution.py:1200
  141.8 2.4 %collective-permute-done.25 = bf16[200,256]{1,0:T(8,128)(2,1)S(1)} collective-permute-done((bf16[200,256]{1,0:T(8,128)(2,1)S(1)}, bf16[200,256]{1,0:T(8,128)(2,1)S(1)}, u32[]{:S(2)}, u32[]{:S(2)}) %collective-permute-start.25) | collective-permute-done | bytes 102432 | tf_op jit(solution)/shard_map/ppermute | solution.py:1200
  144.4 3.9 %all-to-all-start.2 = ((bf16[32,7,8,256]{3,2,1,0:T(8,128)(2,1)}), bf16[32,7,8,256]{3,2,1,0:T(8,128)(2,1)S(1)}, u32[]{:S(2)}, u32[]{:S(2)}) async-start(bf16[32,7,8,256]{3,2,1,0:T(8,128)(2,1)} %split.1), calls=%async_computation.2 | async-start | bytes 1835008 | tf_op jit(solution)/shard_map/all_to_all | solution.py:1521
  148.8 2.0 %collective-permute-start.28 = (bf16[4,200,256]{2,1,0:T(8,128)(2,1)S(1)}, bf16[4,200,256]{2,1,0:T(8,128)(2,1)S(1)}, u32[]{:S(2)}, u32[]{:S(2)}) collective-permute-start(bf16[4,200,256]{2,1,0:T(8,128)(2,1)S(1)} %pad_maximum_fusion.refs_0_), channel_id=1, source_target_pairs={{0,4},{2,6},{4,0},{6,2},{8,12},{10,14},{12,8},{14,10},{16,20},{18,... | collective-permute-start | bytes 1228808 | tf_op jit(solution)/shard_map/ppermute | solution.py:1200
  151.7 2.1 %lay.1 = bf16[7,7,16,256]{3,2,1,0:T(8,128)(2,1)} custom-call(s32[7]{0:T(128)S(1)} %copy-done.3, bf16[4,7,8,256]{3,2,1,0:T(8,128)(2,1)} %get-tuple-element.116.refs_1_, bf16[4,7,8,256]{3,2,1,0:T(8,128)(2,1)} %copy-done.21, bf16[4,7,8,256]{3,2,1,0:T(8,128)(2,1)} %copy-done.22, bf16[4,7,8,256]{3,2,1,0:T(8,128)(2,1)} %copy-done.23), custom_call_target="tpu_custom_call" | custom-call | bytes 458752 | tf_op jit(solution)/shard_map/lay/pallas_call | solution.py:1160
  153.8 6.8 %collective-permute-done.27.refs_1_ = bf16[4,200,256]{2,1,0:T(8,128)(2,1)S(1)} collective-permute-done((bf16[4,200,256]{2,1,0:T(8,128)(2,1)S(1)}, bf16[4,200,256]{2,1,0:T(8,128)(2,1)S(1)}, u32[]{:S(2)}, u32[]{:S(2)}) %collective-permute-start.27) | collective-permute-done | bytes 409632 | tf_op jit(solution)/shard_map/ppermute | solution.py:1200
  160.6 7.9 %all-to-all-done.2.refs_8_ = bf16[32,7,8,256]{3,2,1,0:T(8,128)(2,1)S(1)} async-done(((bf16[32,7,8,256]{3,2,1,0:T(8,128)(2,1)}), bf16[32,7,8,256]{3,2,1,0:T(8,128)(2,1)S(1)}, u32[]{:S(2)}, u32[]{:S(2)}) %all-to-all-start.2) | async-done | bytes 917536 | tf_op jit(solution)/shard_map/all_to_all | solution.py:1521
  168.5 2.4 %join.1 = f32[7,7,16,256]{3,2,1,0:T(8,128)} custom-call(s32[7]{0:T(128)S(1)} %copy-done.3, s32[40]{0:T(128)S(1)} %copy-done.7, s32[4,16]{1,0:T(4,128)S(1)} %bitcast.36, f32[16]{0:T(128)S(1)} %copy-done.5, bf16[4,7,8,256]{3,2,1,0:T(8,128)(2,1)S(1)} %get-tuple-element.130.refs_4_, bf16[4,7,8,256]{3,2,1,0:T(8,128)(2,1)S(1)} %collective-permute-done.11.refs_5_, ...), custom_call_target="tpu_custom_call" | custom-call | bytes 1376256 | tf_op jit(solution)/shard_map/join/pallas_call | solution.py:1160
  170.9 4.1 %collective-permute-done.28.refs_2_ = bf16[4,200,256]{2,1,0:T(8,128)(2,1)S(1)} collective-permute-done((bf16[4,200,256]{2,1,0:T(8,128)(2,1)S(1)}, bf16[4,200,256]{2,1,0:T(8,128)(2,1)S(1)}, u32[]{:S(2)}, u32[]{:S(2)}) %collective-permute-start.28) | collective-permute-done | bytes 409632 | tf_op jit(solution)/shard_map/ppermute | solution.py:1200
  177.4 3.9 %unpack.1 = (f32[2,2,256]{2,1,0:T(2,128)}, f32[2,2,256]{2,1,0:T(2,128)}, f32[2,256,768]{2,1,0:T(8,128)}, f32[2,512]{1,0:T(2,128)}, f32[3,3,2,256]{3,2,1,0:T(2,12...) custom-call(s32[7]{0:T(128)S(1)} %copy-done.3, ...), custom_call_target="tpu_custom_call" | custom-call | tf_op jit(solution)/shard_map/unpack/pallas_call | solution.py:1549
  (119 shorter events, 38.1 us)
Async XLA Ops:
  5.3 30.5 %all-to-all-start = ((bf16[32,7,8,256]{3,2,1,0:T(8,128)(2,1)}), bf16[32,7,8,256]{3,2,1,0:T(8,128)(2,1)S(1)}, u32[]{:S(2)}, u32[]{:S(2)}) async-start(bf16[32,7,8,256]{3,2,1,0:T(8,128)(2,1)} %get-tuple-element.89), calls=%async_computation | async-start | bytes 1835008 | tf_op jit(solution)/shard_map/all_to_all | solution.py:1307
  15.4 6.2 %collective-permute-start.1 = (bf16[4,7,8,256]{3,2,1,0:T(8,128)(2,1)}, bf16[4,7,8,256]{3,2,1,0:T(8,128)(2,1)S(1)}, u32[]{:S(2)}, u32[]{:S(2)}) collective-permute-start(bf16[4,7,8,256]{3,2,1,0:T(8,128)(2,1)} %get-tuple-element.93), channel_id=1, source_target_pairs={{0,2},{1,3},{2,0},{3,1},{4,6},{5,7},{6,4},{7,5},{8,10},{9,11},{10,... | collective-permute-start | bytes 344072 | tf_op jit(solution)/shard_map/ppermute | solution.py:1200
  16.9 6.3 %collective-permute-start.2 = (bf16[4,7,8,256]{3,2,1,0:T(8,128)(2,1)}, bf16[4,7,8,256]{3,2,1,0:T(8,128)(2,1)S(1)}, u32[]{:S(2)}, u32[]{:S(2)}) collective-permute-start(bf16[4,7,8,256]{3,2,1,0:T(8,128)(2,1)} %get-tuple-element.94), channel_id=1, source_target_pairs={{0,3},{1,2},{2,1},{3,0},{4,7},{5,6},{6,5},{7,4},{8,11},{9,10},{10,... | collective-permute-start | bytes 344072 | tf_op jit(solution)/shard_map/ppermute | solution.py:1200
  73.2 25.2 %collective-permute-start.7 = (bf16[4,7,8,256]{3,2,1,0:T(8,128)(2,1)}, bf16[4,7,8,256]{3,2,1,0:T(8,128)(2,1)S(1)}, u32[]{:S(2)}, u32[]{:S(2)}) collective-permute-start(bf16[4,7,8,256]{3,2,1,0:T(8,128)(2,1)} %get-tuple-element.113), channel_id=1, source_target_pairs={{0,1},{1,0},{2,3},{3,2},{4,5},{5,4},{6,7},{7,6},{8,9},{9,8},{10,11... | collective-permute-start | bytes 344072 | tf_op jit(solution)/shard_map/ppermute | solution.py:1200
  73.4 25.0 %collective-permute-start.8 = (bf16[4,7,8,256]{3,2,1,0:T(8,128)(2,1)}, bf16[4,7,8,256]{3,2,1,0:T(8,128)(2,1)S(1)}, u32[]{:S(2)}, u32[]{:S(2)}) collective-permute-start(bf16[4,7,8,256]{3,2,1,0:T(8,128)(2,1)} %get-tuple-element.114), channel_id=1, source_target_pairs={{0,2},{1,3},{2,0},{3,1},{4,6},{5,7},{6,4},{7,5},{8,10},{9,11},{10,... | collective-permute-start | bytes 344072 | tf_op jit(solution)/shard_map/ppermute | solution.py:1200
  74.9 23.5 %collective-permute-start.9 = (bf16[4,7,8,256]{3,2,1,0:T(8,128)(2,1)}, bf16[4,7,8,256]{3,2,1,0:T(8,128)(2,1)S(1)}, u32[]{:S(2)}, u32[]{:S(2)}) collective-permute-start(bf16[4,7,8,256]{3,2,1,0:T(8,128)(2,1)} %get-tuple-element.115), channel_id=1, source_target_pairs={{0,3},{1,2},{2,1},{3,0},{4,7},{5,6},{6,5},{7,4},{8,11},{9,10},{10,... | collective-permute-start | bytes 344072 | tf_op jit(solution)/shard_map/ppermute | solution.py:1200
  76.0 22.4 %all-to-all-start.1 = ((bf16[16,64,256]{2,1,0:T(8,128)(2,1)}), bf16[16,64,256]{2,1,0:T(8,128)(2,1)S(1)}, u32[]{:S(2)}, u32[]{:S(2)}) async-start(bf16[16,64,256]{2,1,0:T(8,128)(2,1)} %bitcast.12.refs_18_), calls=%async_computation.1 | async-start | bytes 1048576 | tf_op jit(solution)/shard_map/all_to_all | solution.py:1394
  101.1 13.9 %collective-permute-start.14 = (bf16[416,256]{1,0:T(8,128)(2,1)S(1)}, bf16[416,256]{1,0:T(8,128)(2,1)S(1)}, u32[]{:S(2)}, u32[]{:S(2)}) collective-permute-start(bf16[416,256]{1,0:T(8,128)(2,1)S(1)} %get-tuple-element.164.refs_17_), channel_id=1, source_target_pairs={{0,2},{2,0},{4,6},{6,4},{8,10},{10,8},{12,14},{14,12},{16,18},{18,... | collective-permute-start | bytes 638984 | tf_op jit(solution)/shard_map/ppermute | solution.py:1200
  103.1 11.9 %collective-permute-start.15 = (bf16[416,256]{1,0:T(8,128)(2,1)S(1)}, bf16[416,256]{1,0:T(8,128)(2,1)}, u32[]{:S(2)}, u32[]{:S(2)}) collective-permute-start(bf16[416,256]{1,0:T(8,128)(2,1)S(1)} %get-tuple-element.163.refs_18_), channel_id=1, source_target_pairs={{0,4},{2,6},{4,0},{6,2},{8,12},{10,14},{12,8},{14,10},{16,20},{18,... | collective-permute-start | bytes 638984 | tf_op jit(solution)/shard_map/ppermute | solution.py:1200
  104.5 10.5 %collective-permute-start.16 = (bf16[416,256]{1,0:T(8,128)(2,1)S(1)}, bf16[416,256]{1,0:T(8,128)(2,1)}, u32[]{:S(2)}, u32[]{:S(2)}) collective-permute-start(bf16[416,256]{1,0:T(8,128)(2,1)S(1)} %get-tuple-element.162.refs_19_), channel_id=1, source_target_pairs={{0,6},{2,4},{4,2},{6,0},{8,14},{10,12},{12,10},{14,8},{16,22},{18,... | collective-permute-start | bytes 638984 | tf_op jit(solution)/shard_map/ppermute | solution.py:1200
  126.9 6.7 %collective-permute-start.22 = (bf16[136,256]{1,0:T(8,128)(2,1)S(1)}, bf16[136,256]{1,0:T(8,128)(2,1)S(1)}, u32[]{:S(2)}, u32[]{:S(2)}) collective-permute-start(bf16[136,256]{1,0:T(8,128)(2,1)S(1)} %get-tuple-element.171), channel_id=1, source_target_pairs={{0,16},{2,18},{4,20},{6,22},{8,24},{10,26},{12,28},{14,30},{16,0},... | collective-permute-start | bytes 208904 | tf_op jit(solution)/shard_map/ppermute | solution.py:1200
  129.2 6.1 %collective-permute-start.23 = (bf16[136,256]{1,0:T(8,128)(2,1)S(1)}, bf16[136,256]{1,0:T(8,128)(2,1)S(1)}, u32[]{:S(2)}, u32[]{:S(2)}) collective-permute-start(bf16[136,256]{1,0:T(8,128)(2,1)S(1)} %get-tuple-element.172), channel_id=1, source_target_pairs={{0,24},{2,26},{4,28},{6,30},{8,16},{10,18},{12,20},{14,22},{16,8},... | collective-permute-start | bytes 208904 | tf_op jit(solution)/shard_map/ppermute | solution.py:1200
  129.8 7.2 %collective-permute-start.11 = (bf16[4,7,8,256]{3,2,1,0:T(8,128)(2,1)S(1)}, bf16[4,7,8,256]{3,2,1,0:T(8,128)(2,1)S(1)}, u32[]{:S(2)}, u32[]{:S(2)}) collective-permute-start(bf16[4,7,8,256]{3,2,1,0:T(8,128)(2,1)S(1)} %get-tuple-element.131), channel_id=1, source_target_pairs={{0,1},{1,0},{2,3},{3,2},{4,5},{5,4},{6,7},{7,6},{8,9},{9,8},{10,11... | collective-permute-start | bytes 344072 | tf_op jit(solution)/shard_map/ppermute | solution.py:1200
  129.8 10.1 %collective-permute-start.12 = (bf16[4,7,8,256]{3,2,1,0:T(8,128)(2,1)S(1)}, bf16[4,7,8,256]{3,2,1,0:T(8,128)(2,1)S(1)}, u32[]{:S(2)}, u32[]{:S(2)}) collective-permute-start(bf16[4,7,8,256]{3,2,1,0:T(8,128)(2,1)S(1)} %get-tuple-element.132), channel_id=1, source_target_pairs={{0,2},{1,3},{2,0},{3,1},{4,6},{5,7},{6,4},{7,5},{8,10},{9,11},{10,... | collective-permute-start | bytes 344072 | tf_op jit(solution)/shard_map/ppermute | solution.py:1200
  130.4 9.5 %collective-permute-start.13 = (bf16[4,7,8,256]{3,2,1,0:T(8,128)(2,1)S(1)}, bf16[4,7,8,256]{3,2,1,0:T(8,128)(2,1)S(1)}, u32[]{:S(2)}, u32[]{:S(2)}) collective-permute-start(bf16[4,7,8,256]{3,2,1,0:T(8,128)(2,1)S(1)} %get-tuple-element.133), channel_id=1, source_target_pairs={{0,3},{1,2},{2,1},{3,0},{4,7},{5,6},{6,5},{7,4},{8,11},{9,10},{10,... | collective-permute-start | bytes 344072 | tf_op jit(solution)/shard_map/ppermute | solution.py:1200
  135.4 6.4 %collective-permute-start.24 = (bf16[200,256]{1,0:T(8,128)(2,1)S(1)}, bf16[200,256]{1,0:T(8,128)(2,1)S(1)}, u32[]{:S(2)}, u32[]{:S(2)}) collective-permute-start(bf16[200,256]{1,0:T(8,128)(2,1)S(1)} %get-tuple-element.174), channel_id=1, source_target_pairs={{0,8},{2,10},{4,12},{6,14},{8,0},{10,2},{12,4},{14,6},{16,24},{18,... | collective-permute-start | bytes 307208 | tf_op jit(solution)/shard_map/ppermute | solution.py:1200
  135.5 8.8 %collective-permute-start.25 = (bf16[200,256]{1,0:T(8,128)(2,1)S(1)}, bf16[200,256]{1,0:T(8,128)(2,1)S(1)}, u32[]{:S(2)}, u32[]{:S(2)}) collective-permute-start(bf16[200,256]{1,0:T(8,128)(2,1)S(1)} %get-tuple-element.174), channel_id=1, source_target_pairs={{0,16},{2,18},{4,20},{6,22},{8,24},{10,26},{12,28},{14,30},{16,0},... | collective-permute-start | bytes 307208 | tf_op jit(solution)/shard_map/ppermute | solution.py:1200
  137.0 7.3 %collective-permute-start.26 = (bf16[200,256]{1,0:T(8,128)(2,1)S(1)}, bf16[200,256]{1,0:T(8,128)(2,1)S(1)}, u32[]{:S(2)}, u32[]{:S(2)}) collective-permute-start(bf16[200,256]{1,0:T(8,128)(2,1)S(1)} %get-tuple-element.174), channel_id=1, source_target_pairs={{0,24},{2,26},{4,28},{6,30},{8,16},{10,18},{12,20},{14,22},{16,8},... | collective-permute-start | bytes 307208 | tf_op jit(solution)/shard_map/ppermute | solution.py:1200
  144.4 24.2 %all-to-all-start.2 = ((bf16[32,7,8,256]{3,2,1,0:T(8,128)(2,1)}), bf16[32,7,8,256]{3,2,1,0:T(8,128)(2,1)S(1)}, u32[]{:S(2)}, u32[]{:S(2)}) async-start(bf16[32,7,8,256]{3,2,1,0:T(8,128)(2,1)} %split.1), calls=%async_computation.2 | async-start | bytes 1835008 | tf_op jit(solution)/shard_map/all_to_all | solution.py:1521
  148.2 12.4 %collective-permute-start.27 = (bf16[4,200,256]{2,1,0:T(8,128)(2,1)S(1)}, bf16[4,200,256]{2,1,0:T(8,128)(2,1)S(1)}, u32[]{:S(2)}, u32[]{:S(2)}) collective-permute-start(bf16[4,200,256]{2,1,0:T(8,128)(2,1)S(1)} %pad_maximum_fusion.refs_0_), channel_id=1, source_target_pairs={{0,2},{2,0},{4,6},{6,4},{8,10},{10,8},{12,14},{14,12},{16,18},{18,... | collective-permute-start | bytes 1228808 | tf_op jit(solution)/shard_map/ppermute | solution.py:1200
  148.8 26.3 %collective-permute-start.28 = (bf16[4,200,256]{2,1,0:T(8,128)(2,1)S(1)}, bf16[4,200,256]{2,1,0:T(8,128)(2,1)S(1)}, u32[]{:S(2)}, u32[]{:S(2)}) collective-permute-start(bf16[4,200,256]{2,1,0:T(8,128)(2,1)S(1)} %pad_maximum_fusion.refs_0_), channel_id=1, source_target_pairs={{0,4},{2,6},{4,0},{6,2},{8,12},{10,14},{12,8},{14,10},{16,20},{18,... | collective-permute-start | bytes 1228808 | tf_op jit(solution)/shard_map/ppermute | solution.py:1200
  150.8 24.2 %collective-permute-start.29 = (bf16[4,200,256]{2,1,0:T(8,128)(2,1)S(1)}, bf16[4,200,256]{2,1,0:T(8,128)(2,1)S(1)}, u32[]{:S(2)}, u32[]{:S(2)}) collective-permute-start(bf16[4,200,256]{2,1,0:T(8,128)(2,1)S(1)} %pad_maximum_fusion.refs_0_), channel_id=1, source_target_pairs={{0,6},{2,4},{4,2},{6,0},{8,14},{10,12},{12,10},{14,8},{16,22},{18,... | collective-permute-start | bytes 1228808 | tf_op jit(solution)/shard_map/ppermute | solution.py:1200
  153.8 21.7 %collective-permute-start.30 = (bf16[4,200,256]{2,1,0:T(8,128)(2,1)S(1)}, bf16[4,200,256]{2,1,0:T(8,128)(2,1)S(1)}, u32[]{:S(2)}, u32[]{:S(2)}) collective-permute-start(bf16[4,200,256]{2,1,0:T(8,128)(2,1)S(1)} %pad_maximum_fusion.refs_0_), channel_id=1, source_target_pairs={{0,1},{1,0},{2,3},{3,2},{4,5},{5,4},{6,7},{7,6},{8,9},{9,8},{10,11... | collective-permute-start | bytes 1228808 | tf_op jit(solution)/shard_map/ppermute | solution.py:1183
  160.6 14.9 %collective-permute-start.31 = (bf16[4,200,256]{2,1,0:T(8,128)(2,1)S(1)}, bf16[4,200,256]{2,1,0:T(8,128)(2,1)}, u32[]{:S(2)}, u32[]{:S(2)}) collective-permute-start(bf16[4,200,256]{2,1,0:T(8,128)(2,1)S(1)} %collective-permute-done.27.refs_1_), channel_id=1, source_target_pairs={{0,1},{1,0},{2,3},{3,2},{4,5},{5,4},{6,7},{7,6},{8,9},{9,8},{10,11... | collective-permute-start | bytes 1228808 | tf_op jit(solution)/shard_map/ppermute | solution.py:1183
  (37 other events, 706.0 us)
where the time goes:
time: 182 us; the launch traced here: 181 us
  Pallas kernels  73.3 us (40%)
  waiting for transfers between devices  58.5 us (32%)
  starting transfers between devices  44.1 us (24%)
  other arithmetic  2.62 us (1%)
    pallas_call x9, Pallas kernels, run(): pl.pallas_call(body, out_shape=out_shape, in_specs=[SMEM] * len(scalars)...  69.4 us
    ppermute x27, waiting for transfers between devices, across(): return lax.ppermute(values, axes, [(i, i ^ mask) for i in range(size)])  32.7 us
    ppermute x27, starting transfers between devices, across(): return lax.ppermute(values, axes, [(i, i ^ mask) for i in range(size)])  27 us
    all_to_all x1, waiting for transfers between devices, local(): lax.all_to_all(outgoing, 'dp', split_axis=0, concat_axis=0, tiled=True)  12.5 us
    all_to_all x1, waiting for transfers between devices, local(): back = lax.all_to_all(parted, 'dp', split_axis=0, concat_axis=0, tiled=True)  7.89 us
    all_to_all x1, starting transfers between devices, local(): lax.all_to_all(outgoing, 'dp', split_axis=0, concat_axis=0, tiled=True)  7.42 us
    ppermute x7, waiting for transfers between devices, swap(): return lax.ppermute(values, axis, [(0, 1), (1, 0)])  5.38 us
    all_to_all x1, starting transfers between devices, local(): lax.all_to_all(sent1, RANKS, split_axis=0, concat_axis=0, tiled=True)  4.53 us
  transfers between devices with their start and end apart: 37, of which 17 were waited for; matrix products, arithmetic and copies ran while one was open for 1% of the time, Pallas kernels for 21%

commit v1 on v0

--- a/solution.py
+++ b/solution.py
@@ -715,17 +715,16 @@
 
 
 def pick_kernel(
-    place_ref, mix_ref, cut_ref, images_ref, index_out, take_out, sent_out, own_out, flat, counts
+    moves, mix_ref, cut_ref, images_ref, index_out, take_out, sent_out, own_out, flat, counts
 ):
+    moves.fetch(images_ref)
     count = images_ref.shape[2]
     slots = sent_out.shape[0]
     capacity = slots // counts.shape[0]
-    me = place_ref[0]
+    me = lax.axis_index("dp")
 
     def put(n, tile):
         own_out[n] = tile
-
-    untangle(images_ref, flat, put)
 
     @pl.loop(0, slots, unroll=8)
     def _(s):
@@ -743,10 +742,6 @@
                 index_out[jnp.where(hit, rank, slots)] = wanted - owner * count
                 rank = rank + hit.astype(jnp.int32)
 
-    @pl.loop(0, slots)
-    def _(s):
-        sent_out[s] = own_out[jnp.minimum(index_out[s], count - 1)]
-
     for part, ref in enumerate((mix_ref, cut_ref)):
 
         @pl.loop(0, count)
@@ -755,6 +750,13 @@
             rank = counts[owner]
             take_out[part * count + j] = owner * capacity + rank
             counts[owner] = rank + 1
+
+    moves.need(images_ref)
+    untangle(images_ref, flat, put)
+
+    @pl.loop(0, slots, unroll=4)
+    def _(s):
+        sent_out[s] = own_out[jnp.minimum(index_out[s], count - 1)]
 
 
 def deal_kernel(place_ref, source, out_a, out_b, out_c, out_d, flat):
@@ -1033,6 +1035,24 @@
     return pltpu.with_memory_space_constraint(values, pltpu.HBM)
 
 
+class Here:
+    def __init__(self, ranks):
+        self.ranks = ranks
+
+    def seat(self):
+        group, row, col = (lax.axis_index(axis) for axis in ("dp", "row", "col"))
+        bits = self.ranks.bit_length() - 1
+        rank = 2 * group + row
+        order = jnp.int32(0)
+        for bit in range(0, bits, 2):
+            count = min(2, bits - bit)
+            part = jnp.bitwise_and(lax.shift_right_logical(rank, bit), (1 << count) - 1)
+            order = order * (1 << count) + part
+        rest = self.ranks // 4
+        first = jnp.bitwise_and(rank, 3)
+        return (group, row, col, 2 * row + col, order, first, order - first * rest)
+
+
 class Moves:
     def __init__(self, fetched, sent):
         self.fetched, self.sent = dict(fetched), dict(sent)
@@ -1103,6 +1123,9 @@
     near=((), ()),
 ):
     outs = list(outs)
+    here = None
+    if scalars and isinstance(scalars[0], Here):
+        here, scalars = scalars[0], scalars[1:]
     first_in, first_out = (len(arrays), len(outs)) if lazy is None else lazy
     eager, late = list(arrays[:first_in]), list(arrays[first_in:])
     n_in = len(scalars) + len(eager)
@@ -1122,6 +1145,8 @@
         results, refs = refs[: len(scalar_outs) + first_out], refs[len(scalar_outs) + first_out :]
         targets, refs = refs[:n_sent], refs[n_sent:]
         own, refs = refs[:n_own], refs[n_own:]
+        if here is not None:
+            given = (here.seat(),) + tuple(given)
         if lazy is None:
             kernel(*given, *results, *own)
             return
@@ -1269,24 +1294,12 @@
     images_here = images.shape[0]
     width = images.shape[3]
     units = expand_weight.shape[2]
-    row, col = lax.axis_index("row"), lax.axis_index("col")
     share = images_here // 4
     rows = 4 * share * PAD
     ranks = 2 * groups
     capacity = (2 * images_here + groups - 1) // groups
     slots = groups * capacity
-    order = rank_order(lax.axis_index(RANKS), ranks)
-    place = jnp.stack(
-        [
-            lax.axis_index("dp"),
-            row,
-            col,
-            2 * row + col,
-            order,
-            order // (ranks // 4),
-            order % (ranks // 4),
-        ]
-    ).astype(jnp.int32)
+    place = Here(ranks)
     spots = [0] * ranks
     for rank in range(ranks):
         spots[rank_order(rank, ranks)] = rank
@@ -1296,17 +1309,19 @@
     flat = ((width // 128, images_here * PAD, 128), F32)
     index, take, outgoing, own = run(
         pick_kernel,
-        [place, mix_partner, cut_partner],
+        [mix_partner, cut_partner],
         [images.transpose(1, 2, 0, 3)],
         [((slots, TILE, 8, width), BF), ((images_here, TILE, 8, width), BF)],
         [flat, (pltpu.SMEM((groups,), jnp.int32), None)],
         name="pick",
         vmem=60,
+        lazy=(0, 2),
+        near=((), (0, 1)),
         scalar_outs=(((slots + 8,), jnp.int32), ((2 * images_here,), jnp.int32)),
     )
     arrived = lax.all_to_all(outgoing, "dp", split_axis=0, concat_axis=0, tiled=True)
     cot = deal(
-        run(deal_kernel, [place], [cotangent.transpose(1, 2, 0, 3)], [quad] * 4, [flat], name="deal", vmem=60)
+        run(deal_kernel, [place], [cotangent.transpose(1, 2, 0, 3)], [quad] * 4, [flat], name="deal")
     )
     mixed = deal(
         run(
@@ -1547,9 +1562,9 @@
     ]
     gains, shifts, entry, entry_b, conv, conv_b, exit_, exit_b, expand, expand_b, shrink, shrink_b = (
         pl.pallas_call(
-            functools.partial(unpack_kernel, ranks, counts),
+            lambda *refs: unpack_kernel(ranks, counts, place.seat(), *refs),
             out_shape=[jax.ShapeDtypeStruct(shape, F32) for shape in shapes],
-            in_specs=[SMEM] + [VMEM] * 8,
+            in_specs=[VMEM] * 8,
             out_specs=[ANYWHERE] * 12,
             scratch_shapes=[
                 pltpu.VMEM((width // 2, width), F32),
@@ -1558,7 +1573,7 @@
             + [pltpu.SemaphoreType.DMA((16,))],
             compiler_params=pltpu.CompilerParams(vmem_limit_bytes=24 * 1024 * 1024),
             name="unpack",
-        )(place, *full)
+        )(*full)
     )
     return (
         activations.transpose(2, 0, 1, 3),

time: 182 us -> 179 us (0.984)
  Pallas kernels: 73.3 us -> 69.8 us
  waiting for transfers between devices: 58.5 us -> 60.6 us
    pallas_call x9, Pallas kernels: 69.4 us -> 65.9 us  [run(): pl.pallas_call(body, out_shape=out_shape, in_specs=[SMEM] * len(scalars)...]
    all_to_all x1, waiting for transfers between devices: 12.5 us -> 14.6 us  [local(): lax.all_to_all(outgoing, 'dp', split_axis=0, concat_axis=0, tiled=True)]
  transfers between devices with their start and end apart: 37 -> 37, of which waited for: 17 -> 18; matrix products, arithmetic and copies ran while one was open for 1% -> 1% of each run, Pallas kernels for 21% -> 19%
where the time goes in v1:
time: 179 us; the launch traced here: 178 us
  Pallas kernels  69.8 us (39%)
  waiting for transfers between devices  60.6 us (34%)
  starting transfers between devices  44.1 us (25%)
  other arithmetic  2.53 us (1%)
    pallas_call x9, Pallas kernels, run(): pl.pallas_call(body, out_shape=out_shape, in_specs=[SMEM] * len(scalars)...  65.9 us
    ppermute x27, waiting for transfers between devices, across(): return lax.ppermute(values, axes, [(i, i ^ mask) for i in range(size)])  32.7 us
    ppermute x27, starting transfers between devices, across(): return lax.ppermute(values, axes, [(i, i ^ mask) for i in range(size)])  27.1 us
    all_to_all x1, waiting for transfers between devices, local(): lax.all_to_all(outgoing, 'dp', split_axis=0, concat_axis=0, tiled=True)  14.6 us
    all_to_all x1, waiting for transfers between devices, local(): back = lax.all_to_all(parted, 'dp', split_axis=0, concat_axis=0, tiled=True)  7.89 us
    all_to_all x1, starting transfers between devices, local(): lax.all_to_all(outgoing, 'dp', split_axis=0, concat_axis=0, tiled=True)  7.43 us
    ppermute x7, waiting for transfers between devices, swap(): return lax.ppermute(values, axis, [(0, 1), (1, 0)])  5.38 us
    all_to_all x1, starting transfers between devices, local(): lax.all_to_all(sent1, RANKS, split_axis=0, concat_axis=0, tiled=True)  4.54 us
  transfers between devices with their start and end apart: 37, of which 18 were waited for; matrix products, arithmetic and copies ran while one was open for 1% of the time, Pallas kernels for 19%

profile of v1, /device:TPU:0, one launch (start us, length us, event | category | flops | bytes accessed | tf_op | source)
XLA Modules:
  0.0 178.4 jit_solution(1293199397133895857)
XLA Ops:
  0.7 3.5 %pick.1 = (s32[40]{0:T(128)}, s32[32]{0:T(128)}, bf16[32,7,8,256]{3,2,1,0:T(8,128)(2,1)}, bf16[16,7,8,256]{3,2,1,0:T(8,128)(2,1)}) custom-call(s32[128]{0:T(128)} %refs_0_.2, s32[128]{0:T(128)} %refs_1_.3, bf16[7,7,16,256]{3,2,1,0:T(8,128)(2,1)} %bitcast.41), custom_call_target="tpu_custom_call" | custom-call | bytes 401408 | tf_op jit(solution)/shard_map/pick/pallas_call | solution.py:1185
  4.4 7.4 %all-to-all-start = ((bf16[32,7,8,256]{3,2,1,0:T(8,128)(2,1)}), bf16[32,7,8,256]{3,2,1,0:T(8,128)(2,1)S(1)}, u32[]{:S(2)}, u32[]{:S(2)}) async-start(bf16[32,7,8,256]{3,2,1,0:T(8,128)(2,1)} %get-tuple-element.89), calls=%async_computation | async-start | bytes 1835008 | tf_op jit(solution)/shard_map/all_to_all | solution.py:1322
  14.5 4.1 %collective-permute-done.1.refs_7_.refs_15_ = bf16[4,7,8,256]{3,2,1,0:T(8,128)(2,1)S(1)} collective-permute-done((bf16[4,7,8,256]{3,2,1,0:T(8,128)(2,1)S(1)}, bf16[4,7,8,256]{3,2,1,0:T(8,128)(2,1)S(1)}, u32[]{:S(2)}, u32[]{:S(2)}) %collective-permute-start.1) | collective-permute-done | bytes 114720 | tf_op jit(solution)/shard_map/ppermute | solution.py:1225
  20.2 14.6 %all-to-all-done.refs_3_ = bf16[32,7,8,256]{3,2,1,0:T(8,128)(2,1)S(1)} async-done(((bf16[32,7,8,256]{3,2,1,0:T(8,128)(2,1)}), bf16[32,7,8,256]{3,2,1,0:T(8,128)(2,1)S(1)}, u32[]{:S(2)}, u32[]{:S(2)}) %all-to-all-start) | async-done | bytes 917536 | tf_op jit(solution)/shard_map/all_to_all | solution.py:1322
  37.9 4.1 %collective-permute-done.4.refs_3_.refs_8_ = bf16[4,7,8,256]{3,2,1,0:T(8,128)(2,1)S(1)} collective-permute-done((bf16[4,7,8,256]{3,2,1,0:T(8,128)(2,1)S(1)}, bf16[4,7,8,256]{3,2,1,0:T(8,128)(2,1)S(1)}, u32[]{:S(2)}, u32[]{:S(2)}) %collective-permute-start.4) | collective-permute-done | bytes 114720 | tf_op jit(solution)/shard_map/ppermute | solution.py:1225
  43.7 26.9 %first.1 = (f32[7,8,256]{2,1,0:T(8,128)}, bf16[1024,256]{1,0:T(8,128)(2,1)S(1)}, bf16[1024,256]{1,0:T(8,128)(2,1)S(1)}, bf16[4,7,8,256]{3,2,1,0:T(8,128)(2,1)}, ...) custom-call(s32[4,16]{1,0:T(4,128)S(1)} %bitcast.34, ...), custom_call_target="tpu_custom_call" | custom-call | flops 70464307200 | bytes 4108288 | tf_op jit(solution)/shard_map/first/pallas_call | solution.py:1185
  73.8 4.5 %all-to-all-start.1 = ((bf16[16,64,256]{2,1,0:T(8,128)(2,1)}), bf16[16,64,256]{2,1,0:T(8,128)(2,1)S(1)}, u32[]{:S(2)}, u32[]{:S(2)}) async-start(bf16[16,64,256]{2,1,0:T(8,128)(2,1)} %bitcast.5.refs_17_), calls=%async_computation.1 | async-start | bytes 1048576 | tf_op jit(solution)/shard_map/all_to_all | solution.py:1409
  78.4 17.4 %second.1 = (f32[15,8,256]{2,1,0:T(8,128)}, f32[9,8,256]{2,1,0:T(8,128)}, bf16[1664,256]{1,0:T(8,128)(2,1)S(1)}, bf16[1664,256]{1,0:T(8,128)(2,1)S(1)}, f32[896,256]{1,0:T(8,128)}, /*index=5*/f32[896,256]{1,0:T(8,128)}) custom-call(s32[4,16]{1,0:T(4,128)S(1)} %bitcast.35, f32[2,2,256]{2,1,0:T(2,128)S(1)} %copy-done.14, f32[2,2,256]{2,1,0:T(2,128)S(1)} %copy-done.15, ...), custom_call_target="tpu_custom_call" | custom-call | flops 42278584320 | bytes 13723648 | tf_op jit(solution)/shard_map/second/pallas_call | solution.py:1185
  96.2 2.1 %collective-permute-done.10 = bf16[1664,256]{1,0:T(8,128)(2,1)S(1)} collective-permute-done((bf16[1664,256]{1,0:T(8,128)(2,1)S(1)}, bf16[1664,256]{1,0:T(8,128)(2,1)S(1)}, u32[]{:S(2)}, u32[]{:S(2)}) %collective-permute-start.10) | collective-permute-done | bytes 852000 | tf_op jit(solution)/shard_map/ppermute | solution.py:1208
  98.5 2.0 %collective-permute-start.14 = (bf16[416,256]{1,0:T(8,128)(2,1)S(1)}, bf16[416,256]{1,0:T(8,128)(2,1)S(1)}, u32[]{:S(2)}, u32[]{:S(2)}) collective-permute-start(bf16[416,256]{1,0:T(8,128)(2,1)S(1)} %get-tuple-element.164.refs_16_), channel_id=1, source_target_pairs={{0,2},{2,0},{4,6},{6,4},{8,10},{10,8},{12,14},{14,12},{16,18},{18,... | collective-permute-start | bytes 638984 | tf_op jit(solution)/shard_map/ppermute | solution.py:1225
  102.1 9.9 %third.1 = (bf16[4,7,8,256]{3,2,1,0:T(8,128)(2,1)S(1)}, bf16[4,7,8,256]{3,2,1,0:T(8,128)(2,1)S(1)}, bf16[4,7,8,256]{3,2,1,0:T(8,128)(2,1)S(1)}, bf16[4,7,8,256]{...) custom-call(f32[2,2,256]{2,1,0:T(2,128)S(1)} %copy-done.14, ...), custom_call_target="tpu_custom_call" | custom-call | flops 21139292160 | bytes 6572032 | tf_op jit(solution)/shard_map/third/pallas_call | solution.py:1185
  113.7 2.0 %collective-permute-start.18 = (bf16[128,256]{1,0:T(8,128)(2,1)S(1)}, bf16[128,256]{1,0:T(8,128)(2,1)S(1)}, u32[]{:S(2)}, u32[]{:S(2)}) collective-permute-start(bf16[128,256]{1,0:T(8,128)(2,1)S(1)} %get-tuple-element.168), channel_id=1, source_target_pairs={{0,2},{2,0},{4,6},{6,4},{8,10},{10,8},{12,14},{14,12},{16,18},{18,... | collective-permute-start | bytes 196616 | tf_op jit(solution)/shard_map/ppermute | solution.py:1225
  119.9 2.4 %collective-permute-done.20 = bf16[128,256]{1,0:T(8,128)(2,1)S(1)} collective-permute-done((bf16[128,256]{1,0:T(8,128)(2,1)S(1)}, bf16[128,256]{1,0:T(8,128)(2,1)S(1)}, u32[]{:S(2)}, u32[]{:S(2)}) %collective-permute-start.20) | collective-permute-done | bytes 65568 | tf_op jit(solution)/shard_map/ppermute | solution.py:1225
  123.9 2.4 %collective-permute-start.22 = (bf16[136,256]{1,0:T(8,128)(2,1)S(1)}, bf16[136,256]{1,0:T(8,128)(2,1)S(1)}, u32[]{:S(2)}, u32[]{:S(2)}) collective-permute-start(bf16[136,256]{1,0:T(8,128)(2,1)S(1)} %get-tuple-element.171), channel_id=1, source_target_pairs={{0,16},{2,18},{4,20},{6,22},{8,24},{10,26},{12,28},{14,30},{16,0},... | collective-permute-start | bytes 208904 | tf_op jit(solution)/shard_map/ppermute | solution.py:1225
  134.0 2.9 %collective-permute-start.26 = (bf16[200,256]{1,0:T(8,128)(2,1)S(1)}, bf16[200,256]{1,0:T(8,128)(2,1)S(1)}, u32[]{:S(2)}, u32[]{:S(2)}) collective-permute-start(bf16[200,256]{1,0:T(8,128)(2,1)S(1)} %get-tuple-element.174), channel_id=1, source_target_pairs={{0,24},{2,26},{4,28},{6,30},{8,16},{10,18},{12,20},{14,22},{16,8},... | collective-permute-start | bytes 307208 | tf_op jit(solution)/shard_map/ppermute | solution.py:1225
  138.8 2.5 %collective-permute-done.25 = bf16[200,256]{1,0:T(8,128)(2,1)S(1)} collective-permute-done((bf16[200,256]{1,0:T(8,128)(2,1)S(1)}, bf16[200,256]{1,0:T(8,128)(2,1)S(1)}, u32[]{:S(2)}, u32[]{:S(2)}) %collective-permute-start.25) | collective-permute-done | bytes 102432 | tf_op jit(solution)/shard_map/ppermute | solution.py:1225
  141.4 3.8 %all-to-all-start.2 = ((bf16[32,7,8,256]{3,2,1,0:T(8,128)(2,1)}), bf16[32,7,8,256]{3,2,1,0:T(8,128)(2,1)S(1)}, u32[]{:S(2)}, u32[]{:S(2)}) async-start(bf16[32,7,8,256]{3,2,1,0:T(8,128)(2,1)} %split.1), calls=%async_computation.2 | async-start | bytes 1835008 | tf_op jit(solution)/shard_map/all_to_all | solution.py:1536
  145.8 2.0 %collective-permute-start.28 = (bf16[4,200,256]{2,1,0:T(8,128)(2,1)S(1)}, bf16[4,200,256]{2,1,0:T(8,128)(2,1)S(1)}, u32[]{:S(2)}, u32[]{:S(2)}) collective-permute-start(bf16[4,200,256]{2,1,0:T(8,128)(2,1)S(1)} %pad_maximum_fusion.refs_0_), channel_id=1, source_target_pairs={{0,4},{2,6},{4,0},{6,2},{8,12},{10,14},{12,8},{14,10},{16,20},{18,... | collective-permute-start | bytes 1228808 | tf_op jit(solution)/shard_map/ppermute | solution.py:1225
  148.7 2.1 %lay.1 = bf16[7,7,16,256]{3,2,1,0:T(8,128)(2,1)} custom-call(bf16[4,7,8,256]{3,2,1,0:T(8,128)(2,1)} %get-tuple-element.116.refs_0_, bf16[4,7,8,256]{3,2,1,0:T(8,128)(2,1)} %collective-permute-done.7.refs_1_, bf16[4,7,8,256]{3,2,1,0:T(8,128)(2,1)} %collective-permute-done.8.refs_2_, bf16[4,7,8,256]{3,2,1,0:T(8,128)(2,1)} %collective-permute-done.9.refs_3_), custom_call_target="tpu_custom_call" | custom-call | bytes 458752 | tf_op jit(solution)/shard_map/lay/pallas_call | solution.py:1185
  150.8 6.9 %collective-permute-done.27.refs_1_ = bf16[4,200,256]{2,1,0:T(8,128)(2,1)S(1)} collective-permute-done((bf16[4,200,256]{2,1,0:T(8,128)(2,1)S(1)}, bf16[4,200,256]{2,1,0:T(8,128)(2,1)S(1)}, u32[]{:S(2)}, u32[]{:S(2)}) %collective-permute-start.27) | collective-permute-done | bytes 409632 | tf_op jit(solution)/shard_map/ppermute | solution.py:1225
  157.7 7.9 %all-to-all-done.2.refs_7_ = bf16[32,7,8,256]{3,2,1,0:T(8,128)(2,1)S(1)} async-done(((bf16[32,7,8,256]{3,2,1,0:T(8,128)(2,1)}), bf16[32,7,8,256]{3,2,1,0:T(8,128)(2,1)S(1)}, u32[]{:S(2)}, u32[]{:S(2)}) %all-to-all-start.2) | async-done | bytes 917536 | tf_op jit(solution)/shard_map/all_to_all | solution.py:1536
  165.5 2.3 %join.1 = f32[7,7,16,256]{3,2,1,0:T(8,128)} custom-call(s32[40]{0:T(128)S(1)} %copy-done.5, s32[4,16]{1,0:T(4,128)S(1)} %bitcast.30, f32[16]{0:T(128)S(1)} %copy-done.3, bf16[4,7,8,256]{3,2,1,0:T(8,128)(2,1)S(1)} %get-tuple-element.130.refs_3_, bf16[4,7,8,256]{3,2,1,0:T(8,128)(2,1)S(1)} %collective-permute-done.11.refs_4_, ...), custom_call_target="tpu_custom_call" | custom-call | bytes 1376256 | tf_op jit(solution)/shard_map/join/pallas_call | solution.py:1185
  167.9 4.2 %collective-permute-done.28.refs_2_ = bf16[4,200,256]{2,1,0:T(8,128)(2,1)S(1)} collective-permute-done((bf16[4,200,256]{2,1,0:T(8,128)(2,1)S(1)}, bf16[4,200,256]{2,1,0:T(8,128)(2,1)S(1)}, u32[]{:S(2)}, u32[]{:S(2)}) %collective-permute-start.28) | collective-permute-done | bytes 409632 | tf_op jit(solution)/shard_map/ppermute | solution.py:1225
  174.4 3.9 %unpack.1 = (f32[2,2,256]{2,1,0:T(2,128)}, f32[2,2,256]{2,1,0:T(2,128)}, f32[2,256,768]{2,1,0:T(8,128)}, f32[2,512]{1,0:T(2,128)}, f32[3,3,2,256]{3,2,1,0:T(2,12...) custom-call(bf16[4,200,256]{2,1,0:T(8,128)(2,1)S(1)} %pad_maximum_fu, ...), custom_call_target="tpu_custom_call" | custom-call | tf_op jit(solution)/shard_map/unpack/pallas_call | solution.py:1564
  (116 shorter events, 35.2 us)
Async XLA Ops:
  4.4 30.5 %all-to-all-start = ((bf16[32,7,8,256]{3,2,1,0:T(8,128)(2,1)}), bf16[32,7,8,256]{3,2,1,0:T(8,128)(2,1)S(1)}, u32[]{:S(2)}, u32[]{:S(2)}) async-start(bf16[32,7,8,256]{3,2,1,0:T(8,128)(2,1)} %get-tuple-element.89), calls=%async_computation | async-start | bytes 1835008 | tf_op jit(solution)/shard_map/all_to_all | solution.py:1322
  12.6 6.0 %collective-permute-start.1 = (bf16[4,7,8,256]{3,2,1,0:T(8,128)(2,1)S(1)}, bf16[4,7,8,256]{3,2,1,0:T(8,128)(2,1)S(1)}, u32[]{:S(2)}, u32[]{:S(2)}) collective-permute-start(bf16[4,7,8,256]{3,2,1,0:T(8,128)(2,1)S(1)} %get-tuple-element.93), channel_id=1, source_target_pairs={{0,2},{1,3},{2,0},{3,1},{4,6},{5,7},{6,4},{7,5},{8,10},{9,11},{10,... | collective-permute-start | bytes 344072 | tf_op jit(solution)/shard_map/ppermute | solution.py:1225
  36.1 6.0 %collective-permute-start.4 = (bf16[4,7,8,256]{3,2,1,0:T(8,128)(2,1)S(1)}, bf16[4,7,8,256]{3,2,1,0:T(8,128)(2,1)S(1)}, u32[]{:S(2)}, u32[]{:S(2)}) collective-permute-start(bf16[4,7,8,256]{3,2,1,0:T(8,128)(2,1)S(1)} %get-tuple-element.97), channel_id=1, source_target_pairs={{0,2},{1,3},{2,0},{3,1},{4,6},{5,7},{6,4},{7,5},{8,10},{9,11},{10,... | collective-permute-start | bytes 344072 | tf_op jit(solution)/shard_map/ppermute | solution.py:1225
  71.0 24.9 %collective-permute-start.7 = (bf16[4,7,8,256]{3,2,1,0:T(8,128)(2,1)}, bf16[4,7,8,256]{3,2,1,0:T(8,128)(2,1)}, u32[]{:S(2)}, u32[]{:S(2)}) collective-permute-start(bf16[4,7,8,256]{3,2,1,0:T(8,128)(2,1)} %get-tuple-element.113), channel_id=1, source_target_pairs={{0,1},{1,0},{2,3},{3,2},{4,5},{5,4},{6,7},{7,6},{8,9},{9,8},{10,11... | collective-permute-start | bytes 344072 | tf_op jit(solution)/shard_map/ppermute | solution.py:1225
  71.2 24.6 %collective-permute-start.8 = (bf16[4,7,8,256]{3,2,1,0:T(8,128)(2,1)}, bf16[4,7,8,256]{3,2,1,0:T(8,128)(2,1)}, u32[]{:S(2)}, u32[]{:S(2)}) collective-permute-start(bf16[4,7,8,256]{3,2,1,0:T(8,128)(2,1)} %get-tuple-element.114), channel_id=1, source_target_pairs={{0,2},{1,3},{2,0},{3,1},{4,6},{5,7},{6,4},{7,5},{8,10},{9,11},{10,... | collective-permute-start | bytes 344072 | tf_op jit(solution)/shard_map/ppermute | solution.py:1225
  72.7 23.2 %collective-permute-start.9 = (bf16[4,7,8,256]{3,2,1,0:T(8,128)(2,1)}, bf16[4,7,8,256]{3,2,1,0:T(8,128)(2,1)}, u32[]{:S(2)}, u32[]{:S(2)}) collective-permute-start(bf16[4,7,8,256]{3,2,1,0:T(8,128)(2,1)} %get-tuple-element.115), channel_id=1, source_target_pairs={{0,3},{1,2},{2,1},{3,0},{4,7},{5,6},{6,5},{7,4},{8,11},{9,10},{10,... | collective-permute-start | bytes 344072 | tf_op jit(solution)/shard_map/ppermute | solution.py:1225
  73.8 22.1 %all-to-all-start.1 = ((bf16[16,64,256]{2,1,0:T(8,128)(2,1)}), bf16[16,64,256]{2,1,0:T(8,128)(2,1)S(1)}, u32[]{:S(2)}, u32[]{:S(2)}) async-start(bf16[16,64,256]{2,1,0:T(8,128)(2,1)} %bitcast.5.refs_17_), calls=%async_computation.1 | async-start | bytes 1048576 | tf_op jit(solution)/shard_map/all_to_all | solution.py:1409
  98.5 13.5 %collective-permute-start.14 = (bf16[416,256]{1,0:T(8,128)(2,1)S(1)}, bf16[416,256]{1,0:T(8,128)(2,1)S(1)}, u32[]{:S(2)}, u32[]{:S(2)}) collective-permute-start(bf16[416,256]{1,0:T(8,128)(2,1)S(1)} %get-tuple-element.164.refs_16_), channel_id=1, source_target_pairs={{0,2},{2,0},{4,6},{6,4},{8,10},{10,8},{12,14},{14,12},{16,18},{18,... | collective-permute-start | bytes 638984 | tf_op jit(solution)/shard_map/ppermute | solution.py:1225
  100.5 11.6 %collective-permute-start.15 = (bf16[416,256]{1,0:T(8,128)(2,1)S(1)}, bf16[416,256]{1,0:T(8,128)(2,1)S(1)}, u32[]{:S(2)}, u32[]{:S(2)}) collective-permute-start(bf16[416,256]{1,0:T(8,128)(2,1)S(1)} %get-tuple-element.163.refs_17_), channel_id=1, source_target_pairs={{0,4},{2,6},{4,0},{6,2},{8,12},{10,14},{12,8},{14,10},{16,20},{18,... | collective-permute-start | bytes 638984 | tf_op jit(solution)/shard_map/ppermute | solution.py:1225
  102.0 10.1 %collective-permute-start.16 = (bf16[416,256]{1,0:T(8,128)(2,1)S(1)}, bf16[416,256]{1,0:T(8,128)(2,1)}, u32[]{:S(2)}, u32[]{:S(2)}) collective-permute-start(bf16[416,256]{1,0:T(8,128)(2,1)S(1)} %get-tuple-element.162.refs_18_), channel_id=1, source_target_pairs={{0,6},{2,4},{4,2},{6,0},{8,14},{10,12},{12,10},{14,8},{16,22},{18,... | collective-permute-start | bytes 638984 | tf_op jit(solution)/shard_map/ppermute | solution.py:1225
  123.9 6.7 %collective-permute-start.22 = (bf16[136,256]{1,0:T(8,128)(2,1)S(1)}, bf16[136,256]{1,0:T(8,128)(2,1)S(1)}, u32[]{:S(2)}, u32[]{:S(2)}) collective-permute-start(bf16[136,256]{1,0:T(8,128)(2,1)S(1)} %get-tuple-element.171), channel_id=1, source_target_pairs={{0,16},{2,18},{4,20},{6,22},{8,24},{10,26},{12,28},{14,30},{16,0},... | collective-permute-start | bytes 208904 | tf_op jit(solution)/shard_map/ppermute | solution.py:1225
  126.3 6.1 %collective-permute-start.23 = (bf16[136,256]{1,0:T(8,128)(2,1)S(1)}, bf16[136,256]{1,0:T(8,128)(2,1)S(1)}, u32[]{:S(2)}, u32[]{:S(2)}) collective-permute-start(bf16[136,256]{1,0:T(8,128)(2,1)S(1)} %get-tuple-element.172), channel_id=1, source_target_pairs={{0,24},{2,26},{4,28},{6,30},{8,16},{10,18},{12,20},{14,22},{16,8},... | collective-permute-start | bytes 208904 | tf_op jit(solution)/shard_map/ppermute | solution.py:1225
  126.8 7.2 %collective-permute-start.11 = (bf16[4,7,8,256]{3,2,1,0:T(8,128)(2,1)S(1)}, bf16[4,7,8,256]{3,2,1,0:T(8,128)(2,1)S(1)}, u32[]{:S(2)}, u32[]{:S(2)}) collective-permute-start(bf16[4,7,8,256]{3,2,1,0:T(8,128)(2,1)S(1)} %get-tuple-element.131), channel_id=1, source_target_pairs={{0,1},{1,0},{2,3},{3,2},{4,5},{5,4},{6,7},{7,6},{8,9},{9,8},{10,11... | collective-permute-start | bytes 344072 | tf_op jit(solution)/shard_map/ppermute | solution.py:1225
  126.8 10.1 %collective-permute-start.12 = (bf16[4,7,8,256]{3,2,1,0:T(8,128)(2,1)S(1)}, bf16[4,7,8,256]{3,2,1,0:T(8,128)(2,1)S(1)}, u32[]{:S(2)}, u32[]{:S(2)}) collective-permute-start(bf16[4,7,8,256]{3,2,1,0:T(8,128)(2,1)S(1)} %get-tuple-element.132), channel_id=1, source_target_pairs={{0,2},{1,3},{2,0},{3,1},{4,6},{5,7},{6,4},{7,5},{8,10},{9,11},{10,... | collective-permute-start | bytes 344072 | tf_op jit(solution)/shard_map/ppermute | solution.py:1225
  127.4 9.5 %collective-permute-start.13 = (bf16[4,7,8,256]{3,2,1,0:T(8,128)(2,1)S(1)}, bf16[4,7,8,256]{3,2,1,0:T(8,128)(2,1)S(1)}, u32[]{:S(2)}, u32[]{:S(2)}) collective-permute-start(bf16[4,7,8,256]{3,2,1,0:T(8,128)(2,1)S(1)} %get-tuple-element.133), channel_id=1, source_target_pairs={{0,3},{1,2},{2,1},{3,0},{4,7},{5,6},{6,5},{7,4},{8,11},{9,10},{10,... | collective-permute-start | bytes 344072 | tf_op jit(solution)/shard_map/ppermute | solution.py:1225
  132.5 6.4 %collective-permute-start.24 = (bf16[200,256]{1,0:T(8,128)(2,1)S(1)}, bf16[200,256]{1,0:T(8,128)(2,1)S(1)}, u32[]{:S(2)}, u32[]{:S(2)}) collective-permute-start(bf16[200,256]{1,0:T(8,128)(2,1)S(1)} %get-tuple-element.174), channel_id=1, source_target_pairs={{0,8},{2,10},{4,12},{6,14},{8,0},{10,2},{12,4},{14,6},{16,24},{18,... | collective-permute-start | bytes 307208 | tf_op jit(solution)/shard_map/ppermute | solution.py:1225
  132.5 8.8 %collective-permute-start.25 = (bf16[200,256]{1,0:T(8,128)(2,1)S(1)}, bf16[200,256]{1,0:T(8,128)(2,1)S(1)}, u32[]{:S(2)}, u32[]{:S(2)}) collective-permute-start(bf16[200,256]{1,0:T(8,128)(2,1)S(1)} %get-tuple-element.174), channel_id=1, source_target_pairs={{0,16},{2,18},{4,20},{6,22},{8,24},{10,26},{12,28},{14,30},{16,0},... | collective-permute-start | bytes 307208 | tf_op jit(solution)/shard_map/ppermute | solution.py:1225
  134.0 7.3 %collective-permute-start.26 = (bf16[200,256]{1,0:T(8,128)(2,1)S(1)}, bf16[200,256]{1,0:T(8,128)(2,1)S(1)}, u32[]{:S(2)}, u32[]{:S(2)}) collective-permute-start(bf16[200,256]{1,0:T(8,128)(2,1)S(1)} %get-tuple-element.174), channel_id=1, source_target_pairs={{0,24},{2,26},{4,28},{6,30},{8,16},{10,18},{12,20},{14,22},{16,8},... | collective-permute-start | bytes 307208 | tf_op jit(solution)/shard_map/ppermute | solution.py:1225
  141.4 24.1 %all-to-all-start.2 = ((bf16[32,7,8,256]{3,2,1,0:T(8,128)(2,1)}), bf16[32,7,8,256]{3,2,1,0:T(8,128)(2,1)S(1)}, u32[]{:S(2)}, u32[]{:S(2)}) async-start(bf16[32,7,8,256]{3,2,1,0:T(8,128)(2,1)} %split.1), calls=%async_computation.2 | async-start | bytes 1835008 | tf_op jit(solution)/shard_map/all_to_all | solution.py:1536
  145.2 12.4 %collective-permute-start.27 = (bf16[4,200,256]{2,1,0:T(8,128)(2,1)S(1)}, bf16[4,200,256]{2,1,0:T(8,128)(2,1)S(1)}, u32[]{:S(2)}, u32[]{:S(2)}) collective-permute-start(bf16[4,200,256]{2,1,0:T(8,128)(2,1)S(1)} %pad_maximum_fusion.refs_0_), channel_id=1, source_target_pairs={{0,2},{2,0},{4,6},{6,4},{8,10},{10,8},{12,14},{14,12},{16,18},{18,... | collective-permute-start | bytes 1228808 | tf_op jit(solution)/shard_map/ppermute | solution.py:1225
  145.8 26.3 %collective-permute-start.28 = (bf16[4,200,256]{2,1,0:T(8,128)(2,1)S(1)}, bf16[4,200,256]{2,1,0:T(8,128)(2,1)S(1)}, u32[]{:S(2)}, u32[]{:S(2)}) collective-permute-start(bf16[4,200,256]{2,1,0:T(8,128)(2,1)S(1)} %pad_maximum_fusion.refs_0_), channel_id=1, source_target_pairs={{0,4},{2,6},{4,0},{6,2},{8,12},{10,14},{12,8},{14,10},{16,20},{18,... | collective-permute-start | bytes 1228808 | tf_op jit(solution)/shard_map/ppermute | solution.py:1225
  147.8 24.2 %collective-permute-start.29 = (bf16[4,200,256]{2,1,0:T(8,128)(2,1)S(1)}, bf16[4,200,256]{2,1,0:T(8,128)(2,1)S(1)}, u32[]{:S(2)}, u32[]{:S(2)}) collective-permute-start(bf16[4,200,256]{2,1,0:T(8,128)(2,1)S(1)} %pad_maximum_fusion.refs_0_), channel_id=1, source_target_pairs={{0,6},{2,4},{4,2},{6,0},{8,14},{10,12},{12,10},{14,8},{16,22},{18,... | collective-permute-start | bytes 1228808 | tf_op jit(solution)/shard_map/ppermute | solution.py:1225
  150.8 21.8 %collective-permute-start.30 = (bf16[4,200,256]{2,1,0:T(8,128)(2,1)S(1)}, bf16[4,200,256]{2,1,0:T(8,128)(2,1)S(1)}, u32[]{:S(2)}, u32[]{:S(2)}) collective-permute-start(bf16[4,200,256]{2,1,0:T(8,128)(2,1)S(1)} %pad_maximum_fusion.refs_0_), channel_id=1, source_target_pairs={{0,1},{1,0},{2,3},{3,2},{4,5},{5,4},{6,7},{7,6},{8,9},{9,8},{10,11... | collective-permute-start | bytes 1228808 | tf_op jit(solution)/shard_map/ppermute | solution.py:1208
  157.6 14.9 %collective-permute-start.31 = (bf16[4,200,256]{2,1,0:T(8,128)(2,1)S(1)}, bf16[4,200,256]{2,1,0:T(8,128)(2,1)}, u32[]{:S(2)}, u32[]{:S(2)}) collective-permute-start(bf16[4,200,256]{2,1,0:T(8,128)(2,1)S(1)} %collective-permute-done.27.refs_1_), channel_id=1, source_target_pairs={{0,1},{1,0},{2,3},{3,2},{4,5},{5,4},{6,7},{7,6},{8,9},{9,8},{10,11... | collective-permute-start | bytes 1228808 | tf_op jit(solution)/shard_map/ppermute | solution.py:1208
  (36 other events, 693.4 us)

commit v2 on v1

--- a/solution.py
+++ b/solution.py
@@ -200,7 +200,7 @@
         across = direction == 0
         lane = direction * HALF
 
-        @pl.loop(0, 8, unroll=4)
+        @pl.loop(0, 8, unroll=8)
         def _(window, across=across, lane=lane, direction=direction):
             at = window_rows(across, window)
             queries = take_window(wide, at, lane)

time: 179 us -> 178 us (level)
  no operation moved by 1% of the time
where the time goes in v2:
time: 178 us; the launch traced here: 177 us
  Pallas kernels  68.5 us (38%)
  waiting for transfers between devices  60.7 us (34%)
  starting transfers between devices  44.1 us (25%)
  other arithmetic  2.53 us (1%)
    pallas_call x9, Pallas kernels, run(): pl.pallas_call(body, out_shape=out_shape, in_specs=[SMEM] * len(scalars)...  64.6 us
    ppermute x27, waiting for transfers between devices, across(): return lax.ppermute(values, axes, [(i, i ^ mask) for i in range(size)])  32.7 us
    ppermute x27, starting transfers between devices, across(): return lax.ppermute(values, axes, [(i, i ^ mask) for i in range(size)])  27.1 us
    all_to_all x1, waiting for transfers between devices, local(): lax.all_to_all(outgoing, 'dp', split_axis=0, concat_axis=0, tiled=True)  14.6 us
    all_to_all x1, waiting for transfers between devices, local(): back = lax.all_to_all(parted, 'dp', split_axis=0, concat_axis=0, tiled=True)  7.89 us
    all_to_all x1, starting transfers between devices, local(): lax.all_to_all(outgoing, 'dp', split_axis=0, concat_axis=0, tiled=True)  7.42 us
    ppermute x7, waiting for transfers between devices, swap(): return lax.ppermute(values, axis, [(0, 1), (1, 0)])  5.43 us
    all_to_all x1, starting transfers between devices, local(): lax.all_to_all(sent1, RANKS, split_axis=0, concat_axis=0, tiled=True)  4.55 us
  transfers between devices with their start and end apart: 37, of which 18 were waited for; matrix products, arithmetic and copies ran while one was open for 1% of the time, Pallas kernels for 19%

profile of v2, /device:TPU:0, one launch (start us, length us, event | category | flops | bytes accessed | tf_op | source)
XLA Modules:
  0.0 177.1 jit_solution(14753486915795714079)
XLA Ops:
  0.7 3.5 %pick.1 = (s32[40]{0:T(128)}, s32[32]{0:T(128)}, bf16[32,7,8,256]{3,2,1,0:T(8,128)(2,1)}, bf16[16,7,8,256]{3,2,1,0:T(8,128)(2,1)}) custom-call(s32[128]{0:T(128)} %refs_0_.2, s32[128]{0:T(128)} %refs_1_.3, bf16[7,7,16,256]{3,2,1,0:T(8,128)(2,1)} %bitcast.41), custom_call_target="tpu_custom_call" | custom-call | bytes 401408 | tf_op jit(solution)/shard_map/pick/pallas_call | solution.py:1185
  4.4 7.4 %all-to-all-start = ((bf16[32,7,8,256]{3,2,1,0:T(8,128)(2,1)}), bf16[32,7,8,256]{3,2,1,0:T(8,128)(2,1)S(1)}, u32[]{:S(2)}, u32[]{:S(2)}) async-start(bf16[32,7,8,256]{3,2,1,0:T(8,128)(2,1)} %get-tuple-element.89), calls=%async_computation | async-start | bytes 1835008 | tf_op jit(solution)/shard_map/all_to_all | solution.py:1322
  14.5 4.1 %collective-permute-done.1.refs_7_.refs_15_ = bf16[4,7,8,256]{3,2,1,0:T(8,128)(2,1)S(1)} collective-permute-done((bf16[4,7,8,256]{3,2,1,0:T(8,128)(2,1)S(1)}, bf16[4,7,8,256]{3,2,1,0:T(8,128)(2,1)S(1)}, u32[]{:S(2)}, u32[]{:S(2)}) %collective-permute-start.1) | collective-permute-done | bytes 114720 | tf_op jit(solution)/shard_map/ppermute | solution.py:1225
  20.2 14.6 %all-to-all-done.refs_3_ = bf16[32,7,8,256]{3,2,1,0:T(8,128)(2,1)S(1)} async-done(((bf16[32,7,8,256]{3,2,1,0:T(8,128)(2,1)}), bf16[32,7,8,256]{3,2,1,0:T(8,128)(2,1)S(1)}, u32[]{:S(2)}, u32[]{:S(2)}) %all-to-all-start) | async-done | bytes 917536 | tf_op jit(solution)/shard_map/all_to_all | solution.py:1322
  37.9 4.1 %collective-permute-done.4.refs_3_.refs_8_ = bf16[4,7,8,256]{3,2,1,0:T(8,128)(2,1)S(1)} collective-permute-done((bf16[4,7,8,256]{3,2,1,0:T(8,128)(2,1)S(1)}, bf16[4,7,8,256]{3,2,1,0:T(8,128)(2,1)S(1)}, u32[]{:S(2)}, u32[]{:S(2)}) %collective-permute-start.4) | collective-permute-done | bytes 114720 | tf_op jit(solution)/shard_map/ppermute | solution.py:1225
  43.7 25.6 %first.1 = (f32[7,8,256]{2,1,0:T(8,128)}, bf16[1024,256]{1,0:T(8,128)(2,1)S(1)}, bf16[1024,256]{1,0:T(8,128)(2,1)S(1)}, bf16[4,7,8,256]{3,2,1,0:T(8,128)(2,1)}, ...) custom-call(s32[4,16]{1,0:T(4,128)S(1)} %bitcast.34, ...), custom_call_target="tpu_custom_call" | custom-call | flops 70464307200 | bytes 4108288 | tf_op jit(solution)/shard_map/first/pallas_call | solution.py:1185
  72.5 4.5 %all-to-all-start.1 = ((bf16[16,64,256]{2,1,0:T(8,128)(2,1)}), bf16[16,64,256]{2,1,0:T(8,128)(2,1)S(1)}, u32[]{:S(2)}, u32[]{:S(2)}) async-start(bf16[16,64,256]{2,1,0:T(8,128)(2,1)} %bitcast.5.refs_17_), calls=%async_computation.1 | async-start | bytes 1048576 | tf_op jit(solution)/shard_map/all_to_all | solution.py:1409
  77.0 17.7 %second.1 = (f32[15,8,256]{2,1,0:T(8,128)}, f32[9,8,256]{2,1,0:T(8,128)}, bf16[1664,256]{1,0:T(8,128)(2,1)S(1)}, bf16[1664,256]{1,0:T(8,128)(2,1)S(1)}, f32[896,256]{1,0:T(8,128)}, /*index=5*/f32[896,256]{1,0:T(8,128)}) custom-call(s32[4,16]{1,0:T(4,128)S(1)} %bitcast.35, f32[2,2,256]{2,1,0:T(2,128)S(1)} %copy-done.14, f32[2,2,256]{2,1,0:T(2,128)S(1)} %copy-done.15, ...), custom_call_target="tpu_custom_call" | custom-call | flops 42278584320 | bytes 13723648 | tf_op jit(solution)/shard_map/second/pallas_call | solution.py:1185
  95.1 2.2 %collective-permute-done.10 = bf16[1664,256]{1,0:T(8,128)(2,1)S(1)} collective-permute-done((bf16[1664,256]{1,0:T(8,128)(2,1)S(1)}, bf16[1664,256]{1,0:T(8,128)(2,1)S(1)}, u32[]{:S(2)}, u32[]{:S(2)}) %collective-permute-start.10) | collective-permute-done | bytes 852000 | tf_op jit(solution)/shard_map/ppermute | solution.py:1208
  97.5 2.0 %collective-permute-start.14 = (bf16[416,256]{1,0:T(8,128)(2,1)S(1)}, bf16[416,256]{1,0:T(8,128)(2,1)S(1)}, u32[]{:S(2)}, u32[]{:S(2)}) collective-permute-start(bf16[416,256]{1,0:T(8,128)(2,1)S(1)} %get-tuple-element.164.refs_16_), channel_id=1, source_target_pairs={{0,2},{2,0},{4,6},{6,4},{8,10},{10,8},{12,14},{14,12},{16,18},{18,... | collective-permute-start | bytes 638984 | tf_op jit(solution)/shard_map/ppermute | solution.py:1225
  101.0 9.7 %third.1 = (bf16[4,7,8,256]{3,2,1,0:T(8,128)(2,1)S(1)}, bf16[4,7,8,256]{3,2,1,0:T(8,128)(2,1)S(1)}, bf16[4,7,8,256]{3,2,1,0:T(8,128)(2,1)S(1)}, bf16[4,7,8,256]{...) custom-call(f32[2,2,256]{2,1,0:T(2,128)S(1)} %copy-done.14, ...), custom_call_target="tpu_custom_call" | custom-call | flops 21139292160 | bytes 6572032 | tf_op jit(solution)/shard_map/third/pallas_call | solution.py:1185
  118.6 2.4 %collective-permute-done.20 = bf16[128,256]{1,0:T(8,128)(2,1)S(1)} collective-permute-done((bf16[128,256]{1,0:T(8,128)(2,1)S(1)}, bf16[128,256]{1,0:T(8,128)(2,1)S(1)}, u32[]{:S(2)}, u32[]{:S(2)}) %collective-permute-start.20) | collective-permute-done | bytes 65568 | tf_op jit(solution)/shard_map/ppermute | solution.py:1225
  122.6 2.4 %collective-permute-start.22 = (bf16[136,256]{1,0:T(8,128)(2,1)S(1)}, bf16[136,256]{1,0:T(8,128)(2,1)S(1)}, u32[]{:S(2)}, u32[]{:S(2)}) collective-permute-start(bf16[136,256]{1,0:T(8,128)(2,1)S(1)} %get-tuple-element.171), channel_id=1, source_target_pairs={{0,16},{2,18},{4,20},{6,22},{8,24},{10,26},{12,28},{14,30},{16,0},... | collective-permute-start | bytes 208904 | tf_op jit(solution)/shard_map/ppermute | solution.py:1225
  132.7 2.9 %collective-permute-start.26 = (bf16[200,256]{1,0:T(8,128)(2,1)S(1)}, bf16[200,256]{1,0:T(8,128)(2,1)S(1)}, u32[]{:S(2)}, u32[]{:S(2)}) collective-permute-start(bf16[200,256]{1,0:T(8,128)(2,1)S(1)} %get-tuple-element.174), channel_id=1, source_target_pairs={{0,24},{2,26},{4,28},{6,30},{8,16},{10,18},{12,20},{14,22},{16,8},... | collective-permute-start | bytes 307208 | tf_op jit(solution)/shard_map/ppermute | solution.py:1225
  135.6 1.9 %split.1 = bf16[32,7,8,256]{3,2,1,0:T(8,128)(2,1)} custom-call(s32[32]{0:T(128)S(1)} %copy-done.4, s32[4,16]{1,0:T(4,128)S(1)} %bitcast.29, f32[16]{0:T(128)S(1)} %copy-done.3, bf16[4,7,8,256]{3,2,1,0:T(8,128)(2,1)S(1)} %get-tuple-element.130.refs_3_, bf16[4,7,8,256]{3,2,1,0:T(8,128)(2,1)S(1)} %collective-permute-done.11.refs_4_, ...), custom_call_target="tpu_custom_call" | custom-call | bytes 458752 | tf_op jit(solution)/shard_map/split/pallas_call | solution.py:1185
  137.5 2.5 %collective-permute-done.25 = bf16[200,256]{1,0:T(8,128)(2,1)S(1)} collective-permute-done((bf16[200,256]{1,0:T(8,128)(2,1)S(1)}, bf16[200,256]{1,0:T(8,128)(2,1)S(1)}, u32[]{:S(2)}, u32[]{:S(2)}) %collective-permute-start.25) | collective-permute-done | bytes 102432 | tf_op jit(solution)/shard_map/ppermute | solution.py:1225
  140.1 3.8 %all-to-all-start.2 = ((bf16[32,7,8,256]{3,2,1,0:T(8,128)(2,1)}), bf16[32,7,8,256]{3,2,1,0:T(8,128)(2,1)S(1)}, u32[]{:S(2)}, u32[]{:S(2)}) async-start(bf16[32,7,8,256]{3,2,1,0:T(8,128)(2,1)} %split.1), calls=%async_computation.2 | async-start | bytes 1835008 | tf_op jit(solution)/shard_map/all_to_all | solution.py:1536
  144.5 2.0 %collective-permute-start.28 = (bf16[4,200,256]{2,1,0:T(8,128)(2,1)S(1)}, bf16[4,200,256]{2,1,0:T(8,128)(2,1)S(1)}, u32[]{:S(2)}, u32[]{:S(2)}) collective-permute-start(bf16[4,200,256]{2,1,0:T(8,128)(2,1)S(1)} %pad_maximum_fusion.refs_0_), channel_id=1, source_target_pairs={{0,4},{2,6},{4,0},{6,2},{8,12},{10,14},{12,8},{14,10},{16,20},{18,... | collective-permute-start | bytes 1228808 | tf_op jit(solution)/shard_map/ppermute | solution.py:1225
  147.4 2.1 %lay.1 = bf16[7,7,16,256]{3,2,1,0:T(8,128)(2,1)} custom-call(bf16[4,7,8,256]{3,2,1,0:T(8,128)(2,1)} %get-tuple-element.116.refs_0_, bf16[4,7,8,256]{3,2,1,0:T(8,128)(2,1)} %collective-permute-done.7.refs_1_, bf16[4,7,8,256]{3,2,1,0:T(8,128)(2,1)} %collective-permute-done.8.refs_2_, bf16[4,7,8,256]{3,2,1,0:T(8,128)(2,1)} %collective-permute-done.9.refs_3_), custom_call_target="tpu_custom_call" | custom-call | bytes 458752 | tf_op jit(solution)/shard_map/lay/pallas_call | solution.py:1185
  149.5 6.9 %collective-permute-done.27.refs_1_ = bf16[4,200,256]{2,1,0:T(8,128)(2,1)S(1)} collective-permute-done((bf16[4,200,256]{2,1,0:T(8,128)(2,1)S(1)}, bf16[4,200,256]{2,1,0:T(8,128)(2,1)S(1)}, u32[]{:S(2)}, u32[]{:S(2)}) %collective-permute-start.27) | collective-permute-done | bytes 409632 | tf_op jit(solution)/shard_map/ppermute | solution.py:1225
  156.3 7.9 %all-to-all-done.2.refs_7_ = bf16[32,7,8,256]{3,2,1,0:T(8,128)(2,1)S(1)} async-done(((bf16[32,7,8,256]{3,2,1,0:T(8,128)(2,1)}), bf16[32,7,8,256]{3,2,1,0:T(8,128)(2,1)S(1)}, u32[]{:S(2)}, u32[]{:S(2)}) %all-to-all-start.2) | async-done | bytes 917536 | tf_op jit(solution)/shard_map/all_to_all | solution.py:1536
  164.2 2.3 %join.1 = f32[7,7,16,256]{3,2,1,0:T(8,128)} custom-call(s32[40]{0:T(128)S(1)} %copy-done.5, s32[4,16]{1,0:T(4,128)S(1)} %bitcast.30, f32[16]{0:T(128)S(1)} %copy-done.3, bf16[4,7,8,256]{3,2,1,0:T(8,128)(2,1)S(1)} %get-tuple-element.130.refs_3_, bf16[4,7,8,256]{3,2,1,0:T(8,128)(2,1)S(1)} %collective-permute-done.11.refs_4_, ...), custom_call_target="tpu_custom_call" | custom-call | bytes 1376256 | tf_op jit(solution)/shard_map/join/pallas_call | solution.py:1185
  166.6 4.2 %collective-permute-done.28.refs_2_ = bf16[4,200,256]{2,1,0:T(8,128)(2,1)S(1)} collective-permute-done((bf16[4,200,256]{2,1,0:T(8,128)(2,1)S(1)}, bf16[4,200,256]{2,1,0:T(8,128)(2,1)S(1)}, u32[]{:S(2)}, u32[]{:S(2)}) %collective-permute-start.28) | collective-permute-done | bytes 409632 | tf_op jit(solution)/shard_map/ppermute | solution.py:1225
  173.1 3.9 %unpack.1 = (f32[2,2,256]{2,1,0:T(2,128)}, f32[2,2,256]{2,1,0:T(2,128)}, f32[2,256,768]{2,1,0:T(8,128)}, f32[2,512]{1,0:T(2,128)}, f32[3,3,2,256]{3,2,1,0:T(2,12...) custom-call(bf16[4,200,256]{2,1,0:T(8,128)(2,1)S(1)} %pad_maximum_fu, ...), custom_call_target="tpu_custom_call" | custom-call | tf_op jit(solution)/shard_map/unpack/pallas_call | solution.py:1564
  (116 shorter events, 35.3 us)
Async XLA Ops:
  4.4 30.5 %all-to-all-start = ((bf16[32,7,8,256]{3,2,1,0:T(8,128)(2,1)}), bf16[32,7,8,256]{3,2,1,0:T(8,128)(2,1)S(1)}, u32[]{:S(2)}, u32[]{:S(2)}) async-start(bf16[32,7,8,256]{3,2,1,0:T(8,128)(2,1)} %get-tuple-element.89), calls=%async_computation | async-start | bytes 1835008 | tf_op jit(solution)/shard_map/all_to_all | solution.py:1322
  12.6 6.0 %collective-permute-start.1 = (bf16[4,7,8,256]{3,2,1,0:T(8,128)(2,1)S(1)}, bf16[4,7,8,256]{3,2,1,0:T(8,128)(2,1)S(1)}, u32[]{:S(2)}, u32[]{:S(2)}) collective-permute-start(bf16[4,7,8,256]{3,2,1,0:T(8,128)(2,1)S(1)} %get-tuple-element.93), channel_id=1, source_target_pairs={{0,2},{1,3},{2,0},{3,1},{4,6},{5,7},{6,4},{7,5},{8,10},{9,11},{10,... | collective-permute-start | bytes 344072 | tf_op jit(solution)/shard_map/ppermute | solution.py:1225
  36.1 6.0 %collective-permute-start.4 = (bf16[4,7,8,256]{3,2,1,0:T(8,128)(2,1)S(1)}, bf16[4,7,8,256]{3,2,1,0:T(8,128)(2,1)S(1)}, u32[]{:S(2)}, u32[]{:S(2)}) collective-permute-start(bf16[4,7,8,256]{3,2,1,0:T(8,128)(2,1)S(1)} %get-tuple-element.97), channel_id=1, source_target_pairs={{0,2},{1,3},{2,0},{3,1},{4,6},{5,7},{6,4},{7,5},{8,10},{9,11},{10,... | collective-permute-start | bytes 344072 | tf_op jit(solution)/shard_map/ppermute | solution.py:1225
  69.7 25.1 %collective-permute-start.7 = (bf16[4,7,8,256]{3,2,1,0:T(8,128)(2,1)}, bf16[4,7,8,256]{3,2,1,0:T(8,128)(2,1)}, u32[]{:S(2)}, u32[]{:S(2)}) collective-permute-start(bf16[4,7,8,256]{3,2,1,0:T(8,128)(2,1)} %get-tuple-element.113), channel_id=1, source_target_pairs={{0,1},{1,0},{2,3},{3,2},{4,5},{5,4},{6,7},{7,6},{8,9},{9,8},{10,11... | collective-permute-start | bytes 344072 | tf_op jit(solution)/shard_map/ppermute | solution.py:1225
  69.9 24.9 %collective-permute-start.8 = (bf16[4,7,8,256]{3,2,1,0:T(8,128)(2,1)}, bf16[4,7,8,256]{3,2,1,0:T(8,128)(2,1)}, u32[]{:S(2)}, u32[]{:S(2)}) collective-permute-start(bf16[4,7,8,256]{3,2,1,0:T(8,128)(2,1)} %get-tuple-element.114), channel_id=1, source_target_pairs={{0,2},{1,3},{2,0},{3,1},{4,6},{5,7},{6,4},{7,5},{8,10},{9,11},{10,... | collective-permute-start | bytes 344072 | tf_op jit(solution)/shard_map/ppermute | solution.py:1225
  71.4 23.4 %collective-permute-start.9 = (bf16[4,7,8,256]{3,2,1,0:T(8,128)(2,1)}, bf16[4,7,8,256]{3,2,1,0:T(8,128)(2,1)}, u32[]{:S(2)}, u32[]{:S(2)}) collective-permute-start(bf16[4,7,8,256]{3,2,1,0:T(8,128)(2,1)} %get-tuple-element.115), channel_id=1, source_target_pairs={{0,3},{1,2},{2,1},{3,0},{4,7},{5,6},{6,5},{7,4},{8,11},{9,10},{10,... | collective-permute-start | bytes 344072 | tf_op jit(solution)/shard_map/ppermute | solution.py:1225
  72.5 22.3 %all-to-all-start.1 = ((bf16[16,64,256]{2,1,0:T(8,128)(2,1)}), bf16[16,64,256]{2,1,0:T(8,128)(2,1)S(1)}, u32[]{:S(2)}, u32[]{:S(2)}) async-start(bf16[16,64,256]{2,1,0:T(8,128)(2,1)} %bitcast.5.refs_17_), calls=%async_computation.1 | async-start | bytes 1048576 | tf_op jit(solution)/shard_map/all_to_all | solution.py:1409
  97.5 13.2 %collective-permute-start.14 = (bf16[416,256]{1,0:T(8,128)(2,1)S(1)}, bf16[416,256]{1,0:T(8,128)(2,1)S(1)}, u32[]{:S(2)}, u32[]{:S(2)}) collective-permute-start(bf16[416,256]{1,0:T(8,128)(2,1)S(1)} %get-tuple-element.164.refs_16_), channel_id=1, source_target_pairs={{0,2},{2,0},{4,6},{6,4},{8,10},{10,8},{12,14},{14,12},{16,18},{18,... | collective-permute-start | bytes 638984 | tf_op jit(solution)/shard_map/ppermute | solution.py:1225
  99.4 11.6 %collective-permute-start.15 = (bf16[416,256]{1,0:T(8,128)(2,1)S(1)}, bf16[416,256]{1,0:T(8,128)(2,1)S(1)}, u32[]{:S(2)}, u32[]{:S(2)}) collective-permute-start(bf16[416,256]{1,0:T(8,128)(2,1)S(1)} %get-tuple-element.163.refs_17_), channel_id=1, source_target_pairs={{0,4},{2,6},{4,0},{6,2},{8,12},{10,14},{12,8},{14,10},{16,20},{18,... | collective-permute-start | bytes 638984 | tf_op jit(solution)/shard_map/ppermute | solution.py:1225
  100.9 10.1 %collective-permute-start.16 = (bf16[416,256]{1,0:T(8,128)(2,1)S(1)}, bf16[416,256]{1,0:T(8,128)(2,1)}, u32[]{:S(2)}, u32[]{:S(2)}) collective-permute-start(bf16[416,256]{1,0:T(8,128)(2,1)S(1)} %get-tuple-element.162.refs_18_), channel_id=1, source_target_pairs={{0,6},{2,4},{4,2},{6,0},{8,14},{10,12},{12,10},{14,8},{16,22},{18,... | collective-permute-start | bytes 638984 | tf_op jit(solution)/shard_map/ppermute | solution.py:1225
  122.6 6.7 %collective-permute-start.22 = (bf16[136,256]{1,0:T(8,128)(2,1)S(1)}, bf16[136,256]{1,0:T(8,128)(2,1)S(1)}, u32[]{:S(2)}, u32[]{:S(2)}) collective-permute-start(bf16[136,256]{1,0:T(8,128)(2,1)S(1)} %get-tuple-element.171), channel_id=1, source_target_pairs={{0,16},{2,18},{4,20},{6,22},{8,24},{10,26},{12,28},{14,30},{16,0},... | collective-permute-start | bytes 208904 | tf_op jit(solution)/shard_map/ppermute | solution.py:1225
  125.0 6.1 %collective-permute-start.23 = (bf16[136,256]{1,0:T(8,128)(2,1)S(1)}, bf16[136,256]{1,0:T(8,128)(2,1)S(1)}, u32[]{:S(2)}, u32[]{:S(2)}) collective-permute-start(bf16[136,256]{1,0:T(8,128)(2,1)S(1)} %get-tuple-element.172), channel_id=1, source_target_pairs={{0,24},{2,26},{4,28},{6,30},{8,16},{10,18},{12,20},{14,22},{16,8},... | collective-permute-start | bytes 208904 | tf_op jit(solution)/shard_map/ppermute | solution.py:1225
  125.5 7.2 %collective-permute-start.11 = (bf16[4,7,8,256]{3,2,1,0:T(8,128)(2,1)S(1)}, bf16[4,7,8,256]{3,2,1,0:T(8,128)(2,1)S(1)}, u32[]{:S(2)}, u32[]{:S(2)}) collective-permute-start(bf16[4,7,8,256]{3,2,1,0:T(8,128)(2,1)S(1)} %get-tuple-element.131), channel_id=1, source_target_pairs={{0,1},{1,0},{2,3},{3,2},{4,5},{5,4},{6,7},{7,6},{8,9},{9,8},{10,11... | collective-permute-start | bytes 344072 | tf_op jit(solution)/shard_map/ppermute | solution.py:1225
  125.5 10.1 %collective-permute-start.12 = (bf16[4,7,8,256]{3,2,1,0:T(8,128)(2,1)S(1)}, bf16[4,7,8,256]{3,2,1,0:T(8,128)(2,1)S(1)}, u32[]{:S(2)}, u32[]{:S(2)}) collective-permute-start(bf16[4,7,8,256]{3,2,1,0:T(8,128)(2,1)S(1)} %get-tuple-element.132), channel_id=1, source_target_pairs={{0,2},{1,3},{2,0},{3,1},{4,6},{5,7},{6,4},{7,5},{8,10},{9,11},{10,... | collective-permute-start | bytes 344072 | tf_op jit(solution)/shard_map/ppermute | solution.py:1225
  126.1 9.5 %collective-permute-start.13 = (bf16[4,7,8,256]{3,2,1,0:T(8,128)(2,1)S(1)}, bf16[4,7,8,256]{3,2,1,0:T(8,128)(2,1)S(1)}, u32[]{:S(2)}, u32[]{:S(2)}) collective-permute-start(bf16[4,7,8,256]{3,2,1,0:T(8,128)(2,1)S(1)} %get-tuple-element.133), channel_id=1, source_target_pairs={{0,3},{1,2},{2,1},{3,0},{4,7},{5,6},{6,5},{7,4},{8,11},{9,10},{10,... | collective-permute-start | bytes 344072 | tf_op jit(solution)/shard_map/ppermute | solution.py:1225
  131.1 6.4 %collective-permute-start.24 = (bf16[200,256]{1,0:T(8,128)(2,1)S(1)}, bf16[200,256]{1,0:T(8,128)(2,1)S(1)}, u32[]{:S(2)}, u32[]{:S(2)}) collective-permute-start(bf16[200,256]{1,0:T(8,128)(2,1)S(1)} %get-tuple-element.174), channel_id=1, source_target_pairs={{0,8},{2,10},{4,12},{6,14},{8,0},{10,2},{12,4},{14,6},{16,24},{18,... | collective-permute-start | bytes 307208 | tf_op jit(solution)/shard_map/ppermute | solution.py:1225
  131.2 8.8 %collective-permute-start.25 = (bf16[200,256]{1,0:T(8,128)(2,1)S(1)}, bf16[200,256]{1,0:T(8,128)(2,1)S(1)}, u32[]{:S(2)}, u32[]{:S(2)}) collective-permute-start(bf16[200,256]{1,0:T(8,128)(2,1)S(1)} %get-tuple-element.174), channel_id=1, source_target_pairs={{0,16},{2,18},{4,20},{6,22},{8,24},{10,26},{12,28},{14,30},{16,0},... | collective-permute-start | bytes 307208 | tf_op jit(solution)/shard_map/ppermute | solution.py:1225
  132.7 7.3 %collective-permute-start.26 = (bf16[200,256]{1,0:T(8,128)(2,1)S(1)}, bf16[200,256]{1,0:T(8,128)(2,1)S(1)}, u32[]{:S(2)}, u32[]{:S(2)}) collective-permute-start(bf16[200,256]{1,0:T(8,128)(2,1)S(1)} %get-tuple-element.174), channel_id=1, source_target_pairs={{0,24},{2,26},{4,28},{6,30},{8,16},{10,18},{12,20},{14,22},{16,8},... | collective-permute-start | bytes 307208 | tf_op jit(solution)/shard_map/ppermute | solution.py:1225
  140.1 24.2 %all-to-all-start.2 = ((bf16[32,7,8,256]{3,2,1,0:T(8,128)(2,1)}), bf16[32,7,8,256]{3,2,1,0:T(8,128)(2,1)S(1)}, u32[]{:S(2)}, u32[]{:S(2)}) async-start(bf16[32,7,8,256]{3,2,1,0:T(8,128)(2,1)} %split.1), calls=%async_computation.2 | async-start | bytes 1835008 | tf_op jit(solution)/shard_map/all_to_all | solution.py:1536
  143.9 12.4 %collective-permute-start.27 = (bf16[4,200,256]{2,1,0:T(8,128)(2,1)S(1)}, bf16[4,200,256]{2,1,0:T(8,128)(2,1)S(1)}, u32[]{:S(2)}, u32[]{:S(2)}) collective-permute-start(bf16[4,200,256]{2,1,0:T(8,128)(2,1)S(1)} %pad_maximum_fusion.refs_0_), channel_id=1, source_target_pairs={{0,2},{2,0},{4,6},{6,4},{8,10},{10,8},{12,14},{14,12},{16,18},{18,... | collective-permute-start | bytes 1228808 | tf_op jit(solution)/shard_map/ppermute | solution.py:1225
  144.5 26.3 %collective-permute-start.28 = (bf16[4,200,256]{2,1,0:T(8,128)(2,1)S(1)}, bf16[4,200,256]{2,1,0:T(8,128)(2,1)S(1)}, u32[]{:S(2)}, u32[]{:S(2)}) collective-permute-start(bf16[4,200,256]{2,1,0:T(8,128)(2,1)S(1)} %pad_maximum_fusion.refs_0_), channel_id=1, source_target_pairs={{0,4},{2,6},{4,0},{6,2},{8,12},{10,14},{12,8},{14,10},{16,20},{18,... | collective-permute-start | bytes 1228808 | tf_op jit(solution)/shard_map/ppermute | solution.py:1225
  146.5 24.2 %collective-permute-start.29 = (bf16[4,200,256]{2,1,0:T(8,128)(2,1)S(1)}, bf16[4,200,256]{2,1,0:T(8,128)(2,1)S(1)}, u32[]{:S(2)}, u32[]{:S(2)}) collective-permute-start(bf16[4,200,256]{2,1,0:T(8,128)(2,1)S(1)} %pad_maximum_fusion.refs_0_), channel_id=1, source_target_pairs={{0,6},{2,4},{4,2},{6,0},{8,14},{10,12},{12,10},{14,8},{16,22},{18,... | collective-permute-start | bytes 1228808 | tf_op jit(solution)/shard_map/ppermute | solution.py:1225
  149.5 21.8 %collective-permute-start.30 = (bf16[4,200,256]{2,1,0:T(8,128)(2,1)S(1)}, bf16[4,200,256]{2,1,0:T(8,128)(2,1)S(1)}, u32[]{:S(2)}, u32[]{:S(2)}) collective-permute-start(bf16[4,200,256]{2,1,0:T(8,128)(2,1)S(1)} %pad_maximum_fusion.refs_0_), channel_id=1, source_target_pairs={{0,1},{1,0},{2,3},{3,2},{4,5},{5,4},{6,7},{7,6},{8,9},{9,8},{10,11... | collective-permute-start | bytes 1228808 | tf_op jit(solution)/shard_map/ppermute | solution.py:1208
  156.3 14.9 %collective-permute-start.31 = (bf16[4,200,256]{2,1,0:T(8,128)(2,1)S(1)}, bf16[4,200,256]{2,1,0:T(8,128)(2,1)}, u32[]{:S(2)}, u32[]{:S(2)}) collective-permute-start(bf16[4,200,256]{2,1,0:T(8,128)(2,1)S(1)} %collective-permute-done.27.refs_1_), channel_id=1, source_target_pairs={{0,1},{1,0},{2,3},{3,2},{4,5},{5,4},{6,7},{7,6},{8,9},{9,8},{10,11... | collective-permute-start | bytes 1228808 | tf_op jit(solution)/shard_map/ppermute | solution.py:1208
  (36 other events, 690.7 us)

commit v3 on v2

--- a/solution.py
+++ b/solution.py
@@ -936,6 +936,7 @@
             (vectors, None, 0, 0, middle),
             (entry_out, 0, middle, width, middle),
             (entry_out, 0, 0, 2 * width, width),
+            (None, None, 0, 0, middle),
         ],
         squares(entry_out, 1, 3)
         + tall(exit_out, 1, 1)
@@ -943,16 +944,18 @@
         + tall(shrink_out, 0, units // width)
         + tall(exit_out, 0, 1),
     )
-    inner_ranks = ranks // 4
     moves = []
     base = 0
     for plan, count in zip(plans, counts):
+        lump = sum(part[4] for part in plan) // 8
         at = 0
         for out_ref, block, first_row, lane, length in plan:
             done = 0
             while done < length:
-                step = min(length - done, count - at % count)
-                moves.append((out_ref, block, first_row + done, lane, base, count, at, step))
+                inside = at % lump
+                step = min(length - done, count - inside % count, lump - inside)
+                where = (at // lump, inside // count, base + inside % count)
+                moves.append((out_ref, block, first_row + done, lane, where, step))
                 at += step
                 done += step
         base += count
@@ -965,13 +968,10 @@
         return copy
 
     def place_parts(target, wanted, col, own):
-        for out_ref, block, first_row, lane, base, count, at, step in moves:
+        for out_ref, block, first_row, lane, (number, inner, start), step in moves:
             if out_ref is not target or block != wanted:
                 continue
-            shard, start = at // count, base + at % count
-            half, shard = shard // ranks, shard % ranks
-            first, inner = shard // inner_ranks, shard % inner_ranks
-            piece = pieces[4 * (col ^ half) + (own ^ first)]
+            piece = pieces[4 * (col ^ (number // 4)) + (own ^ (number % 4))]
             inner = jnp.bitwise_xor(place_ref[6], inner)
             values = piece[inner, start : start + step, :].astype(F32)
             place = slice(first_row, first_row + step)
@@ -1513,6 +1513,9 @@
     mine2 = scatter_sum(moved2)
     moved3 = scatter_move(first_parts(keep3, away3), ranks, steps[0])
     mine3 = scatter_sum(gate(moved3, [mine1]))
+    mine2, mine3 = (
+        jnp.pad(values, ((0, -values.shape[0] % (4 * ranks)), (0, 0))) for values in (mine2, mine3)
+    )
     cut = mine2.shape[0] * 4 // ranks
     lot = mine3.shape[0] * 4 // ranks
     joint = jnp.concatenate(

time: 178 us -> 179 us (level)
  transfers between devices with their start and end apart: 37 -> 37, of which waited for: 18 -> 19; matrix products, arithmetic and copies ran while one was open for 1% -> 1% of each run, Pallas kernels for 19% -> 19%
where the time goes in v3:
time: 179 us
  Pallas kernels  68.5 us (38%)
  waiting for transfers between devices  62.1 us (35%)
  starting transfers between devices  44.1 us (25%)
  other arithmetic  2.52 us (1%)
    pallas_call x9, Pallas kernels, run(): pl.pallas_call(body, out_shape=out_shape, in_specs=[SMEM] * len(scalars)...  64.6 us
    ppermute x27, waiting for transfers between devices, across(): return lax.ppermute(values, axes, [(i, i ^ mask) for i in range(size)])  33.8 us
    ppermute x27, starting transfers between devices, across(): return lax.ppermute(values, axes, [(i, i ^ mask) for i in range(size)])  27.1 us
    all_to_all x1, waiting for transfers between devices, local(): lax.all_to_all(outgoing, 'dp', split_axis=0, concat_axis=0, tiled=True)  14.6 us
    all_to_all x1, waiting for transfers between devices, local(): back = lax.all_to_all(parted, 'dp', split_axis=0, concat_axis=0, tiled=True)  8.19 us
    all_to_all x1, starting transfers between devices, local(): lax.all_to_all(outgoing, 'dp', split_axis=0, concat_axis=0, tiled=True)  7.42 us
    ppermute x7, waiting for transfers between devices, swap(): return lax.ppermute(values, axis, [(0, 1), (1, 0)])  5.48 us
    all_to_all x1, starting transfers between devices, local(): lax.all_to_all(sent1, RANKS, split_axis=0, concat_axis=0, tiled=True)  4.55 us
  transfers between devices with their start and end apart: 37, of which 19 were waited for; matrix products, arithmetic and copies ran while one was open for 1% of the time, Pallas kernels for 19%

profile of v3, /device:TPU:0, one launch (start us, length us, event | category | flops | bytes accessed | tf_op | source)
XLA Modules:
  0.0 178.5 jit_solution(9334130801195390781)
XLA Ops:
  0.7 3.5 %pick.1 = (s32[40]{0:T(128)}, s32[32]{0:T(128)}, bf16[32,7,8,256]{3,2,1,0:T(8,128)(2,1)}, bf16[16,7,8,256]{3,2,1,0:T(8,128)(2,1)}) custom-call(s32[128]{0:T(128)} %refs_0_.2, s32[128]{0:T(128)} %refs_1_.3, bf16[7,7,16,256]{3,2,1,0:T(8,128)(2,1)} %bitcast.41), custom_call_target="tpu_custom_call" | custom-call | bytes 401408 | tf_op jit(solution)/shard_map/pick/pallas_call | solution.py:1185
  4.4 7.4 %all-to-all-start = ((bf16[32,7,8,256]{3,2,1,0:T(8,128)(2,1)}), bf16[32,7,8,256]{3,2,1,0:T(8,128)(2,1)S(1)}, u32[]{:S(2)}, u32[]{:S(2)}) async-start(bf16[32,7,8,256]{3,2,1,0:T(8,128)(2,1)} %get-tuple-element.89), calls=%async_computation | async-start | bytes 1835008 | tf_op jit(solution)/shard_map/all_to_all | solution.py:1322
  14.5 4.1 %collective-permute-done.1.refs_7_.refs_15_ = bf16[4,7,8,256]{3,2,1,0:T(8,128)(2,1)S(1)} collective-permute-done((bf16[4,7,8,256]{3,2,1,0:T(8,128)(2,1)S(1)}, bf16[4,7,8,256]{3,2,1,0:T(8,128)(2,1)S(1)}, u32[]{:S(2)}, u32[]{:S(2)}) %collective-permute-start.1) | collective-permute-done | bytes 114720 | tf_op jit(solution)/shard_map/ppermute | solution.py:1225
  20.2 14.6 %all-to-all-done.refs_3_ = bf16[32,7,8,256]{3,2,1,0:T(8,128)(2,1)S(1)} async-done(((bf16[32,7,8,256]{3,2,1,0:T(8,128)(2,1)}), bf16[32,7,8,256]{3,2,1,0:T(8,128)(2,1)S(1)}, u32[]{:S(2)}, u32[]{:S(2)}) %all-to-all-start) | async-done | bytes 917536 | tf_op jit(solution)/shard_map/all_to_all | solution.py:1322
  37.9 4.1 %collective-permute-done.4.refs_3_.refs_8_ = bf16[4,7,8,256]{3,2,1,0:T(8,128)(2,1)S(1)} collective-permute-done((bf16[4,7,8,256]{3,2,1,0:T(8,128)(2,1)S(1)}, bf16[4,7,8,256]{3,2,1,0:T(8,128)(2,1)S(1)}, u32[]{:S(2)}, u32[]{:S(2)}) %collective-permute-start.4) | collective-permute-done | bytes 114720 | tf_op jit(solution)/shard_map/ppermute | solution.py:1225
  43.7 25.6 %first.1 = (f32[7,8,256]{2,1,0:T(8,128)}, bf16[1024,256]{1,0:T(8,128)(2,1)S(1)}, bf16[1024,256]{1,0:T(8,128)(2,1)S(1)}, bf16[4,7,8,256]{3,2,1,0:T(8,128)(2,1)}, ...) custom-call(s32[4,16]{1,0:T(4,128)S(1)} %bitcast.34, ...), custom_call_target="tpu_custom_call" | custom-call | flops 70464307200 | bytes 4108288 | tf_op jit(solution)/shard_map/first/pallas_call | solution.py:1185
  72.5 4.5 %all-to-all-start.1 = ((bf16[16,64,256]{2,1,0:T(8,128)(2,1)}), bf16[16,64,256]{2,1,0:T(8,128)(2,1)S(1)}, u32[]{:S(2)}, u32[]{:S(2)}) async-start(bf16[16,64,256]{2,1,0:T(8,128)(2,1)} %bitcast.5.refs_17_), calls=%async_computation.1 | async-start | bytes 1048576 | tf_op jit(solution)/shard_map/all_to_all | solution.py:1409
  77.0 17.7 %second.1 = (f32[15,8,256]{2,1,0:T(8,128)}, f32[9,8,256]{2,1,0:T(8,128)}, bf16[1664,256]{1,0:T(8,128)(2,1)S(1)}, bf16[1664,256]{1,0:T(8,128)(2,1)S(1)}, f32[896,256]{1,0:T(8,128)}, /*index=5*/f32[896,256]{1,0:T(8,128)}) custom-call(s32[4,16]{1,0:T(4,128)S(1)} %bitcast.35, f32[2,2,256]{2,1,0:T(2,128)S(1)} %copy-done.10, f32[2,2,256]{2,1,0:T(2,128)S(1)} %copy-done.11, ...), custom_call_target="tpu_custom_call" | custom-call | flops 42278584320 | bytes 13723648 | tf_op jit(solution)/shard_map/second/pallas_call | solution.py:1185
  95.1 2.2 %collective-permute-done.10 = bf16[1664,256]{1,0:T(8,128)(2,1)S(1)} collective-permute-done((bf16[1664,256]{1,0:T(8,128)(2,1)S(1)}, bf16[1664,256]{1,0:T(8,128)(2,1)S(1)}, u32[]{:S(2)}, u32[]{:S(2)}) %collective-permute-start.10) | collective-permute-done | bytes 852000 | tf_op jit(solution)/shard_map/ppermute | solution.py:1208
  97.4 2.0 %collective-permute-start.14 = (bf16[416,256]{1,0:T(8,128)(2,1)S(1)}, bf16[416,256]{1,0:T(8,128)(2,1)S(1)}, u32[]{:S(2)}, u32[]{:S(2)}) collective-permute-start(bf16[416,256]{1,0:T(8,128)(2,1)S(1)} %get-tuple-element.164.refs_16_), channel_id=1, source_target_pairs={{0,2},{2,0},{4,6},{6,4},{8,10},{10,8},{12,14},{14,12},{16,18},{18,... | collective-permute-start | bytes 638984 | tf_op jit(solution)/shard_map/ppermute | solution.py:1225
  101.0 9.6 %third.1 = (bf16[4,7,8,256]{3,2,1,0:T(8,128)(2,1)S(1)}, bf16[4,7,8,256]{3,2,1,0:T(8,128)(2,1)S(1)}, bf16[4,7,8,256]{3,2,1,0:T(8,128)(2,1)S(1)}, bf16[4,7,8,256]{...) custom-call(f32[2,2,256]{2,1,0:T(2,128)S(1)} %copy-done.10, ...), custom_call_target="tpu_custom_call" | custom-call | flops 21139292160 | bytes 6572032 | tf_op jit(solution)/shard_map/third/pallas_call | solution.py:1185
  118.6 2.4 %collective-permute-done.20 = bf16[128,256]{1,0:T(8,128)(2,1)S(1)} collective-permute-done((bf16[128,256]{1,0:T(8,128)(2,1)S(1)}, bf16[128,256]{1,0:T(8,128)(2,1)S(1)}, u32[]{:S(2)}, u32[]{:S(2)}) %collective-permute-start.20) | collective-permute-done | bytes 65568 | tf_op jit(solution)/shard_map/ppermute | solution.py:1225
  122.6 2.4 %collective-permute-start.22 = (bf16[144,256]{1,0:T(8,128)(2,1)S(1)}, bf16[144,256]{1,0:T(8,128)(2,1)S(1)}, u32[]{:S(2)}, u32[]{:S(2)}) collective-permute-start(bf16[144,256]{1,0:T(8,128)(2,1)S(1)} %get-tuple-element.171), channel_id=1, source_target_pairs={{0,16},{2,18},{4,20},{6,22},{8,24},{10,26},{12,28},{14,30},{16,0},... | collective-permute-start | bytes 221192 | tf_op jit(solution)/shard_map/ppermute | solution.py:1225
  127.4 2.0 %collective-permute-done.22 = bf16[144,256]{1,0:T(8,128)(2,1)S(1)} collective-permute-done((bf16[144,256]{1,0:T(8,128)(2,1)S(1)}, bf16[144,256]{1,0:T(8,128)(2,1)S(1)}, u32[]{:S(2)}, u32[]{:S(2)}) %collective-permute-start.22) | collective-permute-done | bytes 73760 | tf_op jit(solution)/shard_map/ppermute | solution.py:1225
  132.9 2.7 %collective-permute-start.26 = (bf16[208,256]{1,0:T(8,128)(2,1)S(1)}, bf16[208,256]{1,0:T(8,128)(2,1)S(1)}, u32[]{:S(2)}, u32[]{:S(2)}) collective-permute-start(bf16[208,256]{1,0:T(8,128)(2,1)S(1)} %get-tuple-element.174), channel_id=1, source_target_pairs={{0,24},{2,26},{4,28},{6,30},{8,16},{10,18},{12,20},{14,22},{16,8},... | collective-permute-start | bytes 319496 | tf_op jit(solution)/shard_map/ppermute | solution.py:1225
  137.7 2.7 %collective-permute-done.25 = bf16[208,256]{1,0:T(8,128)(2,1)S(1)} collective-permute-done((bf16[208,256]{1,0:T(8,128)(2,1)S(1)}, bf16[208,256]{1,0:T(8,128)(2,1)S(1)}, u32[]{:S(2)}, u32[]{:S(2)}) %collective-permute-start.25) | collective-permute-done | bytes 106528 | tf_op jit(solution)/shard_map/ppermute | solution.py:1225
  140.4 3.8 %all-to-all-start.2 = ((bf16[32,7,8,256]{3,2,1,0:T(8,128)(2,1)}), bf16[32,7,8,256]{3,2,1,0:T(8,128)(2,1)S(1)}, u32[]{:S(2)}, u32[]{:S(2)}) async-start(bf16[32,7,8,256]{3,2,1,0:T(8,128)(2,1)} %split.1), calls=%async_computation.2 | async-start | bytes 1835008 | tf_op jit(solution)/shard_map/all_to_all | solution.py:1539
  144.9 2.0 %collective-permute-start.28 = (bf16[4,208,256]{2,1,0:T(8,128)(2,1)S(1)}, bf16[4,208,256]{2,1,0:T(8,128)(2,1)S(1)}, u32[]{:S(2)}, u32[]{:S(2)}) collective-permute-start(bf16[4,208,256]{2,1,0:T(8,128)(2,1)S(1)} %pad_maximum_fusion.refs_0_), channel_id=1, source_target_pairs={{0,4},{2,6},{4,0},{6,2},{8,12},{10,14},{12,8},{14,10},{16,20},{18,... | collective-permute-start | bytes 1277960 | tf_op jit(solution)/shard_map/ppermute | solution.py:1225
  147.8 2.1 %lay.1 = bf16[7,7,16,256]{3,2,1,0:T(8,128)(2,1)} custom-call(bf16[4,7,8,256]{3,2,1,0:T(8,128)(2,1)} %get-tuple-element.116.refs_0_, bf16[4,7,8,256]{3,2,1,0:T(8,128)(2,1)} %copy-done.19, bf16[4,7,8,256]{3,2,1,0:T(8,128)(2,1)} %copy-done.20, bf16[4,7,8,256]{3,2,1,0:T(8,128)(2,1)} %copy-done.21), custom_call_target="tpu_custom_call" | custom-call | bytes 458752 | tf_op jit(solution)/shard_map/lay/pallas_call | solution.py:1185
  149.8 7.2 %collective-permute-done.27.refs_1_ = bf16[4,208,256]{2,1,0:T(8,128)(2,1)S(1)} collective-permute-done((bf16[4,208,256]{2,1,0:T(8,128)(2,1)S(1)}, bf16[4,208,256]{2,1,0:T(8,128)(2,1)S(1)}, u32[]{:S(2)}, u32[]{:S(2)}) %collective-permute-start.27) | collective-permute-done | bytes 426016 | tf_op jit(solution)/shard_map/ppermute | solution.py:1225
  157.0 8.2 %all-to-all-done.2.refs_7_ = bf16[32,7,8,256]{3,2,1,0:T(8,128)(2,1)S(1)} async-done(((bf16[32,7,8,256]{3,2,1,0:T(8,128)(2,1)}), bf16[32,7,8,256]{3,2,1,0:T(8,128)(2,1)S(1)}, u32[]{:S(2)}, u32[]{:S(2)}) %all-to-all-start.2) | async-done | bytes 917536 | tf_op jit(solution)/shard_map/all_to_all | solution.py:1539
  165.2 2.3 %join.1 = f32[7,7,16,256]{3,2,1,0:T(8,128)} custom-call(s32[40]{0:T(128)S(1)} %copy-done.5, s32[4,16]{1,0:T(4,128)S(1)} %bitcast.30, f32[16]{0:T(128)S(1)} %copy-done.3, bf16[4,7,8,256]{3,2,1,0:T(8,128)(2,1)S(1)} %get-tuple-element.130.refs_3_, bf16[4,7,8,256]{3,2,1,0:T(8,128)(2,1)S(1)} %collective-permute-done.11.refs_4_, ...), custom_call_target="tpu_custom_call" | custom-call | bytes 1376256 | tf_op jit(solution)/shard_map/join/pallas_call | solution.py:1185
  167.6 4.5 %collective-permute-done.28.refs_2_ = bf16[4,208,256]{2,1,0:T(8,128)(2,1)S(1)} collective-permute-done((bf16[4,208,256]{2,1,0:T(8,128)(2,1)S(1)}, bf16[4,208,256]{2,1,0:T(8,128)(2,1)S(1)}, u32[]{:S(2)}, u32[]{:S(2)}) %collective-permute-start.28) | collective-permute-done | bytes 426016 | tf_op jit(solution)/shard_map/ppermute | solution.py:1225
  174.5 3.9 %unpack.1 = (f32[2,2,256]{2,1,0:T(2,128)}, f32[2,2,256]{2,1,0:T(2,128)}, f32[2,256,768]{2,1,0:T(8,128)}, f32[2,512]{1,0:T(2,128)}, f32[3,3,2,256]{3,2,1,0:T(2,12...) custom-call(bf16[4,208,256]{2,1,0:T(8,128)(2,1)S(1)} %pad_maximum_fu, ...), custom_call_target="tpu_custom_call" | custom-call | tf_op jit(solution)/shard_map/unpack/pallas_call | solution.py:1567
  (115 shorter events, 35.6 us)
Async XLA Ops:
  4.4 30.5 %all-to-all-start = ((bf16[32,7,8,256]{3,2,1,0:T(8,128)(2,1)}), bf16[32,7,8,256]{3,2,1,0:T(8,128)(2,1)S(1)}, u32[]{:S(2)}, u32[]{:S(2)}) async-start(bf16[32,7,8,256]{3,2,1,0:T(8,128)(2,1)} %get-tuple-element.89), calls=%async_computation | async-start | bytes 1835008 | tf_op jit(solution)/shard_map/all_to_all | solution.py:1322
  12.6 6.0 %collective-permute-start.1 = (bf16[4,7,8,256]{3,2,1,0:T(8,128)(2,1)S(1)}, bf16[4,7,8,256]{3,2,1,0:T(8,128)(2,1)S(1)}, u32[]{:S(2)}, u32[]{:S(2)}) collective-permute-start(bf16[4,7,8,256]{3,2,1,0:T(8,128)(2,1)S(1)} %get-tuple-element.93), channel_id=1, source_target_pairs={{0,2},{1,3},{2,0},{3,1},{4,6},{5,7},{6,4},{7,5},{8,10},{9,11},{10,... | collective-permute-start | bytes 344072 | tf_op jit(solution)/shard_map/ppermute | solution.py:1225
  36.1 6.0 %collective-permute-start.4 = (bf16[4,7,8,256]{3,2,1,0:T(8,128)(2,1)S(1)}, bf16[4,7,8,256]{3,2,1,0:T(8,128)(2,1)S(1)}, u32[]{:S(2)}, u32[]{:S(2)}) collective-permute-start(bf16[4,7,8,256]{3,2,1,0:T(8,128)(2,1)S(1)} %get-tuple-element.97), channel_id=1, source_target_pairs={{0,2},{1,3},{2,0},{3,1},{4,6},{5,7},{6,4},{7,5},{8,10},{9,11},{10,... | collective-permute-start | bytes 344072 | tf_op jit(solution)/shard_map/ppermute | solution.py:1225
  69.6 25.1 %collective-permute-start.7 = (bf16[4,7,8,256]{3,2,1,0:T(8,128)(2,1)}, bf16[4,7,8,256]{3,2,1,0:T(8,128)(2,1)S(1)}, u32[]{:S(2)}, u32[]{:S(2)}) collective-permute-start(bf16[4,7,8,256]{3,2,1,0:T(8,128)(2,1)} %get-tuple-element.113), channel_id=1, source_target_pairs={{0,1},{1,0},{2,3},{3,2},{4,5},{5,4},{6,7},{7,6},{8,9},{9,8},{10,11... | collective-permute-start | bytes 344072 | tf_op jit(solution)/shard_map/ppermute | solution.py:1225
  69.9 24.9 %collective-permute-start.8 = (bf16[4,7,8,256]{3,2,1,0:T(8,128)(2,1)}, bf16[4,7,8,256]{3,2,1,0:T(8,128)(2,1)S(1)}, u32[]{:S(2)}, u32[]{:S(2)}) collective-permute-start(bf16[4,7,8,256]{3,2,1,0:T(8,128)(2,1)} %get-tuple-element.114), channel_id=1, source_target_pairs={{0,2},{1,3},{2,0},{3,1},{4,6},{5,7},{6,4},{7,5},{8,10},{9,11},{10,... | collective-permute-start | bytes 344072 | tf_op jit(solution)/shard_map/ppermute | solution.py:1225
  71.4 23.4 %collective-permute-start.9 = (bf16[4,7,8,256]{3,2,1,0:T(8,128)(2,1)}, bf16[4,7,8,256]{3,2,1,0:T(8,128)(2,1)S(1)}, u32[]{:S(2)}, u32[]{:S(2)}) collective-permute-start(bf16[4,7,8,256]{3,2,1,0:T(8,128)(2,1)} %get-tuple-element.115), channel_id=1, source_target_pairs={{0,3},{1,2},{2,1},{3,0},{4,7},{5,6},{6,5},{7,4},{8,11},{9,10},{10,... | collective-permute-start | bytes 344072 | tf_op jit(solution)/shard_map/ppermute | solution.py:1225
  72.5 22.3 %all-to-all-start.1 = ((bf16[16,64,256]{2,1,0:T(8,128)(2,1)}), bf16[16,64,256]{2,1,0:T(8,128)(2,1)S(1)}, u32[]{:S(2)}, u32[]{:S(2)}) async-start(bf16[16,64,256]{2,1,0:T(8,128)(2,1)} %bitcast.5.refs_17_), calls=%async_computation.1 | async-start | bytes 1048576 | tf_op jit(solution)/shard_map/all_to_all | solution.py:1409
  97.4 13.2 %collective-permute-start.14 = (bf16[416,256]{1,0:T(8,128)(2,1)S(1)}, bf16[416,256]{1,0:T(8,128)(2,1)S(1)}, u32[]{:S(2)}, u32[]{:S(2)}) collective-permute-start(bf16[416,256]{1,0:T(8,128)(2,1)S(1)} %get-tuple-element.164.refs_16_), channel_id=1, source_target_pairs={{0,2},{2,0},{4,6},{6,4},{8,10},{10,8},{12,14},{14,12},{16,18},{18,... | collective-permute-start | bytes 638984 | tf_op jit(solution)/shard_map/ppermute | solution.py:1225
  99.4 11.6 %collective-permute-start.15 = (bf16[416,256]{1,0:T(8,128)(2,1)S(1)}, bf16[416,256]{1,0:T(8,128)(2,1)S(1)}, u32[]{:S(2)}, u32[]{:S(2)}) collective-permute-start(bf16[416,256]{1,0:T(8,128)(2,1)S(1)} %get-tuple-element.163.refs_17_), channel_id=1, source_target_pairs={{0,4},{2,6},{4,0},{6,2},{8,12},{10,14},{12,8},{14,10},{16,20},{18,... | collective-permute-start | bytes 638984 | tf_op jit(solution)/shard_map/ppermute | solution.py:1225
  100.9 10.1 %collective-permute-start.16 = (bf16[416,256]{1,0:T(8,128)(2,1)S(1)}, bf16[416,256]{1,0:T(8,128)(2,1)}, u32[]{:S(2)}, u32[]{:S(2)}) collective-permute-start(bf16[416,256]{1,0:T(8,128)(2,1)S(1)} %get-tuple-element.162.refs_18_), channel_id=1, source_target_pairs={{0,6},{2,4},{4,2},{6,0},{8,14},{10,12},{12,10},{14,8},{16,22},{18,... | collective-permute-start | bytes 638984 | tf_op jit(solution)/shard_map/ppermute | solution.py:1225
  122.6 6.8 %collective-permute-start.22 = (bf16[144,256]{1,0:T(8,128)(2,1)S(1)}, bf16[144,256]{1,0:T(8,128)(2,1)S(1)}, u32[]{:S(2)}, u32[]{:S(2)}) collective-permute-start(bf16[144,256]{1,0:T(8,128)(2,1)S(1)} %get-tuple-element.171), channel_id=1, source_target_pairs={{0,16},{2,18},{4,20},{6,22},{8,24},{10,26},{12,28},{14,30},{16,0},... | collective-permute-start | bytes 221192 | tf_op jit(solution)/shard_map/ppermute | solution.py:1225
  125.0 6.2 %collective-permute-start.23 = (bf16[144,256]{1,0:T(8,128)(2,1)S(1)}, bf16[144,256]{1,0:T(8,128)(2,1)S(1)}, u32[]{:S(2)}, u32[]{:S(2)}) collective-permute-start(bf16[144,256]{1,0:T(8,128)(2,1)S(1)} %get-tuple-element.172), channel_id=1, source_target_pairs={{0,24},{2,26},{4,28},{6,30},{8,16},{10,18},{12,20},{14,22},{16,8},... | collective-permute-start | bytes 221192 | tf_op jit(solution)/shard_map/ppermute | solution.py:1225
  125.5 7.4 %collective-permute-start.11 = (bf16[4,7,8,256]{3,2,1,0:T(8,128)(2,1)S(1)}, bf16[4,7,8,256]{3,2,1,0:T(8,128)(2,1)S(1)}, u32[]{:S(2)}, u32[]{:S(2)}) collective-permute-start(bf16[4,7,8,256]{3,2,1,0:T(8,128)(2,1)S(1)} %get-tuple-element.131), channel_id=1, source_target_pairs={{0,1},{1,0},{2,3},{3,2},{4,5},{5,4},{6,7},{7,6},{8,9},{9,8},{10,11... | collective-permute-start | bytes 344072 | tf_op jit(solution)/shard_map/ppermute | solution.py:1225
  125.5 10.1 %collective-permute-start.12 = (bf16[4,7,8,256]{3,2,1,0:T(8,128)(2,1)S(1)}, bf16[4,7,8,256]{3,2,1,0:T(8,128)(2,1)S(1)}, u32[]{:S(2)}, u32[]{:S(2)}) collective-permute-start(bf16[4,7,8,256]{3,2,1,0:T(8,128)(2,1)S(1)} %get-tuple-element.132), channel_id=1, source_target_pairs={{0,2},{1,3},{2,0},{3,1},{4,6},{5,7},{6,4},{7,5},{8,10},{9,11},{10,... | collective-permute-start | bytes 344072 | tf_op jit(solution)/shard_map/ppermute | solution.py:1225
  126.1 9.6 %collective-permute-start.13 = (bf16[4,7,8,256]{3,2,1,0:T(8,128)(2,1)S(1)}, bf16[4,7,8,256]{3,2,1,0:T(8,128)(2,1)S(1)}, u32[]{:S(2)}, u32[]{:S(2)}) collective-permute-start(bf16[4,7,8,256]{3,2,1,0:T(8,128)(2,1)S(1)} %get-tuple-element.133), channel_id=1, source_target_pairs={{0,3},{1,2},{2,1},{3,0},{4,7},{5,6},{6,5},{7,4},{8,11},{9,10},{10,... | collective-permute-start | bytes 344072 | tf_op jit(solution)/shard_map/ppermute | solution.py:1225
  131.2 6.5 %collective-permute-start.24 = (bf16[208,256]{1,0:T(8,128)(2,1)S(1)}, bf16[208,256]{1,0:T(8,128)(2,1)S(1)}, u32[]{:S(2)}, u32[]{:S(2)}) collective-permute-start(bf16[208,256]{1,0:T(8,128)(2,1)S(1)} %get-tuple-element.174), channel_id=1, source_target_pairs={{0,8},{2,10},{4,12},{6,14},{8,0},{10,2},{12,4},{14,6},{16,24},{18,... | collective-permute-start | bytes 319496 | tf_op jit(solution)/shard_map/ppermute | solution.py:1225
  131.3 9.1 %collective-permute-start.25 = (bf16[208,256]{1,0:T(8,128)(2,1)S(1)}, bf16[208,256]{1,0:T(8,128)(2,1)S(1)}, u32[]{:S(2)}, u32[]{:S(2)}) collective-permute-start(bf16[208,256]{1,0:T(8,128)(2,1)S(1)} %get-tuple-element.174), channel_id=1, source_target_pairs={{0,16},{2,18},{4,20},{6,22},{8,24},{10,26},{12,28},{14,30},{16,0},... | collective-permute-start | bytes 319496 | tf_op jit(solution)/shard_map/ppermute | solution.py:1225
  132.9 7.4 %collective-permute-start.26 = (bf16[208,256]{1,0:T(8,128)(2,1)S(1)}, bf16[208,256]{1,0:T(8,128)(2,1)S(1)}, u32[]{:S(2)}, u32[]{:S(2)}) collective-permute-start(bf16[208,256]{1,0:T(8,128)(2,1)S(1)} %get-tuple-element.174), channel_id=1, source_target_pairs={{0,24},{2,26},{4,28},{6,30},{8,16},{10,18},{12,20},{14,22},{16,8},... | collective-permute-start | bytes 319496 | tf_op jit(solution)/shard_map/ppermute | solution.py:1225
  140.4 24.8 %all-to-all-start.2 = ((bf16[32,7,8,256]{3,2,1,0:T(8,128)(2,1)}), bf16[32,7,8,256]{3,2,1,0:T(8,128)(2,1)S(1)}, u32[]{:S(2)}, u32[]{:S(2)}) async-start(bf16[32,7,8,256]{3,2,1,0:T(8,128)(2,1)} %split.1), calls=%async_computation.2 | async-start | bytes 1835008 | tf_op jit(solution)/shard_map/all_to_all | solution.py:1539
  144.3 12.8 %collective-permute-start.27 = (bf16[4,208,256]{2,1,0:T(8,128)(2,1)S(1)}, bf16[4,208,256]{2,1,0:T(8,128)(2,1)S(1)}, u32[]{:S(2)}, u32[]{:S(2)}) collective-permute-start(bf16[4,208,256]{2,1,0:T(8,128)(2,1)S(1)} %pad_maximum_fusion.refs_0_), channel_id=1, source_target_pairs={{0,2},{2,0},{4,6},{6,4},{8,10},{10,8},{12,14},{14,12},{16,18},{18,... | collective-permute-start | bytes 1277960 | tf_op jit(solution)/shard_map/ppermute | solution.py:1225
  144.9 27.2 %collective-permute-start.28 = (bf16[4,208,256]{2,1,0:T(8,128)(2,1)S(1)}, bf16[4,208,256]{2,1,0:T(8,128)(2,1)S(1)}, u32[]{:S(2)}, u32[]{:S(2)}) collective-permute-start(bf16[4,208,256]{2,1,0:T(8,128)(2,1)S(1)} %pad_maximum_fusion.refs_0_), channel_id=1, source_target_pairs={{0,4},{2,6},{4,0},{6,2},{8,12},{10,14},{12,8},{14,10},{16,20},{18,... | collective-permute-start | bytes 1277960 | tf_op jit(solution)/shard_map/ppermute | solution.py:1225
  146.9 25.2 %collective-permute-start.29 = (bf16[4,208,256]{2,1,0:T(8,128)(2,1)S(1)}, bf16[4,208,256]{2,1,0:T(8,128)(2,1)S(1)}, u32[]{:S(2)}, u32[]{:S(2)}) collective-permute-start(bf16[4,208,256]{2,1,0:T(8,128)(2,1)S(1)} %pad_maximum_fusion.refs_0_), channel_id=1, source_target_pairs={{0,6},{2,4},{4,2},{6,0},{8,14},{10,12},{12,10},{14,8},{16,22},{18,... | collective-permute-start | bytes 1277960 | tf_op jit(solution)/shard_map/ppermute | solution.py:1225
  149.8 22.8 %collective-permute-start.30 = (bf16[4,208,256]{2,1,0:T(8,128)(2,1)S(1)}, bf16[4,208,256]{2,1,0:T(8,128)(2,1)S(1)}, u32[]{:S(2)}, u32[]{:S(2)}) collective-permute-start(bf16[4,208,256]{2,1,0:T(8,128)(2,1)S(1)} %pad_maximum_fusion.refs_0_), channel_id=1, source_target_pairs={{0,1},{1,0},{2,3},{3,2},{4,5},{5,4},{6,7},{7,6},{8,9},{9,8},{10,11... | collective-permute-start | bytes 1277960 | tf_op jit(solution)/shard_map/ppermute | solution.py:1208
  157.0 15.6 %collective-permute-start.31 = (bf16[4,208,256]{2,1,0:T(8,128)(2,1)S(1)}, bf16[4,208,256]{2,1,0:T(8,128)(2,1)}, u32[]{:S(2)}, u32[]{:S(2)}) collective-permute-start(bf16[4,208,256]{2,1,0:T(8,128)(2,1)S(1)} %collective-permute-done.27.refs_1_), channel_id=1, source_target_pairs={{0,1},{1,0},{2,3},{3,2},{4,5},{5,4},{6,7},{7,6},{8,9},{9,8},{10,11... | collective-permute-start | bytes 1277960 | tf_op jit(solution)/shard_map/ppermute | solution.py:1208
  (35 other events, 638.5 us)

commit v4 on v2

--- a/solution.py
+++ b/solution.py
@@ -701,7 +701,7 @@
                     :, lane * 128 : (lane + 1) * 128
                 ]
 
-    @pl.loop(0, count)
+    @pl.loop(0, count, unroll=4)
     def _(n):
         rows = pl.ds(pl.multiple_of(n * PAD, 8), PAD)
         tile = jnp.concatenate([flat[lane, rows, :] for lane in range(lanes)], axis=1)
@@ -715,12 +715,12 @@
 
 
 def pick_kernel(
-    moves, mix_ref, cut_ref, images_ref, index_out, take_out, sent_out, own_out, flat, counts
+    groups, moves, mix_ref, cut_ref, images_ref, index_out, sent_out, own_out, flat
 ):
     moves.fetch(images_ref)
     count = images_ref.shape[2]
     slots = sent_out.shape[0]
-    capacity = slots // counts.shape[0]
+    capacity = slots // groups
     me = lax.axis_index("dp")
 
     def put(n, tile):
@@ -730,9 +730,8 @@
     def _(s):
         index_out[s] = count
 
-    @pl.loop(0, counts.shape[0])
+    @pl.loop(0, groups)
     def _(g):
-        counts[g] = 0
         rank = g * capacity
         for ref in (mix_ref, cut_ref):
             for j in range(count):
@@ -742,6 +741,34 @@
                 index_out[jnp.where(hit, rank, slots)] = wanted - owner * count
                 rank = rank + hit.astype(jnp.int32)
 
+    moves.need(images_ref)
+    untangle(images_ref, flat, put)
+
+    @pl.loop(0, slots, unroll=4)
+    def _(s):
+        sent_out[s] = own_out[jnp.minimum(index_out[s], count - 1)]
+
+
+def deal_kernel(
+    capacity, place_ref, mix_ref, cut_ref, source, take_out, out_a, out_b, out_c, out_d, flat, counts
+):
+    outs = (out_a, out_b, out_c, out_d)
+    share = out_a.shape[0]
+
+    def put(n, tile):
+        for d, out in enumerate(outs):
+
+            @pl.when(jnp.bitwise_xor(place_ref[3], d) == n // share)
+            def _(out=out):
+                out[n % share] = tile
+
+    count = source.shape[2]
+    me = place_ref[0]
+
+    @pl.loop(0, counts.shape[0])
+    def _(g):
+        counts[g] = 0
+
     for part, ref in enumerate((mix_ref, cut_ref)):
 
         @pl.loop(0, count)
@@ -750,25 +777,6 @@
             rank = counts[owner]
             take_out[part * count + j] = owner * capacity + rank
             counts[owner] = rank + 1
-
-    moves.need(images_ref)
-    untangle(images_ref, flat, put)
-
-    @pl.loop(0, slots, unroll=4)
-    def _(s):
-        sent_out[s] = own_out[jnp.minimum(index_out[s], count - 1)]
-
-
-def deal_kernel(place_ref, source, out_a, out_b, out_c, out_d, flat):
-    outs = (out_a, out_b, out_c, out_d)
-    share = out_a.shape[0]
-
-    def put(n, tile):
-        for d, out in enumerate(outs):
-
-            @pl.when(jnp.bitwise_xor(place_ref[3], d) == n // share)
-            def _(out=out):
-                out[n % share] = tile
 
     untangle(source, flat, put)
 
@@ -793,7 +801,7 @@
     share = out_a.shape[0]
     for d, out in enumerate((out_a, out_b, out_c, out_d)):
 
-        @pl.loop(0, share)
+        @pl.loop(0, share, unroll=2)
         def _(i, d=d, out=out):
             n = jnp.bitwise_xor(place_ref[3], d) * share + i
             inside = inside_box(corner_ref, n, place_ref)
@@ -1307,22 +1315,29 @@
     corners = corners.T
     masks = drop_masks.T
     flat = ((width // 128, images_here * PAD, 128), F32)
-    index, take, outgoing, own = run(
-        pick_kernel,
+    index, outgoing, own = run(
+        functools.partial(pick_kernel, groups),
         [mix_partner, cut_partner],
         [images.transpose(1, 2, 0, 3)],
         [((slots, TILE, 8, width), BF), ((images_here, TILE, 8, width), BF)],
-        [flat, (pltpu.SMEM((groups,), jnp.int32), None)],
+        [flat],
         name="pick",
         vmem=60,
         lazy=(0, 2),
         near=((), (0, 1)),
-        scalar_outs=(((slots + 8,), jnp.int32), ((2 * images_here,), jnp.int32)),
+        scalar_outs=(((slots + 8,), jnp.int32),),
     )
     arrived = lax.all_to_all(outgoing, "dp", split_axis=0, concat_axis=0, tiled=True)
-    cot = deal(
-        run(deal_kernel, [place], [cotangent.transpose(1, 2, 0, 3)], [quad] * 4, [flat], name="deal")
-    )
+    take, *cot = run(
+        functools.partial(deal_kernel, capacity),
+        [place, mix_partner, cut_partner],
+        [cotangent.transpose(1, 2, 0, 3)],
+        [quad] * 4,
+        [flat, (pltpu.SMEM((groups,), jnp.int32), None)],
+        name="deal",
+        scalar_outs=(((2 * images_here,), jnp.int32),),
+    )
+    cot = deal(cot)
     mixed = deal(
         run(
             mix_kernel,

time: 178 us -> 177 us (level)
  transfers between devices with their start and end apart: 37 -> 37, of which waited for: 18 -> 19; matrix products, arithmetic and copies ran while one was open for 1% -> 1% of each run, Pallas kernels for 19% -> 20%
where the time goes in v4:
time: 177 us
  Pallas kernels  69.5 us (39%)
  waiting for transfers between devices  60.2 us (34%)
  starting transfers between devices  44.1 us (25%)
    pallas_call x9, Pallas kernels, run(): pl.pallas_call(body, out_shape=out_shape, in_specs=[SMEM] * len(scalars)...  65.6 us
    ppermute x27, waiting for transfers between devices, across(): return lax.ppermute(values, axes, [(i, i ^ mask) for i in range(size)])  33.7 us
    ppermute x27, starting transfers between devices, across(): return lax.ppermute(values, axes, [(i, i ^ mask) for i in range(size)])  27.1 us
    all_to_all x1, waiting for transfers between devices, local(): lax.all_to_all(outgoing, 'dp', split_axis=0, concat_axis=0, tiled=True)  13.2 us
    all_to_all x1, waiting for transfers between devices, local(): back = lax.all_to_all(parted, 'dp', split_axis=0, concat_axis=0, tiled=True)  7.89 us
    all_to_all x1, starting transfers between devices, local(): lax.all_to_all(outgoing, 'dp', split_axis=0, concat_axis=0, tiled=True)  7.42 us
    ppermute x7, waiting for transfers between devices, swap(): return lax.ppermute(values, axis, [(0, 1), (1, 0)])  5.44 us
    all_to_all x1, starting transfers between devices, local(): lax.all_to_all(sent1, RANKS, split_axis=0, concat_axis=0, tiled=True)  4.56 us
  transfers between devices with their start and end apart: 37, of which 19 were waited for; matrix products, arithmetic and copies ran while one was open for 1% of the time, Pallas kernels for 20%

profile of v4, /device:TPU:0, one launch (start us, length us, event | category | flops | bytes accessed | tf_op | source)
XLA Modules:
  0.0 176.8 jit_solution(10993125870077162195)
XLA Ops:
  0.7 3.2 %pick.1 = (s32[40]{0:T(128)}, bf16[32,7,8,256]{3,2,1,0:T(8,128)(2,1)}, bf16[16,7,8,256]{3,2,1,0:T(8,128)(2,1)}) custom-call(s32[128]{0:T(128)} %refs_0_.4, s32[128]{0:T(128)} %refs_1_.5, bf16[7,7,16,256]{3,2,1,0:T(8,128)(2,1)} %bitcast.41), custom_call_target="tpu_custom_call" | custom-call | bytes 401408 | tf_op jit(solution)/shard_map/pick/pallas_call | solution.py:1193
  4.1 7.4 %all-to-all-start = ((bf16[32,7,8,256]{3,2,1,0:T(8,128)(2,1)}), bf16[32,7,8,256]{3,2,1,0:T(8,128)(2,1)S(1)}, u32[]{:S(2)}, u32[]{:S(2)}) async-start(bf16[32,7,8,256]{3,2,1,0:T(8,128)(2,1)} %get-tuple-element.89), calls=%async_computation | async-start | bytes 1835008 | tf_op jit(solution)/shard_map/all_to_all | solution.py:1330
  11.5 2.1 %deal.1 = (s32[32]{0:T(128)S(1)}, bf16[4,7,8,256]{3,2,1,0:T(8,128)(2,1)S(1)}, bf16[4,7,8,256]{3,2,1,0:T(8,128)(2,1)S(1)}, bf16[4,7,8,256]{3,2,1,0:T(8,128)(2,1)S(1)}, bf16[4,7,8,256]{3,2,1,0:T(8,128)(2,1)S(1)}) custom-call(s32[128]{0:T(128)S(1)} %copy-done.4, s32[128]{0:T(128)S(1)} %copy-done.5, bf16[7,7,16,256]{3,2,1,0:T(8,128)(2,1)S(1)} %bitcast.27), custom_call_target="tpu_custom_call" | custom-call | bytes 401408 | tf_op jit(solution)/shard_map/deal/pallas_call | solution.py:1193
  15.6 4.1 %collective-permute-done.1.refs_7_.refs_15_ = bf16[4,7,8,256]{3,2,1,0:T(8,128)(2,1)S(1)} collective-permute-done((bf16[4,7,8,256]{3,2,1,0:T(8,128)(2,1)S(1)}, bf16[4,7,8,256]{3,2,1,0:T(8,128)(2,1)S(1)}, u32[]{:S(2)}, u32[]{:S(2)}) %collective-permute-start.1) | collective-permute-done | bytes 114720 | tf_op jit(solution)/shard_map/ppermute | solution.py:1233
  21.3 13.2 %all-to-all-done.refs_3_ = bf16[32,7,8,256]{3,2,1,0:T(8,128)(2,1)S(1)} async-done(((bf16[32,7,8,256]{3,2,1,0:T(8,128)(2,1)}), bf16[32,7,8,256]{3,2,1,0:T(8,128)(2,1)S(1)}, u32[]{:S(2)}, u32[]{:S(2)}) %all-to-all-start) | async-done | bytes 917536 | tf_op jit(solution)/shard_map/all_to_all | solution.py:1330
  37.5 4.1 %collective-permute-done.4.refs_3_.refs_8_ = bf16[4,7,8,256]{3,2,1,0:T(8,128)(2,1)S(1)} collective-permute-done((bf16[4,7,8,256]{3,2,1,0:T(8,128)(2,1)S(1)}, bf16[4,7,8,256]{3,2,1,0:T(8,128)(2,1)S(1)}, u32[]{:S(2)}, u32[]{:S(2)}) %collective-permute-start.4) | collective-permute-done | bytes 114720 | tf_op jit(solution)/shard_map/ppermute | solution.py:1233
  43.3 25.6 %first.1 = (f32[7,8,256]{2,1,0:T(8,128)}, bf16[1024,256]{1,0:T(8,128)(2,1)S(1)}, bf16[1024,256]{1,0:T(8,128)(2,1)S(1)}, bf16[4,7,8,256]{3,2,1,0:T(8,128)(2,1)}, ...) custom-call(s32[4,16]{1,0:T(4,128)S(1)} %bitcast.34, ...), custom_call_target="tpu_custom_call" | custom-call | flops 70464307200 | bytes 4108288 | tf_op jit(solution)/shard_map/first/pallas_call | solution.py:1193
  72.1 4.6 %all-to-all-start.1 = ((bf16[16,64,256]{2,1,0:T(8,128)(2,1)}), bf16[16,64,256]{2,1,0:T(8,128)(2,1)S(1)}, u32[]{:S(2)}, u32[]{:S(2)}) async-start(bf16[16,64,256]{2,1,0:T(8,128)(2,1)} %bitcast.5.refs_17_), calls=%async_computation.1 | async-start | bytes 1048576 | tf_op jit(solution)/shard_map/all_to_all | solution.py:1424
  76.7 17.7 %second.1 = (f32[15,8,256]{2,1,0:T(8,128)}, f32[9,8,256]{2,1,0:T(8,128)}, bf16[1664,256]{1,0:T(8,128)(2,1)S(1)}, bf16[1664,256]{1,0:T(8,128)(2,1)S(1)}, f32[896,256]{1,0:T(8,128)}, /*index=5*/f32[896,256]{1,0:T(8,128)}) custom-call(s32[4,16]{1,0:T(4,128)S(1)} %bitcast.35, f32[2,2,256]{2,1,0:T(2,128)S(1)} %copy-done.15, f32[2,2,256]{2,1,0:T(2,128)S(1)} %copy-done.16, ...), custom_call_target="tpu_custom_call" | custom-call | flops 42278584320 | bytes 13723648 | tf_op jit(solution)/shard_map/second/pallas_call | solution.py:1193
  94.7 2.2 %collective-permute-done.10 = bf16[1664,256]{1,0:T(8,128)(2,1)S(1)} collective-permute-done((bf16[1664,256]{1,0:T(8,128)(2,1)S(1)}, bf16[1664,256]{1,0:T(8,128)(2,1)S(1)}, u32[]{:S(2)}, u32[]{:S(2)}) %collective-permute-start.10) | collective-permute-done | bytes 852000 | tf_op jit(solution)/shard_map/ppermute | solution.py:1216
  97.1 2.0 %collective-permute-start.14 = (bf16[416,256]{1,0:T(8,128)(2,1)S(1)}, bf16[416,256]{1,0:T(8,128)(2,1)S(1)}, u32[]{:S(2)}, u32[]{:S(2)}) collective-permute-start(bf16[416,256]{1,0:T(8,128)(2,1)S(1)} %get-tuple-element.164.refs_16_), channel_id=1, source_target_pairs={{0,2},{2,0},{4,6},{6,4},{8,10},{10,8},{12,14},{14,12},{16,18},{18,... | collective-permute-start | bytes 638984 | tf_op jit(solution)/shard_map/ppermute | solution.py:1233
  100.7 9.7 %third.1 = (bf16[4,7,8,256]{3,2,1,0:T(8,128)(2,1)S(1)}, bf16[4,7,8,256]{3,2,1,0:T(8,128)(2,1)S(1)}, bf16[4,7,8,256]{3,2,1,0:T(8,128)(2,1)S(1)}, bf16[4,7,8,256]{...) custom-call(f32[2,2,256]{2,1,0:T(2,128)S(1)} %copy-done.15, ...), custom_call_target="tpu_custom_call" | custom-call | flops 21139292160 | bytes 6572032 | tf_op jit(solution)/shard_map/third/pallas_call | solution.py:1193
  118.3 2.4 %collective-permute-done.20 = bf16[128,256]{1,0:T(8,128)(2,1)S(1)} collective-permute-done((bf16[128,256]{1,0:T(8,128)(2,1)S(1)}, bf16[128,256]{1,0:T(8,128)(2,1)S(1)}, u32[]{:S(2)}, u32[]{:S(2)}) %collective-permute-start.20) | collective-permute-done | bytes 65568 | tf_op jit(solution)/shard_map/ppermute | solution.py:1233
  122.2 2.4 %collective-permute-start.22 = (bf16[136,256]{1,0:T(8,128)(2,1)S(1)}, bf16[136,256]{1,0:T(8,128)(2,1)S(1)}, u32[]{:S(2)}, u32[]{:S(2)}) collective-permute-start(bf16[136,256]{1,0:T(8,128)(2,1)S(1)} %get-tuple-element.171), channel_id=1, source_target_pairs={{0,16},{2,18},{4,20},{6,22},{8,24},{10,26},{12,28},{14,30},{16,0},... | collective-permute-start | bytes 208904 | tf_op jit(solution)/shard_map/ppermute | solution.py:1233
  132.3 2.9 %collective-permute-start.26 = (bf16[200,256]{1,0:T(8,128)(2,1)S(1)}, bf16[200,256]{1,0:T(8,128)(2,1)S(1)}, u32[]{:S(2)}, u32[]{:S(2)}) collective-permute-start(bf16[200,256]{1,0:T(8,128)(2,1)S(1)} %get-tuple-element.174), channel_id=1, source_target_pairs={{0,24},{2,26},{4,28},{6,30},{8,16},{10,18},{12,20},{14,22},{16,8},... | collective-permute-start | bytes 307208 | tf_op jit(solution)/shard_map/ppermute | solution.py:1233
  137.2 2.5 %collective-permute-done.25 = bf16[200,256]{1,0:T(8,128)(2,1)S(1)} collective-permute-done((bf16[200,256]{1,0:T(8,128)(2,1)S(1)}, bf16[200,256]{1,0:T(8,128)(2,1)S(1)}, u32[]{:S(2)}, u32[]{:S(2)}) %collective-permute-start.25) | collective-permute-done | bytes 102432 | tf_op jit(solution)/shard_map/ppermute | solution.py:1233
  139.7 3.8 %all-to-all-start.2 = ((bf16[32,7,8,256]{3,2,1,0:T(8,128)(2,1)}), bf16[32,7,8,256]{3,2,1,0:T(8,128)(2,1)S(1)}, u32[]{:S(2)}, u32[]{:S(2)}) async-start(bf16[32,7,8,256]{3,2,1,0:T(8,128)(2,1)} %split.1), calls=%async_computation.2 | async-start | bytes 1835008 | tf_op jit(solution)/shard_map/all_to_all | solution.py:1551
  144.1 2.0 %collective-permute-start.28 = (bf16[4,200,256]{2,1,0:T(8,128)(2,1)S(1)}, bf16[4,200,256]{2,1,0:T(8,128)(2,1)S(1)}, u32[]{:S(2)}, u32[]{:S(2)}) collective-permute-start(bf16[4,200,256]{2,1,0:T(8,128)(2,1)S(1)} %pad_maximum_fusion.refs_0_), channel_id=1, source_target_pairs={{0,4},{2,6},{4,0},{6,2},{8,12},{10,14},{12,8},{14,10},{16,20},{18,... | collective-permute-start | bytes 1228808 | tf_op jit(solution)/shard_map/ppermute | solution.py:1233
  147.0 2.1 %lay.1 = bf16[7,7,16,256]{3,2,1,0:T(8,128)(2,1)} custom-call(bf16[4,7,8,256]{3,2,1,0:T(8,128)(2,1)} %get-tuple-element.116.refs_0_, bf16[4,7,8,256]{3,2,1,0:T(8,128)(2,1)} %copy-done.24, bf16[4,7,8,256]{3,2,1,0:T(8,128)(2,1)} %collective-permute-done.8.refs_2_, bf16[4,7,8,256]{3,2,1,0:T(8,128)(2,1)} %collective-permute-done.9.refs_3_), custom_call_target="tpu_custom_call" | custom-call | bytes 458752 | tf_op jit(solution)/shard_map/lay/pallas_call | solution.py:1193
  149.1 6.9 %collective-permute-done.27.refs_1_ = bf16[4,200,256]{2,1,0:T(8,128)(2,1)S(1)} collective-permute-done((bf16[4,200,256]{2,1,0:T(8,128)(2,1)S(1)}, bf16[4,200,256]{2,1,0:T(8,128)(2,1)S(1)}, u32[]{:S(2)}, u32[]{:S(2)}) %collective-permute-start.27) | collective-permute-done | bytes 409632 | tf_op jit(solution)/shard_map/ppermute | solution.py:1233
  156.0 7.9 %all-to-all-done.2.refs_7_ = bf16[32,7,8,256]{3,2,1,0:T(8,128)(2,1)S(1)} async-done(((bf16[32,7,8,256]{3,2,1,0:T(8,128)(2,1)}), bf16[32,7,8,256]{3,2,1,0:T(8,128)(2,1)S(1)}, u32[]{:S(2)}, u32[]{:S(2)}) %all-to-all-start.2) | async-done | bytes 917536 | tf_op jit(solution)/shard_map/all_to_all | solution.py:1551
  163.9 2.3 %join.1 = f32[7,7,16,256]{3,2,1,0:T(8,128)} custom-call(s32[40]{0:T(128)S(1)} %copy-done.6, s32[4,16]{1,0:T(4,128)S(1)} %bitcast.30, f32[16]{0:T(128)S(1)} %copy-done.3, bf16[4,7,8,256]{3,2,1,0:T(8,128)(2,1)S(1)} %get-tuple-element.130.refs_3_, bf16[4,7,8,256]{3,2,1,0:T(8,128)(2,1)S(1)} %collective-permute-done.11.refs_4_, ...), custom_call_target="tpu_custom_call" | custom-call | bytes 1376256 | tf_op jit(solution)/shard_map/join/pallas_call | solution.py:1193
  166.2 4.2 %collective-permute-done.28.refs_2_ = bf16[4,200,256]{2,1,0:T(8,128)(2,1)S(1)} collective-permute-done((bf16[4,200,256]{2,1,0:T(8,128)(2,1)S(1)}, bf16[4,200,256]{2,1,0:T(8,128)(2,1)S(1)}, u32[]{:S(2)}, u32[]{:S(2)}) %collective-permute-start.28) | collective-permute-done | bytes 409632 | tf_op jit(solution)/shard_map/ppermute | solution.py:1233
  172.7 3.9 %unpack.1 = (f32[2,2,256]{2,1,0:T(2,128)}, f32[2,2,256]{2,1,0:T(2,128)}, f32[2,256,768]{2,1,0:T(8,128)}, f32[2,512]{1,0:T(2,128)}, f32[3,3,2,256]{3,2,1,0:T(2,12...) custom-call(bf16[4,200,256]{2,1,0:T(8,128)(2,1)S(1)} %pad_maximum_fu, ...), custom_call_target="tpu_custom_call" | custom-call | tf_op jit(solution)/shard_map/unpack/pallas_call | solution.py:1579
  (120 shorter events, 36.4 us)
Async XLA Ops:
  4.1 30.5 %all-to-all-start = ((bf16[32,7,8,256]{3,2,1,0:T(8,128)(2,1)}), bf16[32,7,8,256]{3,2,1,0:T(8,128)(2,1)S(1)}, u32[]{:S(2)}, u32[]{:S(2)}) async-start(bf16[32,7,8,256]{3,2,1,0:T(8,128)(2,1)} %get-tuple-element.89), calls=%async_computation | async-start | bytes 1835008 | tf_op jit(solution)/shard_map/all_to_all | solution.py:1330
  13.7 6.0 %collective-permute-start.1 = (bf16[4,7,8,256]{3,2,1,0:T(8,128)(2,1)S(1)}, bf16[4,7,8,256]{3,2,1,0:T(8,128)(2,1)S(1)}, u32[]{:S(2)}, u32[]{:S(2)}) collective-permute-start(bf16[4,7,8,256]{3,2,1,0:T(8,128)(2,1)S(1)} %get-tuple-element.93), channel_id=1, source_target_pairs={{0,2},{1,3},{2,0},{3,1},{4,6},{5,7},{6,4},{7,5},{8,10},{9,11},{10,... | collective-permute-start | bytes 344072 | tf_op jit(solution)/shard_map/ppermute | solution.py:1233
  35.7 6.0 %collective-permute-start.4 = (bf16[4,7,8,256]{3,2,1,0:T(8,128)(2,1)S(1)}, bf16[4,7,8,256]{3,2,1,0:T(8,128)(2,1)S(1)}, u32[]{:S(2)}, u32[]{:S(2)}) collective-permute-start(bf16[4,7,8,256]{3,2,1,0:T(8,128)(2,1)S(1)} %get-tuple-element.97), channel_id=1, source_target_pairs={{0,2},{1,3},{2,0},{3,1},{4,6},{5,7},{6,4},{7,5},{8,10},{9,11},{10,... | collective-permute-start | bytes 344072 | tf_op jit(solution)/shard_map/ppermute | solution.py:1233
  69.3 25.1 %collective-permute-start.7 = (bf16[4,7,8,256]{3,2,1,0:T(8,128)(2,1)}, bf16[4,7,8,256]{3,2,1,0:T(8,128)(2,1)S(1)}, u32[]{:S(2)}, u32[]{:S(2)}) collective-permute-start(bf16[4,7,8,256]{3,2,1,0:T(8,128)(2,1)} %get-tuple-element.113), channel_id=1, source_target_pairs={{0,1},{1,0},{2,3},{3,2},{4,5},{5,4},{6,7},{7,6},{8,9},{9,8},{10,11... | collective-permute-start | bytes 344072 | tf_op jit(solution)/shard_map/ppermute | solution.py:1233
  69.5 24.9 %collective-permute-start.8 = (bf16[4,7,8,256]{3,2,1,0:T(8,128)(2,1)}, bf16[4,7,8,256]{3,2,1,0:T(8,128)(2,1)}, u32[]{:S(2)}, u32[]{:S(2)}) collective-permute-start(bf16[4,7,8,256]{3,2,1,0:T(8,128)(2,1)} %get-tuple-element.114), channel_id=1, source_target_pairs={{0,2},{1,3},{2,0},{3,1},{4,6},{5,7},{6,4},{7,5},{8,10},{9,11},{10,... | collective-permute-start | bytes 344072 | tf_op jit(solution)/shard_map/ppermute | solution.py:1233
  71.0 23.4 %collective-permute-start.9 = (bf16[4,7,8,256]{3,2,1,0:T(8,128)(2,1)}, bf16[4,7,8,256]{3,2,1,0:T(8,128)(2,1)}, u32[]{:S(2)}, u32[]{:S(2)}) collective-permute-start(bf16[4,7,8,256]{3,2,1,0:T(8,128)(2,1)} %get-tuple-element.115), channel_id=1, source_target_pairs={{0,3},{1,2},{2,1},{3,0},{4,7},{5,6},{6,5},{7,4},{8,11},{9,10},{10,... | collective-permute-start | bytes 344072 | tf_op jit(solution)/shard_map/ppermute | solution.py:1233
  72.1 22.3 %all-to-all-start.1 = ((bf16[16,64,256]{2,1,0:T(8,128)(2,1)}), bf16[16,64,256]{2,1,0:T(8,128)(2,1)S(1)}, u32[]{:S(2)}, u32[]{:S(2)}) async-start(bf16[16,64,256]{2,1,0:T(8,128)(2,1)} %bitcast.5.refs_17_), calls=%async_computation.1 | async-start | bytes 1048576 | tf_op jit(solution)/shard_map/all_to_all | solution.py:1424
  97.1 13.3 %collective-permute-start.14 = (bf16[416,256]{1,0:T(8,128)(2,1)S(1)}, bf16[416,256]{1,0:T(8,128)(2,1)S(1)}, u32[]{:S(2)}, u32[]{:S(2)}) collective-permute-start(bf16[416,256]{1,0:T(8,128)(2,1)S(1)} %get-tuple-element.164.refs_16_), channel_id=1, source_target_pairs={{0,2},{2,0},{4,6},{6,4},{8,10},{10,8},{12,14},{14,12},{16,18},{18,... | collective-permute-start | bytes 638984 | tf_op jit(solution)/shard_map/ppermute | solution.py:1233
  99.0 11.6 %collective-permute-start.15 = (bf16[416,256]{1,0:T(8,128)(2,1)S(1)}, bf16[416,256]{1,0:T(8,128)(2,1)S(1)}, u32[]{:S(2)}, u32[]{:S(2)}) collective-permute-start(bf16[416,256]{1,0:T(8,128)(2,1)S(1)} %get-tuple-element.163.refs_17_), channel_id=1, source_target_pairs={{0,4},{2,6},{4,0},{6,2},{8,12},{10,14},{12,8},{14,10},{16,20},{18,... | collective-permute-start | bytes 638984 | tf_op jit(solution)/shard_map/ppermute | solution.py:1233
  100.5 10.1 %collective-permute-start.16 = (bf16[416,256]{1,0:T(8,128)(2,1)S(1)}, bf16[416,256]{1,0:T(8,128)(2,1)S(1)}, u32[]{:S(2)}, u32[]{:S(2)}) collective-permute-start(bf16[416,256]{1,0:T(8,128)(2,1)S(1)} %get-tuple-element.162.refs_18_), channel_id=1, source_target_pairs={{0,6},{2,4},{4,2},{6,0},{8,14},{10,12},{12,10},{14,8},{16,22},{18,... | collective-permute-start | bytes 638984 | tf_op jit(solution)/shard_map/ppermute | solution.py:1233
  122.2 6.7 %collective-permute-start.22 = (bf16[136,256]{1,0:T(8,128)(2,1)S(1)}, bf16[136,256]{1,0:T(8,128)(2,1)S(1)}, u32[]{:S(2)}, u32[]{:S(2)}) collective-permute-start(bf16[136,256]{1,0:T(8,128)(2,1)S(1)} %get-tuple-element.171), channel_id=1, source_target_pairs={{0,16},{2,18},{4,20},{6,22},{8,24},{10,26},{12,28},{14,30},{16,0},... | collective-permute-start | bytes 208904 | tf_op jit(solution)/shard_map/ppermute | solution.py:1233
  124.6 6.1 %collective-permute-start.23 = (bf16[136,256]{1,0:T(8,128)(2,1)S(1)}, bf16[136,256]{1,0:T(8,128)(2,1)S(1)}, u32[]{:S(2)}, u32[]{:S(2)}) collective-permute-start(bf16[136,256]{1,0:T(8,128)(2,1)S(1)} %get-tuple-element.172), channel_id=1, source_target_pairs={{0,24},{2,26},{4,28},{6,30},{8,16},{10,18},{12,20},{14,22},{16,8},... | collective-permute-start | bytes 208904 | tf_op jit(solution)/shard_map/ppermute | solution.py:1233
  125.2 7.2 %collective-permute-start.11 = (bf16[4,7,8,256]{3,2,1,0:T(8,128)(2,1)S(1)}, bf16[4,7,8,256]{3,2,1,0:T(8,128)(2,1)S(1)}, u32[]{:S(2)}, u32[]{:S(2)}) collective-permute-start(bf16[4,7,8,256]{3,2,1,0:T(8,128)(2,1)S(1)} %get-tuple-element.131), channel_id=1, source_target_pairs={{0,1},{1,0},{2,3},{3,2},{4,5},{5,4},{6,7},{7,6},{8,9},{9,8},{10,11... | collective-permute-start | bytes 344072 | tf_op jit(solution)/shard_map/ppermute | solution.py:1233
  125.2 10.1 %collective-permute-start.12 = (bf16[4,7,8,256]{3,2,1,0:T(8,128)(2,1)S(1)}, bf16[4,7,8,256]{3,2,1,0:T(8,128)(2,1)S(1)}, u32[]{:S(2)}, u32[]{:S(2)}) collective-permute-start(bf16[4,7,8,256]{3,2,1,0:T(8,128)(2,1)S(1)} %get-tuple-element.132), channel_id=1, source_target_pairs={{0,2},{1,3},{2,0},{3,1},{4,6},{5,7},{6,4},{7,5},{8,10},{9,11},{10,... | collective-permute-start | bytes 344072 | tf_op jit(solution)/shard_map/ppermute | solution.py:1233
  125.7 9.5 %collective-permute-start.13 = (bf16[4,7,8,256]{3,2,1,0:T(8,128)(2,1)S(1)}, bf16[4,7,8,256]{3,2,1,0:T(8,128)(2,1)S(1)}, u32[]{:S(2)}, u32[]{:S(2)}) collective-permute-start(bf16[4,7,8,256]{3,2,1,0:T(8,128)(2,1)S(1)} %get-tuple-element.133), channel_id=1, source_target_pairs={{0,3},{1,2},{2,1},{3,0},{4,7},{5,6},{6,5},{7,4},{8,11},{9,10},{10,... | collective-permute-start | bytes 344072 | tf_op jit(solution)/shard_map/ppermute | solution.py:1233
  130.8 6.4 %collective-permute-start.24 = (bf16[200,256]{1,0:T(8,128)(2,1)S(1)}, bf16[200,256]{1,0:T(8,128)(2,1)S(1)}, u32[]{:S(2)}, u32[]{:S(2)}) collective-permute-start(bf16[200,256]{1,0:T(8,128)(2,1)S(1)} %get-tuple-element.174), channel_id=1, source_target_pairs={{0,8},{2,10},{4,12},{6,14},{8,0},{10,2},{12,4},{14,6},{16,24},{18,... | collective-permute-start | bytes 307208 | tf_op jit(solution)/shard_map/ppermute | solution.py:1233
  130.9 8.8 %collective-permute-start.25 = (bf16[200,256]{1,0:T(8,128)(2,1)S(1)}, bf16[200,256]{1,0:T(8,128)(2,1)S(1)}, u32[]{:S(2)}, u32[]{:S(2)}) collective-permute-start(bf16[200,256]{1,0:T(8,128)(2,1)S(1)} %get-tuple-element.174), channel_id=1, source_target_pairs={{0,16},{2,18},{4,20},{6,22},{8,24},{10,26},{12,28},{14,30},{16,0},... | collective-permute-start | bytes 307208 | tf_op jit(solution)/shard_map/ppermute | solution.py:1233
  132.3 7.3 %collective-permute-start.26 = (bf16[200,256]{1,0:T(8,128)(2,1)S(1)}, bf16[200,256]{1,0:T(8,128)(2,1)S(1)}, u32[]{:S(2)}, u32[]{:S(2)}) collective-permute-start(bf16[200,256]{1,0:T(8,128)(2,1)S(1)} %get-tuple-element.174), channel_id=1, source_target_pairs={{0,24},{2,26},{4,28},{6,30},{8,16},{10,18},{12,20},{14,22},{16,8},... | collective-permute-start | bytes 307208 | tf_op jit(solution)/shard_map/ppermute | solution.py:1233
  139.7 24.2 %all-to-all-start.2 = ((bf16[32,7,8,256]{3,2,1,0:T(8,128)(2,1)}), bf16[32,7,8,256]{3,2,1,0:T(8,128)(2,1)S(1)}, u32[]{:S(2)}, u32[]{:S(2)}) async-start(bf16[32,7,8,256]{3,2,1,0:T(8,128)(2,1)} %split.1), calls=%async_computation.2 | async-start | bytes 1835008 | tf_op jit(solution)/shard_map/all_to_all | solution.py:1551
  143.6 12.4 %collective-permute-start.27 = (bf16[4,200,256]{2,1,0:T(8,128)(2,1)S(1)}, bf16[4,200,256]{2,1,0:T(8,128)(2,1)S(1)}, u32[]{:S(2)}, u32[]{:S(2)}) collective-permute-start(bf16[4,200,256]{2,1,0:T(8,128)(2,1)S(1)} %pad_maximum_fusion.refs_0_), channel_id=1, source_target_pairs={{0,2},{2,0},{4,6},{6,4},{8,10},{10,8},{12,14},{14,12},{16,18},{18,... | collective-permute-start | bytes 1228808 | tf_op jit(solution)/shard_map/ppermute | solution.py:1233
  144.1 26.3 %collective-permute-start.28 = (bf16[4,200,256]{2,1,0:T(8,128)(2,1)S(1)}, bf16[4,200,256]{2,1,0:T(8,128)(2,1)S(1)}, u32[]{:S(2)}, u32[]{:S(2)}) collective-permute-start(bf16[4,200,256]{2,1,0:T(8,128)(2,1)S(1)} %pad_maximum_fusion.refs_0_), channel_id=1, source_target_pairs={{0,4},{2,6},{4,0},{6,2},{8,12},{10,14},{12,8},{14,10},{16,20},{18,... | collective-permute-start | bytes 1228808 | tf_op jit(solution)/shard_map/ppermute | solution.py:1233
  146.1 24.2 %collective-permute-start.29 = (bf16[4,200,256]{2,1,0:T(8,128)(2,1)S(1)}, bf16[4,200,256]{2,1,0:T(8,128)(2,1)S(1)}, u32[]{:S(2)}, u32[]{:S(2)}) collective-permute-start(bf16[4,200,256]{2,1,0:T(8,128)(2,1)S(1)} %pad_maximum_fusion.refs_0_), channel_id=1, source_target_pairs={{0,6},{2,4},{4,2},{6,0},{8,14},{10,12},{12,10},{14,8},{16,22},{18,... | collective-permute-start | bytes 1228808 | tf_op jit(solution)/shard_map/ppermute | solution.py:1233
  149.1 21.8 %collective-permute-start.30 = (bf16[4,200,256]{2,1,0:T(8,128)(2,1)S(1)}, bf16[4,200,256]{2,1,0:T(8,128)(2,1)S(1)}, u32[]{:S(2)}, u32[]{:S(2)}) collective-permute-start(bf16[4,200,256]{2,1,0:T(8,128)(2,1)S(1)} %pad_maximum_fusion.refs_0_), channel_id=1, source_target_pairs={{0,1},{1,0},{2,3},{3,2},{4,5},{5,4},{6,7},{7,6},{8,9},{9,8},{10,11... | collective-permute-start | bytes 1228808 | tf_op jit(solution)/shard_map/ppermute | solution.py:1216
  156.0 14.9 %collective-permute-start.31 = (bf16[4,200,256]{2,1,0:T(8,128)(2,1)S(1)}, bf16[4,200,256]{2,1,0:T(8,128)(2,1)}, u32[]{:S(2)}, u32[]{:S(2)}) collective-permute-start(bf16[4,200,256]{2,1,0:T(8,128)(2,1)S(1)} %collective-permute-done.27.refs_1_), channel_id=1, source_target_pairs={{0,1},{1,0},{2,3},{3,2},{4,5},{5,4},{6,7},{7,6},{8,9},{9,8},{10,11... | collective-permute-start | bytes 1228808 | tf_op jit(solution)/shard_map/ppermute | solution.py:1216
  (38 other events, 685.9 us)
